TPU v7x, 32 devices: a whole 2x2x4 slice. The times are simulated.
32 devices in a mesh: row: 8 (over z, y), col: 4 (over x, core).
Axes of the slice: x: 2, y: 2, z: 4, core: 2. Of those that a mesh axis runs over, the one named last changes fastest.
Arguments:
- inputs: bfloat16 [32, 256, 2048], P('row', 'col'), may hold values from -6 to 6
- output_gradient: bfloat16 [32, 256, 256], P('row', 'col'), may hold values from -6 to 6
- weight: bfloat16 [3, 3, 2048, 256], P(None, None, 'row'), may hold values from -0.125 to 0.125
Outputs:
- grad_in: bfloat16 [32, 256, 2048], P('row', 'col')
- grad_weight: float32 [3, 3, 2048, 256], P(None, None, 'row')
All inputs are finite; a program needn't handle non-finite values.
Results may differ from a plain program's by a relative error of at most 0.001.
Values may be sent and summed in bfloat16 or wider, within the bound.
No kernel may reach another device: no remote copies, remote signals or barrier semaphores. Data moves between devices by JAX's collectives and lax.ppermute only.
A program may use at most 128 MiB of HBM per device.

v0:
```python
import math

import jax
import jax.numpy as jnp
from jax import lax
from jax.sharding import PartitionSpec as P

DILATION_STEP = 12


def extended(x, sides, width):
    for axis, dim in sides:
        peers, length = (lax.axis_size(axis), x.shape[dim])
        up = [(i, (i + 1) % peers) for i in range(peers - 1)]
        down = [(j, i) for i, j in up]
        last = lax.slice_in_dim(x, length - width, length, axis=dim)
        initial = lax.slice_in_dim(x, 0, width, axis=dim)
        before = lax.ppermute(last, axis, up)
        after = lax.ppermute(initial, axis, down)
        x = jnp.concatenate([before, x, after], axis=dim)
    return x


def shards(inputs, output_gradient, weight):
    height, width, in_chans = inputs.shape
    out_chans = output_gradient.shape[2]
    step = DILATION_STEP
    in_strip = lax.all_to_all(inputs, "row", split_axis=2, concat_axis=0, tiled=True)
    strip_rows = in_strip.shape[0]
    panel = in_strip.shape[2]
    in_padded = jnp.pad(in_strip, ((step, step), (0, 0), (0, 0)))
    side_rimmed = extended(output_gradient, (("col", 1),), step)
    piece = lax.all_gather(side_rimmed, "row", axis=0, tiled=True)
    start = jnp.int32(0)
    grad_padded = jnp.zeros((strip_rows + 2 * step, width, panel), jnp.float32)
    count = piece.shape[0]
    new_terms = []
    for kernel_tap_row in range(3):
        in_rows = lax.dynamic_slice_in_dim(in_padded, step * kernel_tap_row, count, 0).reshape(
            count * width, panel
        )
        back = jnp.zeros((count * width, panel), jnp.float32)
        for kernel_tap_column in range(3):
            left_offset = step * (2 - kernel_tap_column)
            window = piece[:, left_offset : left_offset + width, :].reshape(
                count * width, out_chans
            )
            new_terms.append(
                lax.dot_general(
                    in_rows, window, (((0,), (0,)), ((), ())), preferred_element_type=jnp.float32
                )
            )
            back = back + lax.dot_general(
                window,
                weight[kernel_tap_row, kernel_tap_column],
                (((1,), (1,)), ((), ())),
                preferred_element_type=jnp.float32,
            )
        target = start + step * kernel_tap_row
        current = lax.dynamic_slice_in_dim(grad_padded, target, count, 0)
        grad_padded = lax.dynamic_update_slice_in_dim(
            grad_padded, current + back.reshape(count, width, panel), target, 0
        )
    terms = jnp.stack(new_terms).reshape(3, 3, panel, out_chans)
    terms, grad_padded = (terms, grad_padded)
    grad_strip = grad_padded[step : step + strip_rows].astype(jnp.bfloat16)
    grad_in = lax.all_to_all(grad_strip, "row", split_axis=0, concat_axis=2, tiled=True)
    scale = 1.0 / math.sqrt(height * width * lax.axis_size("row") * lax.axis_size("col"))
    terms = terms * scale
    grad_weight = lax.psum(terms, "col")
    return (grad_in, grad_weight)


def solution(mesh):
    return jax.shard_map(
        shards,
        mesh=mesh,
        in_specs=(P("row", "col", None), P("row", "col", None), P(None, None, "row", None)),
        out_specs=(P("row", "col", None), P(None, None, "row", None)),
        check_vma=False,
    )
```

profile of v0, /device:TPU:0, one launch (start us, length us, event | category | flops | bytes accessed | tf_op | source)
XLA Modules:
  0.0 169.4 jit_solution(11614795464881649844)
XLA Ops:
  7.2 0.0 all-gather.2.cloned.1.call-start
  7.2 0.8 fusion.38
  8.0 2.4 %collective-permute-start = (bf16[4,12,256]{2,1,0:T(8,128)(2,1)S(1)}, bf16[4,12,256]{2,1,0:T(8,128)(2,1)S(1)}, u32[]{:S(2)}, u32[]{:S(2)}) collective-permute-start(bf16[4,12,256]{2,1,0:T(8,128)(2,1)S(1)} %get-tuple-element.5), channel_id=1, source_target_pairs={{0,1},{1,2},{2,3},{4,5},{5,6},{6,7},{8,9},{9,10},{10,11},{12,13},{... | collective-permute-start | bytes 73736 | tf_op jit(solution)/shard_map/ppermute | solution.py:18
  10.4 1.3 collective-permute-start.1
  11.7 0.0 collective-permute-done
  11.7 3.9 %collective-permute-done.1 = bf16[4,12,256]{2,1,0:T(8,128)(2,1)S(1)} collective-permute-done((bf16[4,12,256]{2,1,0:T(8,128)(2,1)S(1)}, bf16[4,12,256]{2,1,0:T(8,128)(2,1)S(1)}, u32[]{:S(2)}, u32[]{:S(2)}) %collective-permute-start.1) | collective-permute-done | bytes 24608 | tf_op jit(solution)/shard_map/ppermute | solution.py:19
  15.6 1.6 pad_maximum_fusion
  17.2 0.0 all-gather.2.cloned.1.call-update
  17.2 2.9 %copy.11 = bf16[4,64,2048]{1,0,2:T(4,128)(2,1)S(1)} copy(bf16[4,64,2048]{2,1,0:T(8,128)(2,1)} %param.3) | data formatting | bytes 2097152 | tf_op args[0]
  20.1 1.7 reshape.50
  21.8 45.4 %all_to_all.36 = bf16[8,2,32768]{2,1,0:T(2,128)(2,1)} all-to-all(bf16[8,2,32768]{2,1,0:T(2,128)(2,1)S(1)} %reshape.50), channel_id=1, replica_groups=mesh['row'=8,'col'=4] {'row'}, dimensions={0} | all-to-all | bytes 2097152 | tf_op jit(solution)/shard_map/all_to_all | solution.py:28
  67.2 3.1 %reshape.51 = bf16[2048,4,64]{2,1,0:T(4,128)(2,1)S(1)} reshape(bf16[8,2,32768]{2,1,0:T(2,128)(2,1)} %all_to_all.36) | data formatting | bytes 2097152
  70.3 2.2 %copy.12 = bf16[4,64,8,256]{3,1,0,2:T(8,128)(2,1)} copy(bf16[4,64,8,256]{1,0,3,2:T(4,128)(2,1)S(1)} %bitcast.130) | data formatting | bytes 2097152 | tf_op jit(solution)/shard_map/all_to_all | solution.py:28
  72.5 0.0 copy-start.1
  72.5 0.0 all-gather.2.cloned.1.call-done
  72.5 2.7 %fusion.37 = (bf16[32,64,256]{2,1,0:T(8,128)(2,1)S(1)}, bf16[32,64,256]{2,1,0:T(8,128)(2,1)S(1)}, bf16[32,64,256]{2,1,0:T(8,128)(2,1)S(1)}) fusion(bf16[32,88,256]{2,1,0:T(8,128)(2,1)} %all-gather.2.cloned.1.call-done), kind=kLoop, calls=%fused_computation.58 | loop fusion | bytes 6291456 | tf_op jit(solution)/shard_map/slice | solution.py:45
  75.2 0.0 copy-done.1
  75.2 0.5 fusion.12
  75.6 0.5 fusion.16
  76.1 0.0 copy-start
  76.1 0.0 copy-start.2
  76.1 0.5 fusion.20
  76.6 0.9 copy-done
  77.5 0.3 copy-done.2
  77.8 1.2 fusion.6
  78.9 1.2 fusion.5
  80.1 1.2 fusion.4
  81.2 1.2 fusion.9
  82.5 1.2 fusion.8
  83.7 0.5 convolution_add_fusion.1
  84.2 1.2 fusion.7
  85.4 0.5 convolution_add_fusion
  85.9 0.5 convolution_add_fusion.3
  86.4 0.5 convolution_add_fusion.2
  86.9 0.5 convolution_add_fusion.5
  87.3 0.5 convolution_add_fusion.4
  87.8 0.4 dynamic_update_slice.9
  88.2 0.5 add_dynamic-update-slice_fusion
  88.8 0.5 fusion
  89.3 0.0 copy-start.3
  89.3 1.1 slice.120
  90.4 5.2 %all-to-all-start = ((bf16[32,64,256]{2,1,0:T(8,128)(2,1)}), bf16[32,64,256]{2,1,0:T(8,128)(2,1)S(1)}, u32[]{:S(2)}, u32[]{:S(2)}) async-start(bf16[32,64,256]{2,1,0:T(8,128)(2,1)} %slice.120), calls=%async_computation | async-start | bytes 2097152 | tf_op jit(solution)/shard_map/all_to_all | solution.py:67
  95.6 0.2 all-reduce.4.cloned.1.call-start
  95.9 0.0 copy-done.3
  95.9 1.2 fusion.3
  97.0 1.2 fusion.2
  98.2 1.2 fusion.1
  99.4 3.3 %broadcast_multiply_fusion = f32[9,256,256]{2,1,0:T(8,128)} fusion(f32[9,256,256]{2,1,0:T(8,128)} %fusion.1), kind=kLoop, calls=%fused_computation.10 | loop fusion | flops 589824 | bytes 4718592 | tf_op jit(solution)/shard_map/mul | solution.py:69
  102.7 0.0 all-reduce.4.cloned.1.call-update
  102.7 20.3 %all-to-all-done = bf16[32,64,256]{2,1,0:T(8,128)(2,1)S(1)} async-done(((bf16[32,64,256]{2,1,0:T(8,128)(2,1)}), bf16[32,64,256]{2,1,0:T(8,128)(2,1)S(1)}, u32[]{:S(2)}, u32[]{:S(2)}) %all-to-all-start) | async-done | bytes 1048608 | tf_op jit(solution)/shard_map/all_to_all | solution.py:67
  123.0 0.6 copy.20
  123.6 1.3 all_to_all.29
  124.9 34.5 %all-reduce.4.cloned.1.call-done = f32[3,3,256,256]{3,2,1,0:T(8,128)} async-done(((f32[3,3,256,256]{3,2,1,0:T(8,128)}), f32[3,3,256,256]{3,2,1,0:T(8,128)}) %all-reduce.4.cloned.1.call-update) | async-done | bytes 2359312 | tf_op jit(solution)/shard_map/psum | solution.py:70
  159.3 3.2 %copy.32 = f32[3,3,256,256]{3,2,1,0:T(8,128)} copy(f32[3,3,256,256]{3,2,1,0:T(8,128)} %all-reduce.4.cloned.1.call-done) | data formatting | bytes 4718592
Async XLA Ops:
  7.2 65.3 %all-gather.2.cloned.1.call-start = ((), (), s32[]{:S(2)}) async-start(), calls=%async_computation.2 | async-start | bytes 1622016 | tf_op jit(solution)/shard_map/all_gather | solution.py:33
  8.0 3.7 %collective-permute-start = (bf16[4,12,256]{2,1,0:T(8,128)(2,1)S(1)}, bf16[4,12,256]{2,1,0:T(8,128)(2,1)S(1)}, u32[]{:S(2)}, u32[]{:S(2)}) collective-permute-start(bf16[4,12,256]{2,1,0:T(8,128)(2,1)S(1)} %get-tuple-element.5), channel_id=1, source_target_pairs={{0,1},{1,2},{2,3},{4,5},{5,6},{6,7},{8,9},{9,10},{10,11},{12,13},{... | collective-permute-start | bytes 73736 | tf_op jit(solution)/shard_map/ppermute | solution.py:18
  10.4 5.2 %collective-permute-start.1 = (bf16[4,12,256]{2,1,0:T(8,128)(2,1)S(1)}, bf16[4,12,256]{2,1,0:T(8,128)(2,1)S(1)}, u32[]{:S(2)}, u32[]{:S(2)}) collective-permute-start(bf16[4,12,256]{2,1,0:T(8,128)(2,1)S(1)} %get-tuple-element.6), channel_id=1, source_target_pairs={{1,0},{2,1},{3,2},{5,4},{6,5},{7,6},{9,8},{10,9},{11,10},{13,12},{... | collective-permute-start | bytes 73736 | tf_op jit(solution)/shard_map/ppermute | solution.py:19
  72.5 2.7 %copy-start.1 = (bf16[3,3,256,256]{3,2,1,0:T(8,128)(2,1)S(1)}, bf16[3,3,256,256]{3,2,1,0:T(8,128)(2,1)}, u32[]{:S(2)}) copy-start(bf16[3,3,256,256]{3,2,1,0:T(8,128)(2,1)} %param.5) | copy-start | bytes 3538948
  76.1 1.4 copy-start
  76.1 1.7 copy-start.2
  89.3 6.5 %copy-start.3 = (bf16[4,64,8,256]{3,1,0,2:T(8,128)(2,1)S(1)}, bf16[4,64,8,256]{3,1,0,2:T(8,128)(2,1)}, u32[]{:S(2)}) copy-start(bf16[4,64,8,256]{3,1,0,2:T(8,128)(2,1)} %copy.12) | copy-start | bytes 3145732
  90.4 32.5 %all-to-all-start = ((bf16[32,64,256]{2,1,0:T(8,128)(2,1)}), bf16[32,64,256]{2,1,0:T(8,128)(2,1)S(1)}, u32[]{:S(2)}, u32[]{:S(2)}) async-start(bf16[32,64,256]{2,1,0:T(8,128)(2,1)} %slice.120), calls=%async_computation | async-start | bytes 2097152 | tf_op jit(solution)/shard_map/all_to_all | solution.py:67
  95.6 63.7 %all-reduce.4.cloned.1.call-start = ((), (), s32[]{:S(2)}) async-start(), calls=%async_computation.3 | async-start | bytes 4718592 | tf_op jit(solution)/shard_map/psum | solution.py:70
Sparse Core Ops, SparseCore 0:
  17.3 54.6 all-gather.1
  102.8 56.4 all-reduce.3
where the time goes:
time: 170 us; the launch traced here: 169 us
  waiting for transfers between devices  58.7 us (35%)
  blocking collectives  45.4 us (27%)
  local copies, waits for them, and re-layouts  21.1 us (12%)
  matrix products  14.9 us (9%)
  between operations  14.2 us (8%)
  starting transfers between devices  9.09 us (5%)
  other arithmetic  5.97 us (4%)
    all_to_all x1, blocking collectives, shards(): lax.all_to_all(inputs, 'row', split_axis=2, concat_axis=0, tiled=True)  45.4 us
    psum x1, waiting for transfers between devices, shards(): grad_weight = lax.psum(terms, 'col')  34.5 us
    all_to_all x1, waiting for transfers between devices, shards(): lax.all_to_all(grad_strip, 'row', split_axis=0, concat_axis=2, tiled=True)  20.3 us
    unnamed x12, local copies, waits for them, and re-layouts  12.1 us
    dot_general x9, matrix products, shards(): lax.dot_general(in_rows, window, (((0,), (0,)), ((), ())), preferred_elem...  10.7 us
    all_to_all x1, starting transfers between devices, shards(): lax.all_to_all(grad_strip, 'row', split_axis=0, concat_axis=2, tiled=True)  5.18 us
    dot_general x9, matrix products, shards(): lax.dot_general(window, weight[kernel_tap_row, kernel_tap_column], (((1,)...  4.21 us
    ppermute x1, waiting for transfers between devices, extended(): after = lax.ppermute(initial, axis, down)  3.9 us
  transfers between devices with their start and end apart: 5, of which 3 were waited for; matrix products, arithmetic and copies ran while one was open for 10% of the time, Pallas kernels for 0%

commit v1 on v0

--- a/solution.py
+++ b/solution.py
@@ -3,9 +3,146 @@
 import jax
 import jax.numpy as jnp
 from jax import lax
+from jax.experimental import pallas as pl
+from jax.experimental.pallas import tpu as pltpu
 from jax.sharding import PartitionSpec as P
 
 DILATION_STEP = 12
+VMEM_LIMIT = 48 * 1024 * 1024
+
+
+def swap(x, axis, bit):
+    return lax.ppermute(x, axis, [(i, i ^ bit) for i in range(lax.axis_size(axis))])
+
+
+def rims(x, width):
+    peers, length = lax.axis_size("col"), x.shape[-2]
+    up = [(i, i + 1) for i in range(peers - 1)]
+    down = [(j, i) for i, j in up]
+    before = lax.ppermute(x[..., length - width :, :], "col", up)
+    after = lax.ppermute(x[..., :width, :], "col", down)
+    return before, after
+
+
+def back_kernel(me_ref, own_ref, z_refs, y_ref, left_ref, right_ref, weight_ref, back_ref, windows_ref):
+    me = me_ref[0]
+    tiles, positions, chans = back_ref.shape
+    rows, step, outs = left_ref.shape[1:]
+    width = positions // rows
+    shift = DILATION_STEP // rows
+    for k in range(tiles):
+        if k % 2:
+            tile = y_ref[k // 2]
+        else:
+            tile = z_refs[k // 2 - 1][...] if k else own_ref[...]
+        tile = tile.astype(jnp.float32)
+        left = left_ref[k].astype(jnp.float32)
+        right = right_ref[k].astype(jnp.float32)
+        shifted = (
+            jnp.concatenate([tile[:, step:], right], axis=1),
+            tile,
+            jnp.concatenate([left, tile[:, : width - step]], axis=1),
+        )
+        for b in range(3):
+            windows_ref[me ^ k, :, b * outs : (b + 1) * outs] = (
+                shifted[b].reshape(positions, outs).astype(jnp.bfloat16)
+            )
+    for j in range(tiles):
+        taps = [a for a in range(3) if 0 <= j - shift * (a - 1) < tiles]
+        lhs = jnp.concatenate([windows_ref[j - shift * (a - 1)] for a in taps], axis=1)
+        rhs = weight_ref[taps[0] * 3 * outs : (taps[-1] + 1) * 3 * outs, :]
+        back_ref[j] = jnp.dot(lhs, rhs, preferred_element_type=jnp.float32).astype(back_ref.dtype)
+
+
+def taps_kernel(rows, scale, core_ref, in_ref, windows_ref, mine_ref, other_ref, flipped_ref):
+    core = core_ref[0]
+    tiles, positions, chans = in_ref.shape
+    half = chans // 2
+    outs = windows_ref.shape[2] // 3
+    shift = DILATION_STEP // rows
+    for j in range(tiles):
+        x = in_ref[j]
+        low, high = x[:, :half], x[:, half:]
+        mine = jnp.where(core == 0, low, high)
+        other = jnp.where(core == 0, high, low)
+        flipped_ref[:half, j * positions : (j + 1) * positions] = mine.T
+        flipped_ref[half:, j * positions : (j + 1) * positions] = other.T
+    for a in range(3):
+        move = shift * (a - 1)
+        first, last = max(0, move), min(tiles, tiles + move)
+        lhs = flipped_ref[:, first * positions : last * positions]
+        rhs = windows_ref[first - move : last - move].reshape((last - first) * positions, 3 * outs)
+        terms = jnp.dot(lhs, rhs, preferred_element_type=jnp.float32) * scale
+        for b in range(3):
+            mine_ref[3 * a + b] = terms[:half, b * outs : (b + 1) * outs]
+            other_ref[3 * a + b] = terms[half:, b * outs : (b + 1) * outs]
+
+
+def vmem(n):
+    return [pl.BlockSpec(memory_space=pltpu.VMEM)] * n
+
+
+def quick(inputs, output_gradient, weight):
+    rows, width, in_chans = inputs.shape
+    outs = output_gradient.shape[2]
+    tiles = lax.axis_size("row")
+    panel = in_chans // tiles
+    positions = rows * width
+    me = lax.axis_index("row").astype(jnp.int32)
+    core = (lax.axis_index("col") % 2).astype(jnp.int32)
+    params = pltpu.CompilerParams(vmem_limit_bytes=VMEM_LIMIT)
+
+    z_tiles = [swap(output_gradient, "row", k) for k in (2, 4, 6)]
+    blocks = inputs.reshape(positions, tiles, panel).transpose(1, 0, 2)
+    in_strip = lax.all_to_all(blocks, "row", split_axis=0, concat_axis=0, tiled=True)
+
+    column = jnp.stack([output_gradient, *z_tiles])
+    y_tiles = swap(column, "row", 1)
+    both = jnp.stack([column, y_tiles], axis=1).reshape(tiles, rows, width, outs)
+    left, right = rims(both, DILATION_STEP)
+    flat_weight = weight.transpose(0, 1, 3, 2).reshape(9 * outs, panel)
+
+    smem = pl.BlockSpec(memory_space=pltpu.SMEM)
+    back, windows = pl.pallas_call(
+        lambda me_ref, own, z1, z2, z3, y, lf, rt, w, back_ref, win_ref: back_kernel(
+            me_ref, own, (z1, z2, z3), y, lf, rt, w, back_ref, win_ref
+        ),
+        out_shape=(
+            jax.ShapeDtypeStruct((tiles, positions, panel), jnp.bfloat16),
+            jax.ShapeDtypeStruct((tiles, positions, 3 * outs), jnp.bfloat16),
+        ),
+        in_specs=[smem] + vmem(8),
+        out_specs=tuple(vmem(2)),
+        compiler_params=params,
+        name="back",
+    )(me.reshape(1), output_gradient, *z_tiles, y_tiles, left, right, flat_weight)
+
+    height = rows * tiles
+    scale = 1.0 / math.sqrt(height * width * lax.axis_size("col"))
+    half = jax.ShapeDtypeStruct((9, panel // 2, outs), jnp.float32)
+    mine, other = pl.pallas_call(
+        lambda *refs: taps_kernel(rows, scale, *refs),
+        out_shape=(half, half),
+        in_specs=[smem] + vmem(2),
+        out_specs=tuple(vmem(2)),
+        scratch_shapes=[pltpu.VMEM((panel, tiles * positions), jnp.bfloat16)],
+        compiler_params=params,
+        name="taps",
+    )(core.reshape(1), in_strip, windows)
+
+    grad_back = lax.all_to_all(back, "row", split_axis=0, concat_axis=0, tiled=True)
+    grad_in = grad_back.transpose(1, 0, 2).reshape(rows, width, in_chans)
+
+    chip = [mine[3 * a : 3 * a + 3] + swap(other[3 * a : 3 * a + 3], "col", 1) for a in range(3)]
+    total = [c + swap(c, "col", 2) for c in chip]
+    sibling = [swap(t, "col", 1) for t in total]
+    grad_weight = jnp.stack(
+        [
+            jnp.where(core == 0, jnp.concatenate([t, s], axis=1), jnp.concatenate([s, t], axis=1))
+            for t, s in zip(total, sibling)
+        ]
+    ).reshape(3, 3, panel, outs)
+    return grad_in, grad_weight
 
 
 def extended(x, sides, width):
@@ -21,7 +158,7 @@
     return x
 
 
-def shards(inputs, output_gradient, weight):
+def general(inputs, output_gradient, weight):
     height, width, in_chans = inputs.shape
     out_chans = output_gradient.shape[2]
     step = DILATION_STEP
@@ -71,6 +208,21 @@
     return (grad_in, grad_weight)
 
 
+def shards(inputs, output_gradient, weight):
+    rows, width, in_chans = inputs.shape
+    tiles, strips = lax.axis_size("row"), lax.axis_size("col")
+    fits = (
+        tiles == 8
+        and strips == 4
+        and DILATION_STEP % rows == 0
+        and DILATION_STEP <= width
+        and width % 16 == 0
+        and in_chans % (tiles * 256) == 0
+        and output_gradient.shape[2] % 128 == 0
+    )
+    return (quick if fits else general)(inputs, output_gradient, weight)
+
+
 def solution(mesh):
     return jax.shard_map(
         shards,

time: 170 us -> 125 us (0.74)
  blocking collectives: 45.4 us -> 0 us
  starting transfers between devices: 9.09 us -> 29.9 us
  matrix products: 14.9 us -> 0 us
  between operations: 14.2 us -> 0.82 us
  local copies, waits for them, and re-layouts: 21.1 us -> 8.17 us
  waiting for transfers between devices: 58.7 us -> 71.4 us
  Pallas kernels: 0 us -> 8.69 us
    ppermute x2 -> x15, waiting for transfers between devices: 3.9 us -> 71.4 us  [the longest x13 68.8 us: swap(): lax.ppermute(x, axis, [(i, i ^ bit) for i in range(lax.axis_size(axis))])]
    all_to_all x1 -> x0, blocking collectives: 45.4 us -> none  [shards(): lax.all_to_all(inputs, 'row', split_axis=2, concat_axis=0, tiled=True)]
    psum x1 -> x0, waiting for transfers between devices: 34.5 us -> none  [shards(): grad_weight = lax.psum(terms, 'col')]
    all_to_all x1 -> x2, waiting for transfers between devices: 20.3 us -> 0.01 us  [the longest x1 0.01 us: quick(): lax.all_to_all(blocks, 'row', split_axis=0, concat_axis=0, tiled=True)]
    dot_general x18 -> x0, matrix products: 14.9 us -> none  [the longest x9 10.7 us: shards(): lax.dot_general(in_rows, window, (((0,), (0,)), ((), ())), preferred_elem...]
    ppermute x2 -> x15, starting transfers between devices: 3.65 us -> 15.9 us  [the longest x13 13.3 us: swap(): lax.ppermute(x, axis, [(i, i ^ bit) for i in range(lax.axis_size(axis))])]
    unnamed x12 -> x5, local copies, waits for them, and re-layouts: 12.1 us -> 2.5 us
    all_to_all x1 -> x2, starting transfers between devices: 5.18 us -> 14.1 us  [the longest x1 7.28 us: quick(): lax.all_to_all(blocks, 'row', split_axis=0, concat_axis=0, tiled=True)]
  transfers between devices with their start and end apart: 5 -> 17, of which waited for: 3 -> 10; matrix products, arithmetic and copies ran while one was open for 10% -> 6% of each run, Pallas kernels for 0% -> 7%
where the time goes in v1:
time: 125 us
  waiting for transfers between devices  71.4 us (57%)
  starting transfers between devices  29.9 us (24%)
  Pallas kernels  8.69 us (7%)
  local copies, waits for them, and re-layouts  8.17 us (7%)
  other arithmetic  5.72 us (5%)
    ppermute x13, waiting for transfers between devices, swap(): lax.ppermute(x, axis, [(i, i ^ bit) for i in range(lax.axis_size(axis))])  68.8 us
    ppermute x13, starting transfers between devices, swap(): lax.ppermute(x, axis, [(i, i ^ bit) for i in range(lax.axis_size(axis))])  13.3 us
    all_to_all x1, starting transfers between devices, quick(): lax.all_to_all(blocks, 'row', split_axis=0, concat_axis=0, tiled=True)  7.28 us
    all_to_all x1, starting transfers between devices, quick(): lax.all_to_all(back, 'row', split_axis=0, concat_axis=0, tiled=True)  6.78 us
    pallas_call x1, Pallas kernels, quick(): pl.pallas_call(lambda me_ref, own, z1, z2, z3, y, lf, rt, w, back_ref, wi...  4.74 us
    pallas_call x1, Pallas kernels, quick(): pl.pallas_call(lambda *refs: taps_kernel(rows, scale, *refs), out_shape=(...  3.95 us
    select_n x3, other arithmetic, quick(): jnp.where(core == 0, jnp.concatenate([t, s], axis=1), jnp.concatenate([s,...  3.62 us
    ppermute x1, waiting for transfers between devices, rims(): after = lax.ppermute(x[..., :width, :], 'col', down)  2.59 us
  transfers between devices with their start and end apart: 17, of which 10 were waited for; matrix products, arithmetic and copies ran while one was open for 6% of the time, Pallas kernels for 7%

profile of v1, /device:TPU:0, one launch (start us, length us, event | category | flops | bytes accessed | tf_op | source)
XLA Modules:
  0.0 124.7 jit_solution(3140058272113015479)
XLA Ops:
  0.6 1.5 %copy.11 = bf16[32,8,8,256]{3,2,1,0:T(8,128)(2,1)S(1)} copy(bf16[32,8,8,256]{3,1,2,0:T(8,128)(2,1)} %bitcast.38) | data formatting | bytes 2097152
  2.2 0.0 copy-start.1
  2.2 1.2 copy.13
  3.3 7.3 %all-to-all-start.1 = ((bf16[8,256,256]{2,1,0:T(8,128)(2,1)}), bf16[8,256,256]{2,1,0:T(8,128)(2,1)S(1)}, u32[]{:S(2)}, u32[]{:S(2)}) async-start(bf16[8,256,256]{2,1,0:T(8,128)(2,1)} %bitcast.24), calls=%async_computation.1 | async-start | bytes 2097152 | tf_op jit(solution)/shard_map/all_to_all | solution.py:97
  10.6 0.0 copy-done.1
  10.6 2.0 %collective-permute-start = (bf16[4,64,256]{2,1,0:T(8,128)(2,1)S(1)}, bf16[4,64,256]{2,1,0:T(8,128)(2,1)S(1)}, u32[]{:S(2)}, u32[]{:S(2)}) collective-permute-start(bf16[4,64,256]{2,1,0:T(8,128)(2,1)S(1)} %copy-done.1), channel_id=1, source_target_pairs={{0,8},{4,12},{8,0},{12,4},{16,24},{20,28},{24,16},{28,20},{1,9},{5... | collective-permute-start | bytes 393224 | tf_op jit(solution)/shard_map/ppermute | solution.py:15
  12.7 2.4 %collective-permute-start.1 = (bf16[4,64,256]{2,1,0:T(8,128)(2,1)S(1)}, bf16[4,64,256]{2,1,0:T(8,128)(2,1)S(1)}, u32[]{:S(2)}, u32[]{:S(2)}) collective-permute-start(bf16[4,64,256]{2,1,0:T(8,128)(2,1)S(1)} %copy-done.1), channel_id=1, source_target_pairs={{0,16},{4,20},{8,24},{12,28},{16,0},{20,4},{24,8},{28,12},{1,17},{... | collective-permute-start | bytes 393224 | tf_op jit(solution)/shard_map/ppermute | solution.py:15
  15.0 0.1 collective-permute-start.2
  15.1 16.6 %collective-permute-done.z1 = bf16[4,64,256]{2,1,0:T(8,128)(2,1)S(1)} collective-permute-done((bf16[4,64,256]{2,1,0:T(8,128)(2,1)S(1)}, bf16[4,64,256]{2,1,0:T(8,128)(2,1)S(1)}, u32[]{:S(2)}, u32[]{:S(2)}) %collective-permute-start) | collective-permute-done | bytes 131104 | tf_op jit(solution)/shard_map/ppermute | solution.py:15
  31.7 14.6 %collective-permute-done.1.z2 = bf16[4,64,256]{2,1,0:T(8,128)(2,1)S(1)} collective-permute-done((bf16[4,64,256]{2,1,0:T(8,128)(2,1)S(1)}, bf16[4,64,256]{2,1,0:T(8,128)(2,1)S(1)}, u32[]{:S(2)}, u32[]{:S(2)}) %collective-permute-start.1) | collective-permute-done | bytes 131104 | tf_op jit(solution)/shard_map/ppermute | solution.py:15
  46.2 0.0 collective-permute-done.2.z3
  46.2 0.1 fusion
  46.3 1.1 collective-permute-start.3
  47.5 10.1 %collective-permute-done.3.y = bf16[4,4,64,256]{3,2,1,0:T(8,128)(2,1)S(1)} collective-permute-done((bf16[4,4,64,256]{3,2,1,0:T(8,128)(2,1)S(1)}, bf16[4,4,64,256]{3,2,1,0:T(8,128)(2,1)S(1)}, u32[]{:S(2)}, u32[]{:S(2)}) %collective-permute-start.3) | collective-permute-done | bytes 524320 | tf_op jit(solution)/shard_map/ppermute | solution.py:15
  57.5 0.1 pad_maximum_fusion.1
  57.7 0.1 copy.7
  57.8 0.9 fusion.2
  58.6 1.3 %collective-permute-start.4 = (bf16[8,4,12,256]{3,2,1,0:T(8,128)(2,1)}, bf16[8,4,12,256]{3,2,1,0:T(8,128)(2,1)S(1)}, u32[]{:S(2)}, u32[]{:S(2)}) collective-permute-start(bf16[8,4,12,256]{3,2,1,0:T(8,128)(2,1)} %get-tuple-element.17), channel_id=1, source_target_pairs={{0,1},{1,2},{2,3},{4,5},{5,6},{6,7},{8,9},{9,10},{10,11},{12,13},{... | collective-permute-start | bytes 589832 | tf_op jit(solution)/shard_map/ppermute | solution.py:22
  59.9 1.3 %collective-permute-start.5 = (bf16[8,4,12,256]{3,2,1,0:T(8,128)(2,1)}, bf16[8,4,12,256]{3,2,1,0:T(8,128)(2,1)}, u32[]{:S(2)}, u32[]{:S(2)}) collective-permute-start(bf16[8,4,12,256]{3,2,1,0:T(8,128)(2,1)} %get-tuple-element.16), channel_id=1, source_target_pairs={{1,0},{2,1},{3,2},{5,4},{6,5},{7,6},{9,8},{10,9},{11,10},{13,12},{... | collective-permute-start | bytes 589832 | tf_op jit(solution)/shard_map/ppermute | solution.py:23
  61.2 1.6 %copy.8 = bf16[3,3,256,256]{3,2,1,0:T(8,128)(2,1)S(1)} copy(bf16[3,3,256,256]{2,3,1,0:T(8,128)(2,1)} %bitcast.37) | data formatting | bytes 2359296 | tf_op jit(solution)/shard_map/transpose | solution.py:103
  62.8 0.0 collective-permute-done.4.lf
  62.8 2.6 %collective-permute-done.5.rt = bf16[8,4,12,256]{3,2,1,0:T(8,128)(2,1)} collective-permute-done((bf16[8,4,12,256]{3,2,1,0:T(8,128)(2,1)}, bf16[8,4,12,256]{3,2,1,0:T(8,128)(2,1)}, u32[]{:S(2)}, u32[]{:S(2)}) %collective-permute-start.5) | collective-permute-done | bytes 196640 | tf_op jit(solution)/shard_map/ppermute | solution.py:23
  65.4 4.7 %back.1 = (bf16[8,256,256]{2,1,0:T(8,128)(2,1)S(1)}, bf16[8,256,768]{2,1,0:T(8,128)(2,1)}) custom-call(s32[1]{0:T(128)} %bitcast.me_ref, bf16[4,64,256]{2,1,0:T(8,128)(2,1)S(1)} %copy-done.1, bf16[4,64,256]{2,1,0:T(8,128)(2,1)S(1)} %collective-permute-done.z1, bf16[4,64,256]{2,1,0:T(8,128)(2,1)S(1)} %collective-permute-done.1.z2, ...), custom_call_target="tpu_custom_call" | custom-call | tf_op jit(solution)/shard_map/back/pallas_call | solution.py:106
  70.1 0.0 copy-start
  70.1 1.0 copy-done
  71.1 0.0 all-to-all-done.1.refs_1_
  71.1 6.8 %all-to-all-start = ((bf16[8,256,256]{2,1,0:T(8,128)(2,1)}), bf16[8,256,256]{2,1,0:T(8,128)(2,1)S(1)}, u32[]{:S(2)}, u32[]{:S(2)}) async-start(bf16[8,256,256]{2,1,0:T(8,128)(2,1)} %copy-done), calls=%async_computation | async-start | bytes 2097152 | tf_op jit(solution)/shard_map/all_to_all | solution.py:133
  77.9 3.9 %taps.1 = (f32[9,128,256]{2,1,0:T(8,128)S(1)}, f32[9,128,256]{2,1,0:T(8,128)S(1)}) custom-call(s32[1]{0:T(128)} %bitcast.11.refs_0_, bf16[8,256,256]{2,1,0:T(8,128)(2,1)S(1)} %all-to-all-done.1.refs_1_, bf16[8,256,768]{2,1,0:T(8,128)(2,1)} %get-tuple-element.7.refs_2_), custom_call_target="tpu_custom_call" | custom-call | tf_op jit(solution)/shard_map/taps/pallas_call | solution.py:123
  81.9 0.1 fusion.1
  81.9 4.5 %collective-permute-start.6 = (f32[3,128,256]{2,1,0:T(8,128)S(1)}, f32[3,128,256]{2,1,0:T(8,128)S(1)}, u32[]{:S(2)}, u32[]{:S(2)}) collective-permute-start(f32[3,128,256]{2,1,0:T(8,128)S(1)} %get-tuple-element.13), channel_id=1, source_target_pairs={{0,1},{1,0},{2,3},{3,2},{4,5},{5,4},{6,7},{7,6},{8,9},{9,8},{10,11... | collective-permute-start | bytes 1179656 | tf_op jit(solution)/shard_map/ppermute | solution.py:15
  86.5 0.1 collective-permute-start.12
  86.5 0.4 collective-permute-start.9
  87.0 0.8 collective-permute-done.6
  87.8 0.6 collective-permute-done.12
  88.4 0.6 collective-permute-done.9
  88.9 0.2 slice_add_fusion.2
  89.1 0.4 collective-permute-start.13
  89.5 1.7 %collective-permute-start.10 = (f32[3,128,256]{2,1,0:T(8,128)S(1)}, f32[3,128,256]{2,1,0:T(8,128)S(1)}, u32[]{:S(2)}, u32[]{:S(2)}) collective-permute-start(f32[3,128,256]{2,1,0:T(8,128)S(1)} %get-tuple-element.12), channel_id=1, source_target_pairs={{0,2},{1,3},{2,0},{3,1},{4,6},{5,7},{6,4},{7,5},{8,10},{9,11},{10,... | collective-permute-start | bytes 1179656 | tf_op jit(solution)/shard_map/ppermute | solution.py:15
  91.2 0.4 collective-permute-start.7
  91.6 9.5 %collective-permute-done.13 = f32[3,128,256]{2,1,0:T(8,128)S(1)} collective-permute-done((f32[3,128,256]{2,1,0:T(8,128)S(1)}, f32[3,128,256]{2,1,0:T(8,128)S(1)}, u32[]{:S(2)}, u32[]{:S(2)}) %collective-permute-start.13) | collective-permute-done | bytes 393248 | tf_op jit(solution)/shard_map/ppermute | solution.py:15
  101.1 0.1 add.28
  101.2 0.1 collective-permute-start.14
  101.2 8.3 %collective-permute-done.10 = f32[3,128,256]{2,1,0:T(8,128)S(1)} collective-permute-done((f32[3,128,256]{2,1,0:T(8,128)S(1)}, f32[3,128,256]{2,1,0:T(8,128)S(1)}, u32[]{:S(2)}, u32[]{:S(2)}) %collective-permute-start.10) | collective-permute-done | bytes 393248 | tf_op jit(solution)/shard_map/ppermute | solution.py:15
  109.5 0.1 add.26
  109.6 0.1 collective-permute-start.11
  109.7 7.7 %collective-permute-done.7 = f32[3,128,256]{2,1,0:T(8,128)S(1)} collective-permute-done((f32[3,128,256]{2,1,0:T(8,128)S(1)}, f32[3,128,256]{2,1,0:T(8,128)S(1)}, u32[]{:S(2)}, u32[]{:S(2)}) %collective-permute-start.7) | collective-permute-done | bytes 393248 | tf_op jit(solution)/shard_map/ppermute | solution.py:15
  117.4 0.1 add.24
  117.5 0.1 collective-permute-start.8
  117.6 0.0 all-to-all-done
  117.6 0.6 copy.9
  118.2 1.3 %reshape.190 = bf16[4,64,2048]{2,1,0:T(8,128)(2,1)} reshape(bf16[256,8,256]{2,1,0:T(8,128)(2,1)S(1)} %copy.9) | data formatting | bytes 2097152 | tf_op jit(solution)/shard_map/reshape | solution.py:134
  119.5 0.0 collective-permute-done.14
  119.5 1.2 maximum_select_fusion.2
  120.7 0.0 collective-permute-done.11
  120.7 1.2 maximum_select_fusion.1
  121.9 0.0 collective-permute-done.8
  121.9 1.2 maximum_select_fusion
  123.1 1.6 %pad_maximum_fusion = f32[3,3,256,256]{3,2,1,0:T(8,128)} fusion(f32[1,3,256,256]{3,2,1,0:T(8,128)S(1)} %maximum_select_fusion.2, f32[1,3,256,256]{3,2,1,0:T(8,128)S(1)} %maximum_select_fusion.1, f32[1,3,256,256]{3,2,1,0:T(8,128)S(1)} %maximum_select_fusion), kind=kLoop, calls=%fused_computation | loop fusion | flops 1179648 | bytes 4718592 | tf_op jit(solution)/shard_map/stack | solution.py:139
Async XLA Ops:
  2.2 8.5 %copy-start.1 = (bf16[4,64,256]{2,1,0:T(8,128)(2,1)S(1)}, bf16[4,64,256]{2,1,0:T(8,128)(2,1)}, u32[]{:S(2)}) copy-start(bf16[4,64,256]{2,1,0:T(8,128)(2,1)} %own.1) | copy-start | bytes 393220
  3.3 67.8 %all-to-all-start.1 = ((bf16[8,256,256]{2,1,0:T(8,128)(2,1)}), bf16[8,256,256]{2,1,0:T(8,128)(2,1)S(1)}, u32[]{:S(2)}, u32[]{:S(2)}) async-start(bf16[8,256,256]{2,1,0:T(8,128)(2,1)} %bitcast.24), calls=%async_computation.1 | async-start | bytes 2097152 | tf_op jit(solution)/shard_map/all_to_all | solution.py:97
  10.6 21.0 %collective-permute-start = (bf16[4,64,256]{2,1,0:T(8,128)(2,1)S(1)}, bf16[4,64,256]{2,1,0:T(8,128)(2,1)S(1)}, u32[]{:S(2)}, u32[]{:S(2)}) collective-permute-start(bf16[4,64,256]{2,1,0:T(8,128)(2,1)S(1)} %copy-done.1), channel_id=1, source_target_pairs={{0,8},{4,12},{8,0},{12,4},{16,24},{20,28},{24,16},{28,20},{1,9},{5... | collective-permute-start | bytes 393224 | tf_op jit(solution)/shard_map/ppermute | solution.py:15
  12.7 33.6 %collective-permute-start.1 = (bf16[4,64,256]{2,1,0:T(8,128)(2,1)S(1)}, bf16[4,64,256]{2,1,0:T(8,128)(2,1)S(1)}, u32[]{:S(2)}, u32[]{:S(2)}) collective-permute-start(bf16[4,64,256]{2,1,0:T(8,128)(2,1)S(1)} %copy-done.1), channel_id=1, source_target_pairs={{0,16},{4,20},{8,24},{12,28},{16,0},{20,4},{24,8},{28,12},{1,17},{... | collective-permute-start | bytes 393224 | tf_op jit(solution)/shard_map/ppermute | solution.py:15
  15.0 31.2 %collective-permute-start.2 = (bf16[4,64,256]{2,1,0:T(8,128)(2,1)S(1)}, bf16[4,64,256]{2,1,0:T(8,128)(2,1)S(1)}, u32[]{:S(2)}, u32[]{:S(2)}) collective-permute-start(bf16[4,64,256]{2,1,0:T(8,128)(2,1)S(1)} %copy-done.1), channel_id=1, source_target_pairs={{0,24},{4,28},{8,16},{12,20},{16,8},{20,12},{24,0},{28,4},{1,25},{... | collective-permute-start | bytes 393224 | tf_op jit(solution)/shard_map/ppermute | solution.py:15
  46.3 11.2 %collective-permute-start.3 = (bf16[4,4,64,256]{3,2,1,0:T(8,128)(2,1)S(1)}, bf16[4,4,64,256]{3,2,1,0:T(8,128)(2,1)S(1)}, u32[]{:S(2)}, u32[]{:S(2)}) collective-permute-start(bf16[4,4,64,256]{3,2,1,0:T(8,128)(2,1)S(1)} %get-tuple-element.19), channel_id=1, source_target_pairs={{0,4},{4,0},{8,12},{12,8},{16,20},{20,16},{24,28},{28,24},{1,5},{5... | collective-permute-start | bytes 1572872 | tf_op jit(solution)/shard_map/ppermute | solution.py:15
  58.6 4.2 %collective-permute-start.4 = (bf16[8,4,12,256]{3,2,1,0:T(8,128)(2,1)}, bf16[8,4,12,256]{3,2,1,0:T(8,128)(2,1)S(1)}, u32[]{:S(2)}, u32[]{:S(2)}) collective-permute-start(bf16[8,4,12,256]{3,2,1,0:T(8,128)(2,1)} %get-tuple-element.17), channel_id=1, source_target_pairs={{0,1},{1,2},{2,3},{4,5},{5,6},{6,7},{8,9},{9,10},{10,11},{12,13},{... | collective-permute-start | bytes 589832 | tf_op jit(solution)/shard_map/ppermute | solution.py:22
  59.9 5.5 %collective-permute-start.5 = (bf16[8,4,12,256]{3,2,1,0:T(8,128)(2,1)}, bf16[8,4,12,256]{3,2,1,0:T(8,128)(2,1)}, u32[]{:S(2)}, u32[]{:S(2)}) collective-permute-start(bf16[8,4,12,256]{3,2,1,0:T(8,128)(2,1)} %get-tuple-element.16), channel_id=1, source_target_pairs={{1,0},{2,1},{3,2},{5,4},{6,5},{7,6},{9,8},{10,9},{11,10},{13,12},{... | collective-permute-start | bytes 589832 | tf_op jit(solution)/shard_map/ppermute | solution.py:23
  70.1 1.0 copy-start
  71.1 46.4 %all-to-all-start = ((bf16[8,256,256]{2,1,0:T(8,128)(2,1)}), bf16[8,256,256]{2,1,0:T(8,128)(2,1)S(1)}, u32[]{:S(2)}, u32[]{:S(2)}) async-start(bf16[8,256,256]{2,1,0:T(8,128)(2,1)} %copy-done), calls=%async_computation | async-start | bytes 2097152 | tf_op jit(solution)/shard_map/all_to_all | solution.py:133
  81.9 5.9 %collective-permute-start.6 = (f32[3,128,256]{2,1,0:T(8,128)S(1)}, f32[3,128,256]{2,1,0:T(8,128)S(1)}, u32[]{:S(2)}, u32[]{:S(2)}) collective-permute-start(f32[3,128,256]{2,1,0:T(8,128)S(1)} %get-tuple-element.13), channel_id=1, source_target_pairs={{0,1},{1,0},{2,3},{3,2},{4,5},{5,4},{6,7},{7,6},{8,9},{9,8},{10,11... | collective-permute-start | bytes 1179656 | tf_op jit(solution)/shard_map/ppermute | solution.py:15
  86.5 1.9 %collective-permute-start.12 = (f32[3,128,256]{2,1,0:T(8,128)S(1)}, f32[3,128,256]{2,1,0:T(8,128)S(1)}, u32[]{:S(2)}, u32[]{:S(2)}) collective-permute-start(f32[3,128,256]{2,1,0:T(8,128)S(1)} %get-tuple-element.14), channel_id=1, source_target_pairs={{0,1},{1,0},{2,3},{3,2},{4,5},{5,4},{6,7},{7,6},{8,9},{9,8},{10,11... | collective-permute-start | bytes 1179656 | tf_op jit(solution)/shard_map/ppermute | solution.py:15
  86.5 2.4 %collective-permute-start.9 = (f32[3,128,256]{2,1,0:T(8,128)S(1)}, f32[3,128,256]{2,1,0:T(8,128)S(1)}, u32[]{:S(2)}, u32[]{:S(2)}) collective-permute-start(f32[3,128,256]{2,1,0:T(8,128)S(1)} %get-tuple-element.15), channel_id=1, source_target_pairs={{0,1},{1,0},{2,3},{3,2},{4,5},{5,4},{6,7},{7,6},{8,9},{9,8},{10,11... | collective-permute-start | bytes 1179656 | tf_op jit(solution)/shard_map/ppermute | solution.py:15
  89.1 12.0 %collective-permute-start.13 = (f32[3,128,256]{2,1,0:T(8,128)S(1)}, f32[3,128,256]{2,1,0:T(8,128)S(1)}, u32[]{:S(2)}, u32[]{:S(2)}) collective-permute-start(f32[3,128,256]{2,1,0:T(8,128)S(1)} %get-tuple-element.11), channel_id=1, source_target_pairs={{0,2},{1,3},{2,0},{3,1},{4,6},{5,7},{6,4},{7,5},{8,10},{9,11},{10,... | collective-permute-start | bytes 1179656 | tf_op jit(solution)/shard_map/ppermute | solution.py:15
  89.5 20.0 %collective-permute-start.10 = (f32[3,128,256]{2,1,0:T(8,128)S(1)}, f32[3,128,256]{2,1,0:T(8,128)S(1)}, u32[]{:S(2)}, u32[]{:S(2)}) collective-permute-start(f32[3,128,256]{2,1,0:T(8,128)S(1)} %get-tuple-element.12), channel_id=1, source_target_pairs={{0,2},{1,3},{2,0},{3,1},{4,6},{5,7},{6,4},{7,5},{8,10},{9,11},{10,... | collective-permute-start | bytes 1179656 | tf_op jit(solution)/shard_map/ppermute | solution.py:15
  91.2 26.2 %collective-permute-start.7 = (f32[3,128,256]{2,1,0:T(8,128)S(1)}, f32[3,128,256]{2,1,0:T(8,128)S(1)}, u32[]{:S(2)}, u32[]{:S(2)}) collective-permute-start(f32[3,128,256]{2,1,0:T(8,128)S(1)} %get-tuple-element.10), channel_id=1, source_target_pairs={{0,2},{1,3},{2,0},{3,1},{4,6},{5,7},{6,4},{7,5},{8,10},{9,11},{10,... | collective-permute-start | bytes 1179656 | tf_op jit(solution)/shard_map/ppermute | solution.py:15
  101.2 18.3 %collective-permute-start.14 = (f32[3,128,256]{2,1,0:T(8,128)S(1)}, f32[3,128,256]{2,1,0:T(8,128)}, u32[]{:S(2)}, u32[]{:S(2)}) collective-permute-start(f32[3,128,256]{2,1,0:T(8,128)S(1)} %add.28), channel_id=1, source_target_pairs={{0,1},{1,0},{2,3},{3,2},{4,5},{5,4},{6,7},{7,6},{8,9},{9,8},{10,11... | collective-permute-start | bytes 1179656 | tf_op jit(solution)/shard_map/ppermute | solution.py:15
  109.6 11.1 %collective-permute-start.11 = (f32[3,128,256]{2,1,0:T(8,128)S(1)}, f32[3,128,256]{2,1,0:T(8,128)}, u32[]{:S(2)}, u32[]{:S(2)}) collective-permute-start(f32[3,128,256]{2,1,0:T(8,128)S(1)} %add.26), channel_id=1, source_target_pairs={{0,1},{1,0},{2,3},{3,2},{4,5},{5,4},{6,7},{7,6},{8,9},{9,8},{10,11... | collective-permute-start | bytes 1179656 | tf_op jit(solution)/shard_map/ppermute | solution.py:15
  117.5 4.4 %collective-permute-start.8 = (f32[3,128,256]{2,1,0:T(8,128)S(1)}, f32[3,128,256]{2,1,0:T(8,128)}, u32[]{:S(2)}, u32[]{:S(2)}) collective-permute-start(f32[3,128,256]{2,1,0:T(8,128)S(1)} %add.24), channel_id=1, source_target_pairs={{0,1},{1,0},{2,3},{3,2},{4,5},{5,4},{6,7},{7,6},{8,9},{9,8},{10,11... | collective-permute-start | bytes 1179656 | tf_op jit(solution)/shard_map/ppermute | solution.py:15

commit v2 on v0

--- a/solution.py
+++ b/solution.py
@@ -3,9 +3,260 @@
 import jax
 import jax.numpy as jnp
 from jax import lax
+from jax.experimental import pallas as pl
+from jax.experimental.pallas import tpu as pltpu
 from jax.sharding import PartitionSpec as P
 
 DILATION_STEP = 12
+VMEM_LIMIT = 32 * 1024 * 1024
+
+
+def swap(x, axis, bit):
+    return lax.ppermute(x, axis, [(i, i ^ bit) for i in range(lax.axis_size(axis))])
+
+
+def rims(x, width):
+    peers, length = lax.axis_size("col"), x.shape[-2]
+    up = [(i, i + 1) for i in range(peers - 1)]
+    down = [(j, i) for i, j in up]
+    before = lax.ppermute(x[..., length - width :, :], "col", up)
+    after = lax.ppermute(x[..., :width, :], "col", down)
+    return before, after
+
+
+def split_kernel(y_ref, in_ref, own_ref, stay_ref, go_ref):
+    zs, _, panel = stay_ref.shape
+    for y in range(2):
+
+        @pl.when(y_ref[0] == y)
+        def _(y=y):
+            for z in range(zs):
+                for ref, keep in ((stay_ref, y), (go_ref, 1 - y)):
+                    first = (2 * z + keep) * panel
+                    ref[z] = in_ref[:, first : first + panel]
+
+    go_ref[zs] = own_ref[...]
+
+
+def pack_kernel(z_ref, stay_ref, got_ref, *out_refs):
+    for k, out_ref in enumerate(out_refs):
+        out_ref[0] = stay_ref[z_ref[0] ^ k]
+        out_ref[1] = got_ref[z_ref[0] ^ k]
+
+
+def merge_kernel(block_ref, out_ref):
+    tiles, _, chans = block_ref.shape
+    for t in range(tiles):
+        out_ref[:, t * chans : (t + 1) * chans] = block_ref[t]
+
+
+def windows_of(me_ref, own_ref, own_y_ref, rest_ref, rest_y_ref, left_ref, right_ref, windows_ref):
+    me = me_ref[0]
+    rows, step, outs = left_ref.shape[1:]
+    count = left_ref.shape[0] // 2
+    width = own_ref.shape[1]
+    positions = rows * width
+    pad = (windows_ref.shape[0] - 2 * count) // 2
+    zeros = jnp.zeros(windows_ref.shape[1:], windows_ref.dtype)
+    for k in range(pad):
+        windows_ref[k] = zeros
+        windows_ref[pad + 2 * count + k] = zeros
+    for k in range(2 * count):
+        z, other = k // 2, k % 2
+        first, more = (own_y_ref, rest_y_ref) if other else (own_ref, rest_ref)
+        tile = more[z - 1] if z else first[...]
+        at = (count - 1) * other + z + 1 if z else other
+        left, right = left_ref[at], right_ref[at]
+        tile, left, right = (v.astype(jnp.float32) for v in (tile, left, right))
+        shifted = (
+            jnp.concatenate([tile[:, step:], right], axis=1),
+            tile,
+            jnp.concatenate([left, tile[:, : width - step]], axis=1),
+        )
+        for b in range(3):
+            windows_ref[pad + (me ^ k), :, b * outs : (b + 1) * outs] = (
+                shifted[b].reshape(positions, outs).astype(jnp.bfloat16)
+            )
+
+
+def back_kernel(shift, me_ref, *refs):
+    *piece_refs, weight_ref, back_ref, windows_ref = refs
+    windows_of(me_ref, *piece_refs, windows_ref)
+    for j in range(back_ref.shape[0]):
+        lhs = jnp.concatenate([windows_ref[j - shift * (a - 2)] for a in range(3)], axis=1)
+        back_ref[j] = jnp.dot(
+            lhs, weight_ref[...], preferred_element_type=jnp.float32
+        ).astype(back_ref.dtype)
+
+
+def taps_kernel(pad, scale, parts, me_ref, core_ref, *refs):
+    in_refs, piece_refs, refs = refs[:parts], refs[parts:-3], refs[-3:]
+    piece_refs, out_refs = piece_refs[:-4], piece_refs[-4:]
+    windows_ref, strip_ref, flipped_ref = refs
+    windows_of(me_ref, *piece_refs, windows_ref)
+    core, me = core_ref[0], me_ref[0]
+    tiles, positions, chans = strip_ref.shape
+    half = chans // len(out_refs)
+    outs = windows_ref.shape[2] // 3
+    for k in range(tiles):
+        strip_ref[me ^ k] = in_refs[k // 2][k % 2]
+    for j in range(tiles):
+        x = strip_ref[j]
+        for c in range(len(out_refs) // 2):
+            first = 2 * half * c
+            low, high = x[:, first : first + half], x[:, first + half : first + 2 * half]
+            mine = jnp.where(core == 0, low, high)
+            other = jnp.where(core == 0, high, low)
+            columns = slice(j * positions, (j + 1) * positions)
+            flipped_ref[first : first + half, columns] = mine.T
+            flipped_ref[first + half : first + 2 * half, columns] = other.T
+    for a in range(3):
+        move = pad * (a - 1)
+        first, last = max(0, move), min(tiles, tiles + move)
+        lhs = flipped_ref[:, first * positions : last * positions]
+        rhs = windows_ref[pad + first - move : pad + last - move].reshape(
+            (last - first) * positions, 3 * outs
+        )
+        terms = jnp.dot(lhs, rhs, preferred_element_type=jnp.float32) * scale
+        for n, out_ref in enumerate(out_refs):
+            for b in range(3):
+                out_ref[3 * a + b] = terms[n * half : (n + 1) * half, b * outs : (b + 1) * outs]
+
+
+def join_kernel(core_ref, *refs):
+    *parts, out_ref = refs
+    core = core_ref[0]
+    half = parts[0].shape[1]
+    for c in range(len(parts) // 4):
+        mine, mine_x, other, other_x = parts[4 * c : 4 * c + 4]
+        base = 2 * half * c
+        out_ref[:, pl.ds(base + core * half, half), :] = mine[...] + mine_x[...]
+        out_ref[:, pl.ds(base + (1 - core) * half, half), :] = other[...] + other_x[...]
+
+
+def vmem(n):
+    return [pl.BlockSpec(memory_space=pltpu.VMEM)] * n
+
+
+def whole(*arrays):
+    return [pl.BlockSpec(a.shape, lambda i, n=a.ndim: (0,) * n) for a in arrays]
+
+
+CHUNKS = 2
+
+
+def quick(inputs, output_gradient, weight):
+    rows, width, in_chans = inputs.shape
+    outs = output_gradient.shape[2]
+    tiles = lax.axis_size("row")
+    panel = in_chans // tiles
+    chunk = panel // CHUNKS
+    positions = rows * width
+    shift = DILATION_STEP // rows
+    me = lax.axis_index("row").astype(jnp.int32).reshape(1)
+    core = (lax.axis_index("col") % 2).astype(jnp.int32).reshape(1)
+    params = pltpu.CompilerParams(vmem_limit_bytes=VMEM_LIMIT)
+    smem = pl.BlockSpec(memory_space=pltpu.SMEM)
+
+    zs = tiles // 2
+    flat = inputs.reshape(positions, in_chans)
+    stay, go = pl.pallas_call(
+        split_kernel,
+        grid=(2,),
+        out_shape=[
+            jax.ShapeDtypeStruct((n, positions, panel), jnp.bfloat16) for n in (zs, zs + 1)
+        ],
+        in_specs=[
+            smem,
+            pl.BlockSpec((positions // 2, in_chans), lambda i: (i, 0)),
+            pl.BlockSpec((positions // 2, outs), lambda i: (i, 0)),
+        ],
+        out_specs=[
+            pl.BlockSpec((n, positions // 2, panel), lambda i: (0, i, 0)) for n in (zs, zs + 1)
+        ],
+        compiler_params=params,
+        name="split",
+    )(me % 2, flat, output_gradient.reshape(positions, outs))
+    flat_weight = weight.transpose(0, 1, 3, 2).reshape(9 * outs, panel)
+    rest = jnp.stack([swap(output_gradient, "row", k) for k in (2, 4, 6)])
+    got = swap(go, "row", 1)
+    got, flat_weight = lax.optimization_barrier((got, flat_weight))
+    pairs = pl.pallas_call(
+        pack_kernel,
+        grid=(1,),
+        out_shape=[jax.ShapeDtypeStruct((2, positions, panel), jnp.bfloat16)] * zs,
+        in_specs=[smem] + whole(stay, got),
+        out_specs=[pl.BlockSpec((2, positions, panel), lambda i: (0, 0, 0))] * zs,
+        compiler_params=params,
+        name="pack",
+    )(me // 2, stay, got)
+    rest, *pairs = lax.optimization_barrier((rest, *pairs))
+    strip = [p if k == 0 else swap(p, "row", 2 * k) for k, p in enumerate(pairs)]
+
+    rest_y = swap(rest, "row", 1)
+    own_y = got[zs].reshape(rows, width, outs)
+    stacked = jnp.concatenate([output_gradient[None], own_y[None], rest, rest_y])
+    left, right = rims(stacked, DILATION_STEP)
+
+
+    pieces = (output_gradient, own_y, rest, rest_y, left, right)
+    windows = pltpu.VMEM((tiles + 2 * shift, positions, 3 * outs), jnp.bfloat16)
+
+    back = pl.pallas_call(
+        lambda *refs: back_kernel(shift, *refs),
+        grid=(1,),
+        out_shape=jax.ShapeDtypeStruct((tiles, positions, panel), jnp.bfloat16),
+        in_specs=[smem] + whole(*pieces, flat_weight),
+        out_specs=vmem(1)[0],
+        scratch_shapes=[windows],
+        compiler_params=params,
+        name="back",
+    )(me, *pieces, flat_weight)
+
+    scale = 1.0 / math.sqrt(rows * tiles * width * lax.axis_size("col"))
+    half = jax.ShapeDtypeStruct((9, chunk // 2, outs), jnp.float32)
+    terms = pl.pallas_call(
+        lambda *refs: taps_kernel(shift, scale, zs, *refs),
+        grid=(1,),
+        out_shape=(half,) * (2 * CHUNKS),
+        in_specs=[smem, smem] + whole(*strip, *pieces),
+        out_specs=tuple(vmem(2 * CHUNKS)),
+        scratch_shapes=[
+            windows,
+            pltpu.VMEM((tiles, positions, panel), jnp.bfloat16),
+            pltpu.VMEM((panel, tiles * positions), jnp.bfloat16),
+        ],
+        compiler_params=params,
+        name="taps",
+    )(me, core, *strip, *pieces)
+
+    parts = []
+    for mine, theirs in zip(terms[::2], terms[1::2]):
+        chip = mine + swap(theirs, "col", 1)
+        across = swap(chip, "col", 2)
+        parts += [chip, across, swap(chip, "col", 1), swap(across, "col", 1)]
+
+    grad_back = lax.all_to_all(back, "row", split_axis=0, concat_axis=0, tiled=True)
+    grad_in = pl.pallas_call(
+        merge_kernel,
+        grid=(2,),
+        out_shape=jax.ShapeDtypeStruct((positions, in_chans), jnp.bfloat16),
+        in_specs=[pl.BlockSpec((tiles, positions // 2, panel), lambda i: (0, i, 0))],
+        out_specs=pl.BlockSpec((positions // 2, in_chans), lambda i: (i, 0)),
+        compiler_params=params,
+        name="merge",
+    )(grad_back)
+
+    grad_weight = pl.pallas_call(
+        join_kernel,
+        grid=(3,),
+        out_shape=jax.ShapeDtypeStruct((9, panel, outs), jnp.float32),
+        in_specs=[smem] + [pl.BlockSpec((3, chunk // 2, outs), lambda i: (i, 0, 0))] * len(parts),
+        out_specs=pl.BlockSpec((3, panel, outs), lambda i: (i, 0, 0)),
+        compiler_params=params,
+        name="join",
+    )(core, *parts)
+    return grad_in.reshape(rows, width, in_chans), grad_weight.reshape(3, 3, panel, outs)
 
 
 def extended(x, sides, width):
@@ -21,7 +272,7 @@
     return x
 
 
-def shards(inputs, output_gradient, weight):
+def general(inputs, output_gradient, weight):
     height, width, in_chans = inputs.shape
     out_chans = output_gradient.shape[2]
     step = DILATION_STEP
@@ -71,6 +322,21 @@
     return (grad_in, grad_weight)
 
 
+def shards(inputs, output_gradient, weight):
+    rows, width, in_chans = inputs.shape
+    tiles, strips = lax.axis_size("row"), lax.axis_size("col")
+    fits = (
+        tiles == 8
+        and strips == 4
+        and DILATION_STEP % rows == 0
+        and DILATION_STEP <= width
+        and width % 16 == 0
+        and in_chans % (tiles * 256) == 0
+        and output_gradient.shape[2] % 128 == 0
+    )
+    return (quick if fits else general)(inputs, output_gradient, weight)
+
+
 def solution(mesh):
     return jax.shard_map(
         shards,

time: 170 us -> 92.9 us (0.55)
  blocking collectives: 45.4 us -> 0 us
  starting transfers between devices: 9.09 us -> 29.3 us
  local copies, waits for them, and re-layouts: 21.1 us -> 2.79 us
  waiting for transfers between devices: 58.7 us -> 43.3 us
  matrix products: 14.9 us -> 0 us
  Pallas kernels: 0 us -> 14.2 us
  between operations: 14.2 us -> 0.78 us
  other arithmetic: 5.97 us -> 2.02 us
    all_to_all x1 -> x0, blocking collectives: 45.4 us -> none  [shards(): lax.all_to_all(inputs, 'row', split_axis=2, concat_axis=0, tiled=True)]
    ppermute x2 -> x18, waiting for transfers between devices: 3.9 us -> 43.3 us  [the longest x16 42.1 us: swap(): lax.ppermute(x, axis, [(i, i ^ bit) for i in range(lax.axis_size(axis))])]
    psum x1 -> x0, waiting for transfers between devices: 34.5 us -> none  [shards(): grad_weight = lax.psum(terms, 'col')]
    ppermute x2 -> x18, starting transfers between devices: 3.65 us -> 24.4 us  [the longest x16 20.1 us: swap(): lax.ppermute(x, axis, [(i, i ^ bit) for i in range(lax.axis_size(axis))])]
    all_to_all x1, waiting for transfers between devices: 20.3 us -> 0.01 us  [quick(): lax.all_to_all(back, 'row', split_axis=0, concat_axis=0, tiled=True)]
    dot_general x18 -> x0, matrix products: 14.9 us -> none  [the longest x9 10.7 us: shards(): lax.dot_general(in_rows, window, (((0,), (0,)), ((), ())), preferred_elem...]
    pallas_call x0 -> x6, Pallas kernels: none -> 14.2 us  [the longest x1 5.04 us: quick(): pl.pallas_call(lambda *refs: back_kernel(shift, *refs), grid=(1,), out_sh...]
    unnamed x12 -> x2, local copies, waits for them, and re-layouts: 12.1 us -> 1.22 us
  transfers between devices with their start and end apart: 5 -> 19, of which waited for: 3 -> 8; matrix products, arithmetic and copies ran while one was open for 10% -> 4% of each run, Pallas kernels for 0% -> 12%
where the time goes in v2:
time: 92.9 us; the launch traced here: 92.4 us
  waiting for transfers between devices  43.3 us (47%)
  starting transfers between devices  29.3 us (32%)
  Pallas kernels  14.2 us (15%)
  local copies, waits for them, and re-layouts  2.79 us (3%)
  other arithmetic  2.02 us (2%)
    ppermute x16, waiting for transfers between devices, swap(): lax.ppermute(x, axis, [(i, i ^ bit) for i in range(lax.axis_size(axis))])  42.1 us
    ppermute x16, starting transfers between devices, swap(): lax.ppermute(x, axis, [(i, i ^ bit) for i in range(lax.axis_size(axis))])  20.1 us
    pallas_call x1, Pallas kernels, quick(): pl.pallas_call(lambda *refs: back_kernel(shift, *refs), grid=(1,), out_sh...  5.04 us
    all_to_all x1, starting transfers between devices, quick(): lax.all_to_all(back, 'row', split_axis=0, concat_axis=0, tiled=True)  4.89 us
    pallas_call x1, Pallas kernels, quick(): pl.pallas_call(lambda *refs: taps_kernel(shift, scale, zs, *refs), grid=(...  4.2 us
    ppermute x1, starting transfers between devices, rims(): before = lax.ppermute(x[..., length - width:, :], 'col', up)  3.05 us
    pallas_call x1, Pallas kernels, quick(): pl.pallas_call(join_kernel, grid=(3,), out_shape=jax.ShapeDtypeStruct((9,...  1.92 us
  transfers between devices with their start and end apart: 19, of which 8 were waited for; matrix products, arithmetic and copies ran while one was open for 4% of the time, Pallas kernels for 12%

profile of v2, /device:TPU:0, one launch (start us, length us, event | category | flops | bytes accessed | tf_op | source)
XLA Modules:
  0.0 92.4 jit_solution(7814830461721585743)
XLA Ops:
  0.6 0.0 copy-start
  0.7 1.2 %copy-done = bf16[4,64,2048]{2,1,0:T(8,128)(2,1)S(1)} copy-done((bf16[4,64,2048]{2,1,0:T(8,128)(2,1)S(1)}, bf16[4,64,2048]{2,1,0:T(8,128)(2,1)}, u32[]{:S(2)}) %copy-start) | copy-done | bytes 1048600
  1.9 1.1 %split.1 = (bf16[4,256,256]{2,1,0:T(8,128)(2,1)S(1)}, bf16[5,256,256]{2,1,0:T(8,128)(2,1)S(1)}) custom-call(s32[1]{0:T(128)S(6)} %select_n.18.y_ref, bf16[256,2048]{1,0:T(8,128)(2,1)S(1)} %bitcast.18, bf16[256,256]{1,0:T(8,128)(2,1)} %bitcast.2.own_ref), custom_call_target="tpu_custom_call" | custom-call | tf_op jit(solution)/shard_map/split/pallas_call | solution.py:163
  2.9 3.0 %collective-permute-start = (bf16[5,256,256]{2,1,0:T(8,128)(2,1)S(1)}, bf16[5,256,256]{2,1,0:T(8,128)(2,1)S(1)}, u32[]{:S(2)}, u32[]{:S(2)}) collective-permute-start(bf16[5,256,256]{2,1,0:T(8,128)(2,1)S(1)} %get-tuple-element.19), channel_id=1, source_target_pairs={{0,4},{4,0},{8,12},{12,8},{16,20},{20,16},{24,28},{28,24},{1,5},{5... | collective-permute-start | bytes 1966088 | tf_op jit(solution)/shard_map/ppermute | solution.py:15
  6.0 3.6 %collective-permute-start.3 = (bf16[4,64,256]{2,1,0:T(8,128)(2,1)}, bf16[4,64,256]{2,1,0:T(8,128)(2,1)S(1)}, u32[]{:S(2)}, u32[]{:S(2)}) collective-permute-start(bf16[4,64,256]{2,1,0:T(8,128)(2,1)} %refs_6_.1), channel_id=1, source_target_pairs={{0,24},{4,28},{8,16},{12,20},{16,8},{20,12},{24,0},{28,4},{1,25},{... | collective-permute-start | bytes 393224 | tf_op jit(solution)/shard_map/ppermute | solution.py:15
  9.6 0.0 collective-permute-start.2
  9.6 0.8 collective-permute-start.1
  10.3 1.6 %copy.5 = bf16[3,3,256,256]{3,2,1,0:T(8,128)(2,1)S(1)} copy(bf16[3,3,256,256]{2,3,1,0:T(8,128)(2,1)} %bitcast.20) | data formatting | bytes 2359296 | tf_op jit(solution)/shard_map/transpose | solution.py:180
  11.9 2.5 %collective-permute-done.3 = bf16[4,64,256]{2,1,0:T(8,128)(2,1)S(1)} collective-permute-done((bf16[4,64,256]{2,1,0:T(8,128)(2,1)}, bf16[4,64,256]{2,1,0:T(8,128)(2,1)S(1)}, u32[]{:S(2)}, u32[]{:S(2)}) %collective-permute-start.3) | collective-permute-done | bytes 131104 | tf_op jit(solution)/shard_map/ppermute | solution.py:15
  14.4 6.2 %collective-permute-done.2 = bf16[4,64,256]{2,1,0:T(8,128)(2,1)} collective-permute-done((bf16[4,64,256]{2,1,0:T(8,128)(2,1)}, bf16[4,64,256]{2,1,0:T(8,128)(2,1)}, u32[]{:S(2)}, u32[]{:S(2)}) %collective-permute-start.2) | collective-permute-done | bytes 131104 | tf_op jit(solution)/shard_map/ppermute | solution.py:15
  20.7 0.0 collective-permute-done.1
  20.7 1.0 %pad_maximum_fusion.refs_3_.refs_8_ = bf16[3,4,64,256]{3,2,1,0:T(8,128)(2,1)S(1)} fusion(bf16[1,4,64,256]{3,2,1,0:T(8,128)(2,1)S(1)} %bitcast.22, bf16[1,4,64,256]{3,2,1,0:T(8,128)(2,1)} %bitcast.7, bf16[1,4,64,256]{3,2,1,0:T(8,128)(2,1)} %bitcast.6), kind=kLoop, calls=%fused_computation | loop fusion | flops 393216 | bytes 786432 | tf_op jit(solution)/shard_map/stack | solution.py:181
  21.7 0.0 collective-permute-done.got_ref
  21.7 0.9 %pack.1 = (bf16[2,256,256]{2,1,0:T(8,128)(2,1)S(1)}, bf16[2,256,256]{2,1,0:T(8,128)(2,1)}, bf16[2,256,256]{2,1,0:T(8,128)(2,1)}, bf16[2,256,256]{2,1,0:T(8,128)(2,1)}) custom-call(s32[1]{0:T(128)S(6)} %select_n.19.z_ref, bf16[4,256,256]{2,1,0:T(8,128)(2,1)S(1)} %get-tuple-element.21.stay_ref, bf16[5,256,256]{2,1,0:T(8,128)(2,1)S(1)} %collective-permute-done.got_ref), custom_call_target="tpu_custom_call" | custom-call | tf_op jit(solution)/shard_map/pack/pallas_call | solution.py:184
  22.6 0.7 collective-permute-start.4
  23.4 1.6 %collective-permute-start.7 = (bf16[2,256,256]{2,1,0:T(8,128)(2,1)}, bf16[2,256,256]{2,1,0:T(8,128)(2,1)S(1)}, u32[]{:S(2)}, u32[]{:S(2)}) collective-permute-start(bf16[2,256,256]{2,1,0:T(8,128)(2,1)} %get-tuple-element.29), channel_id=1, source_target_pairs={{0,8},{4,12},{8,0},{12,4},{16,24},{20,28},{24,16},{28,20},{1,9},{5... | collective-permute-start | bytes 786440 | tf_op jit(solution)/shard_map/ppermute | solution.py:15
  25.0 2.6 %collective-permute-start.8 = (bf16[2,256,256]{2,1,0:T(8,128)(2,1)}, bf16[2,256,256]{2,1,0:T(8,128)(2,1)S(1)}, u32[]{:S(2)}, u32[]{:S(2)}) collective-permute-start(bf16[2,256,256]{2,1,0:T(8,128)(2,1)} %get-tuple-element.30), channel_id=1, source_target_pairs={{0,16},{4,20},{8,24},{12,28},{16,0},{20,4},{24,8},{28,12},{1,17},{... | collective-permute-start | bytes 786440 | tf_op jit(solution)/shard_map/ppermute | solution.py:15
  27.6 0.2 collective-permute-start.9
  27.8 4.9 %collective-permute-done.4.refs_4_.refs_9_ = bf16[3,4,64,256]{3,2,1,0:T(8,128)(2,1)S(1)} collective-permute-done((bf16[3,4,64,256]{3,2,1,0:T(8,128)(2,1)S(1)}, bf16[3,4,64,256]{3,2,1,0:T(8,128)(2,1)S(1)}, u32[]{:S(2)}, u32[]{:S(2)}) %collective-permute-start.4) | collective-permute-done | bytes 393248 | tf_op jit(solution)/shard_map/ppermute | solution.py:15
  32.8 0.8 pad_maximum_fusion.1
  33.6 1.3 %collective-permute-start.6 = (bf16[8,4,12,256]{3,2,1,0:T(8,128)(2,1)S(1)}, bf16[8,4,12,256]{3,2,1,0:T(8,128)(2,1)S(1)}, u32[]{:S(2)}, u32[]{:S(2)}) collective-permute-start(bf16[8,4,12,256]{3,2,1,0:T(8,128)(2,1)S(1)} %get-tuple-element.36), channel_id=1, source_target_pairs={{1,0},{2,1},{3,2},{5,4},{6,5},{7,6},{9,8},{10,9},{11,10},{13,12},{... | collective-permute-start | bytes 589832 | tf_op jit(solution)/shard_map/ppermute | solution.py:23
  34.9 3.0 %collective-permute-start.5 = (bf16[8,4,12,256]{3,2,1,0:T(8,128)(2,1)S(1)}, bf16[8,4,12,256]{3,2,1,0:T(8,128)(2,1)S(1)}, u32[]{:S(2)}, u32[]{:S(2)}) collective-permute-start(bf16[8,4,12,256]{3,2,1,0:T(8,128)(2,1)S(1)} %get-tuple-element.37), channel_id=1, source_target_pairs={{0,1},{1,2},{2,3},{4,5},{5,6},{6,7},{8,9},{9,10},{10,11},{12,13},{... | collective-permute-start | bytes 589832 | tf_op jit(solution)/shard_map/ppermute | solution.py:22
  38.0 0.0 collective-permute-done.6.refs_6_.refs_11_
  38.0 1.1 %collective-permute-done.5.refs_5_.refs_10_ = bf16[8,4,12,256]{3,2,1,0:T(8,128)(2,1)S(1)} collective-permute-done((bf16[8,4,12,256]{3,2,1,0:T(8,128)(2,1)S(1)}, bf16[8,4,12,256]{3,2,1,0:T(8,128)(2,1)S(1)}, u32[]{:S(2)}, u32[]{:S(2)}) %collective-permute-start.5) | collective-permute-done | bytes 196640 | tf_op jit(solution)/shard_map/ppermute | solution.py:22
  39.1 5.0 %back.1 = bf16[8,256,256]{2,1,0:T(8,128)(2,1)} custom-call(s32[1]{0:T(128)} %bitcast.refs_0_, bf16[4,64,256]{2,1,0:T(8,128)(2,1)} %refs_6_.1, bf16[4,64,256]{2,1,0:T(8,128)(2,1)S(1)} %bitcast.16, bf16[3,4,64,256]{3,2,1,0:T(8,128)(2,1)S(1)} %pad_maximum_fusion.refs_3_.refs_8_, bf16[3,4,64,256]{3,2,1,0:T(8,128)(2,1)S(1)} %collective-permute-done.4.refs_4_.refs_9_, ...), custom_call_target="tpu_custom_call" | custom-call | tf_op jit(solution)/shard_map/back/pallas_call | solution.py:205
  44.1 4.9 %all-to-all-start = ((bf16[8,256,256]{2,1,0:T(8,128)(2,1)}), bf16[8,256,256]{2,1,0:T(8,128)(2,1)S(1)}, u32[]{:S(2)}, u32[]{:S(2)}) async-start(bf16[8,256,256]{2,1,0:T(8,128)(2,1)} %back.1), calls=%async_computation | async-start | bytes 2097152 | tf_op jit(solution)/shard_map/all_to_all | solution.py:239
  49.0 0.0 collective-permute-done.7.refs_3_
  49.0 0.0 collective-permute-done.8.refs_4_
  49.0 0.0 collective-permute-done.9.refs_5_
  49.1 4.2 %taps.1 = (f32[9,64,256]{2,1,0:T(8,128)S(1)}, f32[9,64,256]{2,1,0:T(8,128)S(1)}, f32[9,64,256]{2,1,0:T(8,128)S(1)}, f32[9,64,256]{2,1,0:T(8,128)S(1)}) custom-call(s32[1]{0:T(128)} %bitcast.refs_0_, s32[1]{0:T(128)} %bitcast.12.refs_1_.core_ref, bf16[2,256,256]{2,1,0:T(8,128)(2,1)S(1)} %get-tuple-element.28.refs_2_, ...), custom_call_target="tpu_custom_call" | custom-call | tf_op jit(solution)/shard_map/taps/pallas_call | solution.py:218
  53.3 3.0 %collective-permute-start.10 = (f32[9,64,256]{2,1,0:T(8,128)S(1)}, f32[9,64,256]{2,1,0:T(8,128)S(1)}, u32[]{:S(2)}, u32[]{:S(2)}) collective-permute-start(f32[9,64,256]{2,1,0:T(8,128)S(1)} %get-tuple-element.33), channel_id=1, source_target_pairs={{0,1},{1,0},{2,3},{3,2},{4,5},{5,4},{6,7},{7,6},{8,9},{9,8},{10,11... | collective-permute-start | bytes 1769480 | tf_op jit(solution)/shard_map/ppermute | solution.py:15
  56.3 0.1 collective-permute-start.14
  56.4 1.6 %collective-permute-done.10 = f32[9,64,256]{2,1,0:T(8,128)S(1)} collective-permute-done((f32[9,64,256]{2,1,0:T(8,128)S(1)}, f32[9,64,256]{2,1,0:T(8,128)S(1)}, u32[]{:S(2)}, u32[]{:S(2)}) %collective-permute-start.10) | collective-permute-done | bytes 589856 | tf_op jit(solution)/shard_map/ppermute | solution.py:15
  57.9 0.1 add.19.refs_0_
  58.0 3.1 %collective-permute-start.11 = (f32[9,64,256]{2,1,0:T(8,128)S(1)}, f32[9,64,256]{2,1,0:T(8,128)S(1)}, u32[]{:S(2)}, u32[]{:S(2)}) collective-permute-start(f32[9,64,256]{2,1,0:T(8,128)S(1)} %add.19.refs_0_), channel_id=1, source_target_pairs={{0,2},{1,3},{2,0},{3,1},{4,6},{5,7},{6,4},{7,5},{8,10},{9,11},{10,... | collective-permute-start | bytes 1769480 | tf_op jit(solution)/shard_map/ppermute | solution.py:15
  61.1 0.0 collective-permute-done.14
  61.1 0.1 add.20.refs_4_
  61.2 0.8 collective-permute-start.15
  62.0 0.0 collective-permute-start.12
  62.0 0.5 collective-permute-start.16
  62.5 12.8 %collective-permute-done.11.refs_1_ = f32[9,64,256]{2,1,0:T(8,128)S(1)} collective-permute-done((f32[9,64,256]{2,1,0:T(8,128)S(1)}, f32[9,64,256]{2,1,0:T(8,128)S(1)}, u32[]{:S(2)}, u32[]{:S(2)}) %collective-permute-start.11) | collective-permute-done | bytes 589856 | tf_op jit(solution)/shard_map/ppermute | solution.py:15
  75.2 0.0 collective-permute-start.13
  75.2 12.2 %collective-permute-done.15.refs_5_ = f32[9,64,256]{2,1,0:T(8,128)S(1)} collective-permute-done((f32[9,64,256]{2,1,0:T(8,128)S(1)}, f32[9,64,256]{2,1,0:T(8,128)S(1)}, u32[]{:S(2)}, u32[]{:S(2)}) %collective-permute-start.15) | collective-permute-done | bytes 589856 | tf_op jit(solution)/shard_map/ppermute | solution.py:15
  87.4 0.0 collective-permute-start.17
  87.4 0.0 collective-permute-done.12.refs_2_
  87.4 0.0 collective-permute-done.16.refs_6_
  87.4 0.0 collective-permute-done.13.refs_3_
  87.4 2.0 %collective-permute-done.17.refs_7_ = f32[9,64,256]{2,1,0:T(8,128)S(1)} collective-permute-done((f32[9,64,256]{2,1,0:T(8,128)S(1)}, f32[9,64,256]{2,1,0:T(8,128)S(1)}, u32[]{:S(2)}, u32[]{:S(2)}) %collective-permute-start.17) | collective-permute-done | bytes 589856 | tf_op jit(solution)/shard_map/ppermute | solution.py:15
  89.4 1.9 %join.1 = f32[9,256,256]{2,1,0:T(8,128)} custom-call(s32[1]{0:T(128)} %bitcast.12.refs_1_.core_ref, f32[9,64,256]{2,1,0:T(8,128)S(1)} %add.19.refs_0_, f32[9,64,256]{2,1,0:T(8,128)S(1)} %collective-permute-done.11.refs_1_, f32[9,64,256]{2,1,0:T(8,128)S(1)} %collective-permute-done.12.refs_2_, f32[9,64,256]{2,1,0:T(8,128)S(1)} %collective-permute-done.13.refs_3_, ...), custom_call_target="tpu_custom_call" | custom-call | tf_op jit(solution)/shard_map/join/pallas_call | solution.py:250
  91.3 0.0 all-to-all-done.block_ref
  91.3 1.1 %merge.1 = bf16[256,2048]{1,0:T(8,128)(2,1)} custom-call(bf16[8,256,256]{2,1,0:T(8,128)(2,1)S(1)} %all-to-all-done.block_ref), custom_call_target="tpu_custom_call" | custom-call | tf_op jit(solution)/shard_map/merge/pallas_call | solution.py:240
  (1 shorter events, 0.0 us)
Async XLA Ops:
  0.6 1.2 %copy-start = (bf16[4,64,2048]{2,1,0:T(8,128)(2,1)S(1)}, bf16[4,64,2048]{2,1,0:T(8,128)(2,1)}, u32[]{:S(2)}) copy-start(bf16[4,64,2048]{2,1,0:T(8,128)(2,1)} %param.3) | copy-start | bytes 3145732
  2.9 18.8 %collective-permute-start = (bf16[5,256,256]{2,1,0:T(8,128)(2,1)S(1)}, bf16[5,256,256]{2,1,0:T(8,128)(2,1)S(1)}, u32[]{:S(2)}, u32[]{:S(2)}) collective-permute-start(bf16[5,256,256]{2,1,0:T(8,128)(2,1)S(1)} %get-tuple-element.19), channel_id=1, source_target_pairs={{0,4},{4,0},{8,12},{12,8},{16,20},{20,16},{24,28},{28,24},{1,5},{5... | collective-permute-start | bytes 1966088 | tf_op jit(solution)/shard_map/ppermute | solution.py:15
  6.0 8.5 %collective-permute-start.3 = (bf16[4,64,256]{2,1,0:T(8,128)(2,1)}, bf16[4,64,256]{2,1,0:T(8,128)(2,1)S(1)}, u32[]{:S(2)}, u32[]{:S(2)}) collective-permute-start(bf16[4,64,256]{2,1,0:T(8,128)(2,1)} %refs_6_.1), channel_id=1, source_target_pairs={{0,24},{4,28},{8,16},{12,20},{16,8},{20,12},{24,0},{28,4},{1,25},{... | collective-permute-start | bytes 393224 | tf_op jit(solution)/shard_map/ppermute | solution.py:15
  9.6 11.1 %collective-permute-start.2 = (bf16[4,64,256]{2,1,0:T(8,128)(2,1)}, bf16[4,64,256]{2,1,0:T(8,128)(2,1)}, u32[]{:S(2)}, u32[]{:S(2)}) collective-permute-start(bf16[4,64,256]{2,1,0:T(8,128)(2,1)} %refs_6_.1), channel_id=1, source_target_pairs={{0,16},{4,20},{8,24},{12,28},{16,0},{20,4},{24,8},{28,12},{1,17},{... | collective-permute-start | bytes 393224 | tf_op jit(solution)/shard_map/ppermute | solution.py:15
  9.6 11.1 %collective-permute-start.1 = (bf16[4,64,256]{2,1,0:T(8,128)(2,1)}, bf16[4,64,256]{2,1,0:T(8,128)(2,1)}, u32[]{:S(2)}, u32[]{:S(2)}) collective-permute-start(bf16[4,64,256]{2,1,0:T(8,128)(2,1)} %refs_6_.1), channel_id=1, source_target_pairs={{0,8},{4,12},{8,0},{12,4},{16,24},{20,28},{24,16},{28,20},{1,9},{5... | collective-permute-start | bytes 393224 | tf_op jit(solution)/shard_map/ppermute | solution.py:15
  22.6 10.1 %collective-permute-start.4 = (bf16[3,4,64,256]{3,2,1,0:T(8,128)(2,1)S(1)}, bf16[3,4,64,256]{3,2,1,0:T(8,128)(2,1)S(1)}, u32[]{:S(2)}, u32[]{:S(2)}) collective-permute-start(bf16[3,4,64,256]{3,2,1,0:T(8,128)(2,1)S(1)} %pad_maximum_fusion.refs_3_.refs_8_), channel_id=1, source_target_pairs={{0,4},{4,0},{8,12},{12,8},{16,20},{20,16},{24,28},{28,24},{1,5},{5... | collective-permute-start | bytes 1179656 | tf_op jit(solution)/shard_map/ppermute | solution.py:15
  23.4 25.7 %collective-permute-start.7 = (bf16[2,256,256]{2,1,0:T(8,128)(2,1)}, bf16[2,256,256]{2,1,0:T(8,128)(2,1)S(1)}, u32[]{:S(2)}, u32[]{:S(2)}) collective-permute-start(bf16[2,256,256]{2,1,0:T(8,128)(2,1)} %get-tuple-element.29), channel_id=1, source_target_pairs={{0,8},{4,12},{8,0},{12,4},{16,24},{20,28},{24,16},{28,20},{1,9},{5... | collective-permute-start | bytes 786440 | tf_op jit(solution)/shard_map/ppermute | solution.py:15
  25.0 24.0 %collective-permute-start.8 = (bf16[2,256,256]{2,1,0:T(8,128)(2,1)}, bf16[2,256,256]{2,1,0:T(8,128)(2,1)S(1)}, u32[]{:S(2)}, u32[]{:S(2)}) collective-permute-start(bf16[2,256,256]{2,1,0:T(8,128)(2,1)} %get-tuple-element.30), channel_id=1, source_target_pairs={{0,16},{4,20},{8,24},{12,28},{16,0},{20,4},{24,8},{28,12},{1,17},{... | collective-permute-start | bytes 786440 | tf_op jit(solution)/shard_map/ppermute | solution.py:15
  27.6 21.4 %collective-permute-start.9 = (bf16[2,256,256]{2,1,0:T(8,128)(2,1)}, bf16[2,256,256]{2,1,0:T(8,128)(2,1)}, u32[]{:S(2)}, u32[]{:S(2)}) collective-permute-start(bf16[2,256,256]{2,1,0:T(8,128)(2,1)} %get-tuple-element.31), channel_id=1, source_target_pairs={{0,24},{4,28},{8,16},{12,20},{16,8},{20,12},{24,0},{28,4},{1,25},{... | collective-permute-start | bytes 786440 | tf_op jit(solution)/shard_map/ppermute | solution.py:15
  33.6 4.4 %collective-permute-start.6 = (bf16[8,4,12,256]{3,2,1,0:T(8,128)(2,1)S(1)}, bf16[8,4,12,256]{3,2,1,0:T(8,128)(2,1)S(1)}, u32[]{:S(2)}, u32[]{:S(2)}) collective-permute-start(bf16[8,4,12,256]{3,2,1,0:T(8,128)(2,1)S(1)} %get-tuple-element.36), channel_id=1, source_target_pairs={{1,0},{2,1},{3,2},{5,4},{6,5},{7,6},{9,8},{10,9},{11,10},{13,12},{... | collective-permute-start | bytes 589832 | tf_op jit(solution)/shard_map/ppermute | solution.py:23
  34.9 4.2 %collective-permute-start.5 = (bf16[8,4,12,256]{3,2,1,0:T(8,128)(2,1)S(1)}, bf16[8,4,12,256]{3,2,1,0:T(8,128)(2,1)S(1)}, u32[]{:S(2)}, u32[]{:S(2)}) collective-permute-start(bf16[8,4,12,256]{3,2,1,0:T(8,128)(2,1)S(1)} %get-tuple-element.37), channel_id=1, source_target_pairs={{0,1},{1,2},{2,3},{4,5},{5,6},{6,7},{8,9},{9,10},{10,11},{12,13},{... | collective-permute-start | bytes 589832 | tf_op jit(solution)/shard_map/ppermute | solution.py:22
  44.1 47.2 %all-to-all-start = ((bf16[8,256,256]{2,1,0:T(8,128)(2,1)}), bf16[8,256,256]{2,1,0:T(8,128)(2,1)S(1)}, u32[]{:S(2)}, u32[]{:S(2)}) async-start(bf16[8,256,256]{2,1,0:T(8,128)(2,1)} %back.1), calls=%async_computation | async-start | bytes 2097152 | tf_op jit(solution)/shard_map/all_to_all | solution.py:239
  53.3 4.7 %collective-permute-start.10 = (f32[9,64,256]{2,1,0:T(8,128)S(1)}, f32[9,64,256]{2,1,0:T(8,128)S(1)}, u32[]{:S(2)}, u32[]{:S(2)}) collective-permute-start(f32[9,64,256]{2,1,0:T(8,128)S(1)} %get-tuple-element.33), channel_id=1, source_target_pairs={{0,1},{1,0},{2,3},{3,2},{4,5},{5,4},{6,7},{7,6},{8,9},{9,8},{10,11... | collective-permute-start | bytes 1769480 | tf_op jit(solution)/shard_map/ppermute | solution.py:15
  56.3 4.8 %collective-permute-start.14 = (f32[9,64,256]{2,1,0:T(8,128)S(1)}, f32[9,64,256]{2,1,0:T(8,128)S(1)}, u32[]{:S(2)}, u32[]{:S(2)}) collective-permute-start(f32[9,64,256]{2,1,0:T(8,128)S(1)} %get-tuple-element.35), channel_id=1, source_target_pairs={{0,1},{1,0},{2,3},{3,2},{4,5},{5,4},{6,7},{7,6},{8,9},{9,8},{10,11... | collective-permute-start | bytes 1769480 | tf_op jit(solution)/shard_map/ppermute | solution.py:15
  58.0 17.2 %collective-permute-start.11 = (f32[9,64,256]{2,1,0:T(8,128)S(1)}, f32[9,64,256]{2,1,0:T(8,128)S(1)}, u32[]{:S(2)}, u32[]{:S(2)}) collective-permute-start(f32[9,64,256]{2,1,0:T(8,128)S(1)} %add.19.refs_0_), channel_id=1, source_target_pairs={{0,2},{1,3},{2,0},{3,1},{4,6},{5,7},{6,4},{7,5},{8,10},{9,11},{10,... | collective-permute-start | bytes 1769480 | tf_op jit(solution)/shard_map/ppermute | solution.py:15
  61.2 26.2 %collective-permute-start.15 = (f32[9,64,256]{2,1,0:T(8,128)S(1)}, f32[9,64,256]{2,1,0:T(8,128)S(1)}, u32[]{:S(2)}, u32[]{:S(2)}) collective-permute-start(f32[9,64,256]{2,1,0:T(8,128)S(1)} %add.20.refs_4_), channel_id=1, source_target_pairs={{0,2},{1,3},{2,0},{3,1},{4,6},{5,7},{6,4},{7,5},{8,10},{9,11},{10,... | collective-permute-start | bytes 1769480 | tf_op jit(solution)/shard_map/ppermute | solution.py:15
  62.0 25.4 %collective-permute-start.12 = (f32[9,64,256]{2,1,0:T(8,128)S(1)}, f32[9,64,256]{2,1,0:T(8,128)S(1)}, u32[]{:S(2)}, u32[]{:S(2)}) collective-permute-start(f32[9,64,256]{2,1,0:T(8,128)S(1)} %add.19.refs_0_), channel_id=1, source_target_pairs={{0,1},{1,0},{2,3},{3,2},{4,5},{5,4},{6,7},{7,6},{8,9},{9,8},{10,11... | collective-permute-start | bytes 1769480 | tf_op jit(solution)/shard_map/ppermute | solution.py:15
  62.0 25.4 %collective-permute-start.16 = (f32[9,64,256]{2,1,0:T(8,128)S(1)}, f32[9,64,256]{2,1,0:T(8,128)S(1)}, u32[]{:S(2)}, u32[]{:S(2)}) collective-permute-start(f32[9,64,256]{2,1,0:T(8,128)S(1)} %add.20.refs_4_), channel_id=1, source_target_pairs={{0,1},{1,0},{2,3},{3,2},{4,5},{5,4},{6,7},{7,6},{8,9},{9,8},{10,11... | collective-permute-start | bytes 1769480 | tf_op jit(solution)/shard_map/ppermute | solution.py:15
  75.2 12.2 %collective-permute-start.13 = (f32[9,64,256]{2,1,0:T(8,128)S(1)}, f32[9,64,256]{2,1,0:T(8,128)S(1)}, u32[]{:S(2)}, u32[]{:S(2)}) collective-permute-start(f32[9,64,256]{2,1,0:T(8,128)S(1)} %collective-permute-done.11.refs_1_), channel_id=1, source_target_pairs={{0,1},{1,0},{2,3},{3,2},{4,5},{5,4},{6,7},{7,6},{8,9},{9,8},{10,11... | collective-permute-start | bytes 1769480 | tf_op jit(solution)/shard_map/ppermute | solution.py:15
  87.4 2.0 %collective-permute-start.17 = (f32[9,64,256]{2,1,0:T(8,128)S(1)}, f32[9,64,256]{2,1,0:T(8,128)S(1)}, u32[]{:S(2)}, u32[]{:S(2)}) collective-permute-start(f32[9,64,256]{2,1,0:T(8,128)S(1)} %collective-permute-done.15.refs_5_), channel_id=1, source_target_pairs={{0,1},{1,0},{2,3},{3,2},{4,5},{5,4},{6,7},{7,6},{8,9},{9,8},{10,11... | collective-permute-start | bytes 1769480 | tf_op jit(solution)/shard_map/ppermute | solution.py:15

commit v3 on v2

--- a/solution.py
+++ b/solution.py
@@ -15,33 +15,37 @@
     return lax.ppermute(x, axis, [(i, i ^ bit) for i in range(lax.axis_size(axis))])
 
 
-def rims(x, width):
+def rims(x, width, core):
     peers, length = lax.axis_size("col"), x.shape[-2]
-    up = [(i, i + 1) for i in range(peers - 1)]
-    down = [(j, i) for i, j in up]
-    before = lax.ppermute(x[..., length - width :, :], "col", up)
-    after = lax.ppermute(x[..., :width, :], "col", down)
-    return before, after
-
-
-def split_kernel(y_ref, in_ref, own_ref, stay_ref, go_ref):
+    first, last = x[..., :width, :], x[..., length - width :, :]
+    near = swap(jnp.where(core == 0, last, first), "col", 1)
+    pairs = [(i, i + 1) for i in range(1, peers - 1, 2)]
+    beside = lax.ppermute(
+        jnp.where(core == 0, first, last), "col", pairs + [(j, i) for i, j in pairs]
+    )
+    return near, beside
+
+
+def split_kernel(me_ref, in_ref, own_ref, stay_ref, go_ref, go_far_ref):
     zs, _, panel = stay_ref.shape
-    for y in range(2):
-
-        @pl.when(y_ref[0] == y)
-        def _(y=y):
-            for z in range(zs):
-                for ref, keep in ((stay_ref, y), (go_ref, 1 - y)):
-                    first = (2 * z + keep) * panel
-                    ref[z] = in_ref[:, first : first + panel]
-
-    go_ref[zs] = own_ref[...]
-
-
-def pack_kernel(z_ref, stay_ref, got_ref, *out_refs):
+
+    def channels(owner):
+        return in_ref[:, pl.ds(pl.multiple_of(owner * panel, 128), panel)]
+
+    for k in range(zs):
+        owner = me_ref[0] ^ (2 * k)
+        stay_ref[k] = channels(owner)
+        if k < zs // 2:
+            go_ref[k] = channels(owner ^ 1)
+        else:
+            go_far_ref[k - zs // 2] = channels(owner ^ 1)
+    go_ref[zs // 2] = own_ref[...]
+
+
+def pack_kernel(first, stay_ref, got_ref, *out_refs):
     for k, out_ref in enumerate(out_refs):
-        out_ref[0] = stay_ref[z_ref[0] ^ k]
-        out_ref[1] = got_ref[z_ref[0] ^ k]
+        out_ref[0] = stay_ref[first + k]
+        out_ref[1] = got_ref[k]
 
 
 def merge_kernel(block_ref, out_ref):
@@ -50,24 +54,49 @@
         out_ref[:, t * chans : (t + 1) * chans] = block_ref[t]
 
 
-def windows_of(me_ref, own_ref, own_y_ref, rest_ref, rest_y_ref, left_ref, right_ref, windows_ref):
-    me = me_ref[0]
-    rows, step, outs = left_ref.shape[1:]
-    count = left_ref.shape[0] // 2
-    width = own_ref.shape[1]
-    positions = rows * width
-    pad = (windows_ref.shape[0] - 2 * count) // 2
+def start_all(copies):
+    for copy in copies:
+        copy.start()
+    return copies
+
+
+def wait_all(copies):
+    for copy in copies:
+        copy.wait()
+
+
+def piece_copies(piece_refs, tile_ref, near_ref, beside_ref, sem):
+    own_ref, got_ref, rest_ref, rest_y_ref, near_from, beside_from = piece_refs
+    tiles = tile_ref.shape[0]
+    copies = []
+    for k in range(tiles):
+        if k < 2:
+            source = got_ref.at[got_ref.shape[0] - 1] if k else own_ref
+        else:
+            source = (rest_y_ref if k % 2 else rest_ref).at[k // 2 - 1]
+        copies.append(pltpu.make_async_copy(source, tile_ref.at[k], sem.at[k]))
+    copies.append(pltpu.make_async_copy(near_from, near_ref, sem.at[tiles]))
+    copies.append(pltpu.make_async_copy(beside_from, beside_ref, sem.at[tiles + 1]))
+    return copies
+
+
+def windows_of(me, core, tile_ref, near_ref, beside_ref, windows_ref):
+    tiles, positions, outs = tile_ref.shape
+    rows, step = near_ref.shape[1:3]
+    width = positions // rows
+    pad = (windows_ref.shape[0] - tiles) // 2
     zeros = jnp.zeros(windows_ref.shape[1:], windows_ref.dtype)
     for k in range(pad):
         windows_ref[k] = zeros
-        windows_ref[pad + 2 * count + k] = zeros
-    for k in range(2 * count):
-        z, other = k // 2, k % 2
-        first, more = (own_y_ref, rest_y_ref) if other else (own_ref, rest_ref)
-        tile = more[z - 1] if z else first[...]
-        at = (count - 1) * other + z + 1 if z else other
-        left, right = left_ref[at], right_ref[at]
-        tile, left, right = (v.astype(jnp.float32) for v in (tile, left, right))
+        windows_ref[pad + tiles + k] = zeros
+    for k in range(tiles):
+        tile = tile_ref[k].reshape(rows, width, outs)
+        at = k if k < 2 else k // 2 + 1 + k % 2 * (tiles // 2 - 1)
+        tile, near, beside = (
+            v.astype(jnp.float32) for v in (tile, near_ref[at], beside_ref[at])
+        )
+        left = jnp.where(core == 0, beside, near)
+        right = jnp.where(core == 0, near, beside)
         shifted = (
             jnp.concatenate([tile[:, step:], right], axis=1),
             tile,
@@ -79,29 +108,41 @@
             )
 
 
-def back_kernel(shift, me_ref, *refs):
-    *piece_refs, weight_ref, back_ref, windows_ref = refs
-    windows_of(me_ref, *piece_refs, windows_ref)
-    for j in range(back_ref.shape[0]):
+def back_kernel(shift, me_ref, core_ref, *refs):
+    piece_refs, weight_ref, back_ref = refs[:6], refs[6], refs[7]
+    tile_ref, near_ref, beside_ref, windows_ref, sem = refs[8:]
+    tiles = tile_ref.shape[0]
+    copies = start_all(piece_copies(piece_refs, tile_ref, near_ref, beside_ref, sem))
+    wait_all(copies)
+    windows_of(me_ref[0], core_ref[0], tile_ref, near_ref, beside_ref, windows_ref)
+    for j in range(tiles):
         lhs = jnp.concatenate([windows_ref[j - shift * (a - 2)] for a in range(3)], axis=1)
         back_ref[j] = jnp.dot(
             lhs, weight_ref[...], preferred_element_type=jnp.float32
         ).astype(back_ref.dtype)
 
 
-def taps_kernel(pad, scale, parts, me_ref, core_ref, *refs):
-    in_refs, piece_refs, refs = refs[:parts], refs[parts:-3], refs[-3:]
-    piece_refs, out_refs = piece_refs[:-4], piece_refs[-4:]
-    windows_ref, strip_ref, flipped_ref = refs
-    windows_of(me_ref, *piece_refs, windows_ref)
-    core, me = core_ref[0], me_ref[0]
+def taps_kernel(pad, scale, count, me_ref, core_ref, *refs):
+    piece_refs, strip_from, out_refs = refs[:6], refs[6 : 6 + count], refs[6 + count : -7]
+    tile_ref, near_ref, beside_ref, windows_ref, strip_ref, flipped_ref, sem = refs[-7:]
     tiles, positions, chans = strip_ref.shape
     half = chans // len(out_refs)
-    outs = windows_ref.shape[2] // 3
-    for k in range(tiles):
-        strip_ref[me ^ k] = in_refs[k // 2][k % 2]
+    outs = tile_ref.shape[2]
+    core, me = core_ref[0], me_ref[0]
+    copies = start_all(piece_copies(piece_refs, tile_ref, near_ref, beside_ref, sem))
+    strips = start_all(
+        [
+            pltpu.make_async_copy(
+                ref, strip_ref.at[pl.ds(2 * k, 2)], sem.at[tiles + 2 + k]
+            )
+            for k, ref in enumerate(strip_from)
+        ]
+    )
+    wait_all(copies)
+    windows_of(me, core, tile_ref, near_ref, beside_ref, windows_ref)
+    wait_all(strips)
     for j in range(tiles):
-        x = strip_ref[j]
+        x = strip_ref[me ^ j]
         for c in range(len(out_refs) // 2):
             first = 2 * half * c
             low, high = x[:, first : first + half], x[:, first + half : first + 2 * half]
@@ -142,7 +183,7 @@
     return [pl.BlockSpec(a.shape, lambda i, n=a.ndim: (0,) * n) for a in arrays]
 
 
-CHUNKS = 2
+CHUNKS = 1
 
 
 def quick(inputs, output_gradient, weight):
@@ -160,76 +201,83 @@
 
     zs = tiles // 2
     flat = inputs.reshape(positions, in_chans)
-    stay, go = pl.pallas_call(
+    sizes = (zs, zs // 2 + 1, zs // 2)
+    stay, go, go_far = pl.pallas_call(
         split_kernel,
         grid=(2,),
-        out_shape=[
-            jax.ShapeDtypeStruct((n, positions, panel), jnp.bfloat16) for n in (zs, zs + 1)
-        ],
+        out_shape=[jax.ShapeDtypeStruct((n, positions, panel), jnp.bfloat16) for n in sizes],
         in_specs=[
             smem,
             pl.BlockSpec((positions // 2, in_chans), lambda i: (i, 0)),
             pl.BlockSpec((positions // 2, outs), lambda i: (i, 0)),
         ],
-        out_specs=[
-            pl.BlockSpec((n, positions // 2, panel), lambda i: (0, i, 0)) for n in (zs, zs + 1)
-        ],
+        out_specs=[pl.BlockSpec((n, positions // 2, panel), lambda i: (0, i, 0)) for n in sizes],
         compiler_params=params,
         name="split",
-    )(me % 2, flat, output_gradient.reshape(positions, outs))
+    )(me, flat, output_gradient.reshape(positions, outs))
     flat_weight = weight.transpose(0, 1, 3, 2).reshape(9 * outs, panel)
-    rest = jnp.stack([swap(output_gradient, "row", k) for k in (2, 4, 6)])
+    own = output_gradient.reshape(positions, outs)
+    rest = jnp.stack([swap(own, "row", k) for k in (2, 4, 6)])
+    got_far = swap(go_far, "row", 1)
     got = swap(go, "row", 1)
     got, flat_weight = lax.optimization_barrier((got, flat_weight))
-    pairs = pl.pallas_call(
-        pack_kernel,
-        grid=(1,),
-        out_shape=[jax.ShapeDtypeStruct((2, positions, panel), jnp.bfloat16)] * zs,
-        in_specs=[smem] + whole(stay, got),
-        out_specs=[pl.BlockSpec((2, positions, panel), lambda i: (0, 0, 0))] * zs,
-        compiler_params=params,
-        name="pack",
-    )(me // 2, stay, got)
-    rest, *pairs = lax.optimization_barrier((rest, *pairs))
+
+    def pack(first, arrived):
+        count = zs // 2
+        return pl.pallas_call(
+            lambda *refs: pack_kernel(first, *refs),
+            grid=(1,),
+            out_shape=[jax.ShapeDtypeStruct((2, positions, panel), jnp.bfloat16)] * count,
+            in_specs=whole(stay, arrived),
+            out_specs=[pl.BlockSpec((2, positions, panel), lambda i: (0, 0, 0))] * count,
+            compiler_params=params,
+            name="pack",
+        )(stay, arrived)
+
+    far_pairs = pack(zs // 2, got_far)
+    rest, *far_pairs = lax.optimization_barrier((rest, *far_pairs))
+    pairs = [*pack(0, got), *far_pairs]
     strip = [p if k == 0 else swap(p, "row", 2 * k) for k, p in enumerate(pairs)]
 
     rest_y = swap(rest, "row", 1)
-    own_y = got[zs].reshape(rows, width, outs)
-    stacked = jnp.concatenate([output_gradient[None], own_y[None], rest, rest_y])
-    left, right = rims(stacked, DILATION_STEP)
-
-
-    pieces = (output_gradient, own_y, rest, rest_y, left, right)
-    windows = pltpu.VMEM((tiles + 2 * shift, positions, 3 * outs), jnp.bfloat16)
-
+    stacked = jnp.concatenate([own[None], got[zs // 2 :], rest, rest_y])
+    near, beside = rims(stacked.reshape(tiles, rows, width, outs), DILATION_STEP, core)
+
+    pieces = (own, got, rest, rest_y, near, beside)
+    hbm = pl.BlockSpec(memory_space=pltpu.HBM)
+    buffers = [
+        pltpu.VMEM((tiles, positions, outs), jnp.bfloat16),
+        pltpu.VMEM(near.shape, jnp.bfloat16),
+        pltpu.VMEM(beside.shape, jnp.bfloat16),
+        pltpu.VMEM((tiles + 2 * shift, positions, 3 * outs), jnp.bfloat16),
+    ]
     back = pl.pallas_call(
         lambda *refs: back_kernel(shift, *refs),
-        grid=(1,),
         out_shape=jax.ShapeDtypeStruct((tiles, positions, panel), jnp.bfloat16),
-        in_specs=[smem] + whole(*pieces, flat_weight),
+        in_specs=[smem, smem] + [hbm] * 6 + vmem(1),
         out_specs=vmem(1)[0],
-        scratch_shapes=[windows],
+        scratch_shapes=buffers + [pltpu.SemaphoreType.DMA((tiles + 2,))],
         compiler_params=params,
         name="back",
-    )(me, *pieces, flat_weight)
-
+    )(me, core, *pieces, flat_weight)
+
+    back, core = lax.optimization_barrier((back, core))
     scale = 1.0 / math.sqrt(rows * tiles * width * lax.axis_size("col"))
     half = jax.ShapeDtypeStruct((9, chunk // 2, outs), jnp.float32)
     terms = pl.pallas_call(
         lambda *refs: taps_kernel(shift, scale, zs, *refs),
-        grid=(1,),
         out_shape=(half,) * (2 * CHUNKS),
-        in_specs=[smem, smem] + whole(*strip, *pieces),
+        in_specs=[smem, smem] + [hbm] * (6 + zs),
         out_specs=tuple(vmem(2 * CHUNKS)),
-        scratch_shapes=[
-            windows,
+        scratch_shapes=buffers
+        + [
             pltpu.VMEM((tiles, positions, panel), jnp.bfloat16),
             pltpu.VMEM((panel, tiles * positions), jnp.bfloat16),
+            pltpu.SemaphoreType.DMA((tiles + 2 + zs,)),
         ],
         compiler_params=params,
         name="taps",
-    )(me, core, *strip, *pieces)
-
+    )(me, core, *pieces, *strip)
     parts = []
     for mine, theirs in zip(terms[::2], terms[1::2]):
         chip = mine + swap(theirs, "col", 1)
@@ -237,6 +285,16 @@
         parts += [chip, across, swap(chip, "col", 1), swap(across, "col", 1)]
 
     grad_back = lax.all_to_all(back, "row", split_axis=0, concat_axis=0, tiled=True)
+    grad_weight = pl.pallas_call(
+        join_kernel,
+        grid=(3,),
+        out_shape=jax.ShapeDtypeStruct((9, panel, outs), jnp.float32),
+        in_specs=[smem] + [pl.BlockSpec((3, chunk // 2, outs), lambda i: (i, 0, 0))] * len(parts),
+        out_specs=pl.BlockSpec((3, panel, outs), lambda i: (i, 0, 0)),
+        compiler_params=params,
+        name="join",
+    )(core, *parts)
+    grad_back, grad_weight = lax.optimization_barrier((grad_back, grad_weight))
     grad_in = pl.pallas_call(
         merge_kernel,
         grid=(2,),
@@ -247,15 +305,6 @@
         name="merge",
     )(grad_back)
 
-    grad_weight = pl.pallas_call(
-        join_kernel,
-        grid=(3,),
-        out_shape=jax.ShapeDtypeStruct((9, panel, outs), jnp.float32),
-        in_specs=[smem] + [pl.BlockSpec((3, chunk // 2, outs), lambda i: (i, 0, 0))] * len(parts),
-        out_specs=pl.BlockSpec((3, panel, outs), lambda i: (i, 0, 0)),
-        compiler_params=params,
-        name="join",
-    )(core, *parts)
     return grad_in.reshape(rows, width, in_chans), grad_weight.reshape(3, 3, panel, outs)
 
 

time: 92.9 us -> 87.1 us (0.938)
  starting transfers between devices: 29.3 us -> 22.3 us
  waiting for transfers between devices: 43.3 us -> 45.9 us
  other arithmetic: 2.02 us -> 0.4 us
  local copies, waits for them, and re-layouts: 2.79 us -> 4.4 us
  Pallas kernels: 14.2 us -> 13 us
    ppermute x16 -> x14, starting transfers between devices: 20.1 us -> 15.8 us  [swap(): lax.ppermute(x, axis, [(i, i ^ bit) for i in range(lax.axis_size(axis))])]
    ppermute x16 -> x14, waiting for transfers between devices: 42.1 us -> 45.9 us  [swap(): lax.ppermute(x, axis, [(i, i ^ bit) for i in range(lax.axis_size(axis))])]
    ppermute x2 -> x1, starting transfers between devices: 4.34 us -> 0.68 us  [rims(): lax.ppermute(jnp.where(core == 0, first, last), 'col', pairs + [(j, i) fo...]
    unnamed x2 -> x10, local copies, waits for them, and re-layouts: 1.22 us -> 2.82 us
    ppermute x2 -> x1, waiting for transfers between devices: 1.12 us -> 0.01 us  [rims(): lax.ppermute(jnp.where(core == 0, first, last), 'col', pairs + [(j, i) fo...]
    all_to_all x1, starting transfers between devices: 4.89 us -> 5.89 us  [quick(): lax.all_to_all(back, 'row', split_axis=0, concat_axis=0, tiled=True)]
    another operation x1, other arithmetic: 1.01 us -> 0.05 us  [quick(): rest = jnp.stack([swap(own, 'row', k) for k in (2, 4, 6)])]
    pallas_call x3 -> x4, Pallas kernels: 10.2 us -> 9.78 us  [the longest x1 5.7 us: quick(): pl.pallas_call(lambda *refs: back_kernel(shift, *refs), out_shape=jax.Sha...]
  transfers between devices with their start and end apart: 19 -> 16, of which waited for: 8 -> 9; matrix products, arithmetic and copies ran while one was open for 4% -> 2% of each run, Pallas kernels for 12% -> 9%
where the time goes in v3:
time: 87.1 us; the launch traced here: 86.8 us
  waiting for transfers between devices  45.9 us (53%)
  starting transfers between devices  22.3 us (26%)
  Pallas kernels  13 us (15%)
  local copies, waits for them, and re-layouts  4.4 us (5%)
    ppermute x14, waiting for transfers between devices, swap(): lax.ppermute(x, axis, [(i, i ^ bit) for i in range(lax.axis_size(axis))])  45.9 us
    ppermute x14, starting transfers between devices, swap(): lax.ppermute(x, axis, [(i, i ^ bit) for i in range(lax.axis_size(axis))])  15.8 us
    all_to_all x1, starting transfers between devices, quick(): lax.all_to_all(back, 'row', split_axis=0, concat_axis=0, tiled=True)  5.89 us
    pallas_call x1, Pallas kernels, quick(): pl.pallas_call(lambda *refs: back_kernel(shift, *refs), out_shape=jax.Sha...  5.7 us
    pallas_call x1, Pallas kernels, quick(): pl.pallas_call(lambda *refs: taps_kernel(shift, scale, zs, *refs), out_sh...  4.01 us
    unnamed x10, local copies, waits for them, and re-layouts  2.82 us
    pallas_call x1, Pallas kernels, quick(): pl.pallas_call(join_kernel, grid=(3,), out_shape=jax.ShapeDtypeStruct((9,...  1.92 us
  transfers between devices with their start and end apart: 16, of which 9 were waited for; matrix products, arithmetic and copies ran while one was open for 2% of the time, Pallas kernels for 9%

profile of v3, /device:TPU:0, one launch (start us, length us, event | category | flops | bytes accessed | tf_op | source)
XLA Modules:
  0.0 86.8 jit_solution(291837127216766239)
XLA Ops:
  0.6 0.0 copy-start
  0.6 0.9 %copy-done = bf16[4,64,256]{2,1,0:T(8,128)(2,1)S(1)} copy-done((bf16[4,64,256]{2,1,0:T(8,128)(2,1)S(1)}, bf16[4,64,256]{2,1,0:T(8,128)(2,1)}, u32[]{:S(2)}) %copy-start) | copy-done | bytes 131096
  1.5 0.0 copy-start.2
  1.5 1.2 %copy-done.2 = bf16[4,64,2048]{2,1,0:T(8,128)(2,1)S(1)} copy-done((bf16[4,64,2048]{2,1,0:T(8,128)(2,1)S(1)}, bf16[4,64,2048]{2,1,0:T(8,128)(2,1)}, u32[]{:S(2)}) %copy-start.2) | copy-done | bytes 1048600
  2.8 0.2 split.1
  3.0 3.0 %collective-permute-start.4 = (bf16[2,256,256]{2,1,0:T(8,128)(2,1)S(1)}, bf16[2,256,256]{2,1,0:T(8,128)(2,1)S(1)}, u32[]{:S(2)}, u32[]{:S(2)}) collective-permute-start(bf16[2,256,256]{2,1,0:T(8,128)(2,1)S(1)} %get-tuple-element.23), channel_id=1, source_target_pairs={{0,4},{4,0},{8,12},{12,8},{16,20},{20,16},{24,28},{28,24},{1,5},{5... | collective-permute-start | bytes 786440 | tf_op jit(solution)/shard_map/ppermute | solution.py:15
  6.1 3.6 %collective-permute-start.3 = (bf16[256,256]{1,0:T(8,128)(2,1)S(1)}, bf16[256,256]{1,0:T(8,128)(2,1)S(1)}, u32[]{:S(2)}, u32[]{:S(2)}) collective-permute-start(bf16[256,256]{1,0:T(8,128)(2,1)S(1)} %bitcast.20), channel_id=1, source_target_pairs={{0,24},{4,28},{8,16},{12,20},{16,8},{20,12},{24,0},{28,4},{1,25},{... | collective-permute-start | bytes 393224 | tf_op jit(solution)/shard_map/ppermute | solution.py:15
  9.7 0.0 collective-permute-start.2
  9.7 0.8 collective-permute-start.1
  10.4 0.3 collective-permute-start
  10.7 3.6 %collective-permute-done.3 = bf16[256,256]{1,0:T(8,128)(2,1)S(1)} collective-permute-done((bf16[256,256]{1,0:T(8,128)(2,1)S(1)}, bf16[256,256]{1,0:T(8,128)(2,1)S(1)}, u32[]{:S(2)}, u32[]{:S(2)}) %collective-permute-start.3) | collective-permute-done | bytes 131104 | tf_op jit(solution)/shard_map/ppermute | solution.py:15
  14.3 6.1 %collective-permute-done.2 = bf16[256,256]{1,0:T(8,128)(2,1)S(1)} collective-permute-done((bf16[256,256]{1,0:T(8,128)(2,1)S(1)}, bf16[256,256]{1,0:T(8,128)(2,1)S(1)}, u32[]{:S(2)}, u32[]{:S(2)}) %collective-permute-start.2) | collective-permute-done | bytes 131104 | tf_op jit(solution)/shard_map/ppermute | solution.py:15
  20.5 0.0 collective-permute-done.1
  20.5 0.0 collective-permute-done.4.refs_1_
  20.6 0.0 copy-start.3
  20.6 0.0 copy-start.4
  20.6 0.7 copy-done.3
  21.3 0.5 collective-permute-start.5
  21.8 0.0 copy-done.4
  21.8 1.6 %copy.5 = bf16[3,3,256,256]{3,2,1,0:T(8,128)(2,1)S(1)} copy(bf16[3,3,256,256]{2,3,1,0:T(8,128)(2,1)} %bitcast.28) | data formatting | bytes 2359296 | tf_op jit(solution)/shard_map/transpose | solution.py:218
  23.4 0.0 copy-start.1
  23.4 0.2 collective-permute-start.9
  23.6 2.4 %collective-permute-start.10 = (bf16[2,256,256]{2,1,0:T(8,128)(2,1)}, bf16[2,256,256]{2,1,0:T(8,128)(2,1)S(1)}, u32[]{:S(2)}, u32[]{:S(2)}) collective-permute-start(bf16[2,256,256]{2,1,0:T(8,128)(2,1)} %copy-done.3), channel_id=1, source_target_pairs={{0,24},{4,28},{8,16},{12,20},{16,8},{20,12},{24,0},{28,4},{1,25},{... | collective-permute-start | bytes 786440 | tf_op jit(solution)/shard_map/ppermute | solution.py:15
  26.0 0.0 collective-permute-done.refs_3_.refs_1_
  26.0 1.0 %collective-permute-start.8 = (bf16[2,256,256]{2,1,0:T(8,128)(2,1)S(1)}, bf16[2,256,256]{2,1,0:T(8,128)(2,1)S(1)}, u32[]{:S(2)}, u32[]{:S(2)}) collective-permute-start(bf16[2,256,256]{2,1,0:T(8,128)(2,1)S(1)} %get-tuple-element.31), channel_id=1, source_target_pairs={{0,8},{4,12},{8,0},{12,4},{16,24},{20,28},{24,16},{28,20},{1,9},{5... | collective-permute-start | bytes 786440 | tf_op jit(solution)/shard_map/ppermute | solution.py:15
  27.1 4.3 %collective-permute-done.5.refs_5_ = bf16[3,256,256]{2,1,0:T(8,128)(2,1)S(1)} collective-permute-done((bf16[3,256,256]{2,1,0:T(8,128)(2,1)S(1)}, bf16[3,256,256]{2,1,0:T(8,128)(2,1)S(1)}, u32[]{:S(2)}, u32[]{:S(2)}) %collective-permute-start.5) | collective-permute-done | bytes 393248 | tf_op jit(solution)/shard_map/ppermute | solution.py:15
  31.4 0.0 copy-done.1
  31.4 0.2 broadcast_select_fusion
  31.6 0.1 collective-permute-start.6
  31.7 0.7 collective-permute-start.7
  32.4 0.8 collective-permute-done.6.refs_6_
  33.2 0.0 collective-permute-done.7.refs_7_
  33.2 5.7 %back.1 = bf16[8,256,256]{2,1,0:T(8,128)(2,1)} custom-call(s32[1]{0:T(128)} %bitcast.me_ref.refs_0_, s32[1]{0:T(128)} %bitcast.1.refs_1_.core_ref, bf16[256,256]{1,0:T(8,128)(2,1)S(1)} %bitcast.24, bf16[3,256,256]{2,1,0:T(8,128)(2,1)S(1)} %collective-permute-done.refs_3_.refs_1_, bf16[3,256,256]{2,1,0:T(8,128)(2,1)S(1)} %pad_maximum_fusion.refs_4_, ...), custom_call_target="tpu_custom_call" | custom-call | tf_op jit(solution)/shard_map/back/pallas_call | solution.py:254
  38.9 3.1 %collective-permute-done.9.refs_10_ = bf16[2,256,256]{2,1,0:T(8,128)(2,1)S(1)} collective-permute-done((bf16[2,256,256]{2,1,0:T(8,128)(2,1)}, bf16[2,256,256]{2,1,0:T(8,128)(2,1)S(1)}, u32[]{:S(2)}, u32[]{:S(2)}) %collective-permute-start.9) | collective-permute-done | bytes 262176 | tf_op jit(solution)/shard_map/ppermute | solution.py:15
  42.0 0.0 collective-permute-done.10.refs_11_
  42.0 1.3 %collective-permute-done.8.refs_9_ = bf16[2,256,256]{2,1,0:T(8,128)(2,1)S(1)} collective-permute-done((bf16[2,256,256]{2,1,0:T(8,128)(2,1)S(1)}, bf16[2,256,256]{2,1,0:T(8,128)(2,1)S(1)}, u32[]{:S(2)}, u32[]{:S(2)}) %collective-permute-start.8) | collective-permute-done | bytes 262176 | tf_op jit(solution)/shard_map/ppermute | solution.py:15
  43.3 4.0 %taps.1 = (f32[9,128,256]{2,1,0:T(8,128)S(1)}, f32[9,128,256]{2,1,0:T(8,128)S(1)}) custom-call(s32[1]{0:T(128)} %bitcast.me_ref.refs_0_, s32[1]{0:T(128)} %bitcast.1.refs_1_.core_ref, bf16[256,256]{1,0:T(8,128)(2,1)S(1)} %bitcast.25, bf16[3,256,256]{2,1,0:T(8,128)(2,1)S(1)} %collective-permute-done.refs_3_.refs_1_, ...), custom_call_target="tpu_custom_call" | custom-call | tf_op jit(solution)/shard_map/taps/pallas_call | solution.py:267
  47.3 2.7 %collective-permute-start.11 = (f32[9,128,256]{2,1,0:T(8,128)S(1)}, f32[9,128,256]{2,1,0:T(8,128)S(1)}, u32[]{:S(2)}, u32[]{:S(2)}) collective-permute-start(f32[9,128,256]{2,1,0:T(8,128)S(1)} %get-tuple-element.35), channel_id=1, source_target_pairs={{0,1},{1,0},{2,3},{3,2},{4,5},{5,4},{6,7},{7,6},{8,9},{9,8},{10,11... | collective-permute-start | bytes 3538952 | tf_op jit(solution)/shard_map/ppermute | solution.py:15
  50.0 2.5 %collective-permute-done.11 = f32[9,128,256]{2,1,0:T(8,128)S(1)} collective-permute-done((f32[9,128,256]{2,1,0:T(8,128)S(1)}, f32[9,128,256]{2,1,0:T(8,128)S(1)}, u32[]{:S(2)}, u32[]{:S(2)}) %collective-permute-start.11) | collective-permute-done | bytes 1179680 | tf_op jit(solution)/shard_map/ppermute | solution.py:15
  52.5 0.2 add.8.refs_0_
  52.6 1.1 %collective-permute-start.12 = (f32[9,128,256]{2,1,0:T(8,128)S(1)}, f32[9,128,256]{2,1,0:T(8,128)S(1)}, u32[]{:S(2)}, u32[]{:S(2)}) collective-permute-start(f32[9,128,256]{2,1,0:T(8,128)S(1)} %add.8.refs_0_), channel_id=1, source_target_pairs={{0,2},{1,3},{2,0},{3,1},{4,6},{5,7},{6,4},{7,5},{8,10},{9,11},{10,... | collective-permute-start | bytes 3538952 | tf_op jit(solution)/shard_map/ppermute | solution.py:15
  53.8 5.9 %all-to-all-start = ((bf16[8,256,256]{2,1,0:T(8,128)(2,1)}), bf16[8,256,256]{2,1,0:T(8,128)(2,1)S(1)}, u32[]{:S(2)}, u32[]{:S(2)}) async-start(bf16[8,256,256]{2,1,0:T(8,128)(2,1)} %back.1), calls=%async_computation | async-start | bytes 2097152 | tf_op jit(solution)/shard_map/all_to_all | solution.py:287
  59.7 0.0 collective-permute-start.13
  59.7 21.3 %collective-permute-done.12.refs_1_ = f32[9,128,256]{2,1,0:T(8,128)S(1)} collective-permute-done((f32[9,128,256]{2,1,0:T(8,128)S(1)}, f32[9,128,256]{2,1,0:T(8,128)S(1)}, u32[]{:S(2)}, u32[]{:S(2)}) %collective-permute-start.12) | collective-permute-done | bytes 1179680 | tf_op jit(solution)/shard_map/ppermute | solution.py:15
  81.0 0.0 collective-permute-start.14
  81.0 0.0 collective-permute-done.13.refs_2_
  81.0 2.8 %collective-permute-done.14.refs_3_ = f32[9,128,256]{2,1,0:T(8,128)S(1)} collective-permute-done((f32[9,128,256]{2,1,0:T(8,128)S(1)}, f32[9,128,256]{2,1,0:T(8,128)S(1)}, u32[]{:S(2)}, u32[]{:S(2)}) %collective-permute-start.14) | collective-permute-done | bytes 1179680 | tf_op jit(solution)/shard_map/ppermute | solution.py:15
  83.8 1.9 %join.1 = f32[9,256,256]{2,1,0:T(8,128)} custom-call(s32[1]{0:T(128)} %bitcast.1.refs_1_.core_ref, f32[9,128,256]{2,1,0:T(8,128)S(1)} %add.8.refs_0_, f32[9,128,256]{2,1,0:T(8,128)S(1)} %collective-permute-done.12.refs_1_, f32[9,128,256]{2,1,0:T(8,128)S(1)} %collective-permute-done.13.refs_2_, f32[9,128,256]{2,1,0:T(8,128)S(1)} %collective-permute-done.14.refs_3_), custom_call_target="tpu_custom_call" | custom-call | tf_op jit(solution)/shard_map/join/pallas_call | solution.py:288
  85.7 0.0 all-to-all-done.block_ref
  85.7 1.1 %merge.1 = bf16[256,2048]{1,0:T(8,128)(2,1)} custom-call(bf16[8,256,256]{2,1,0:T(8,128)(2,1)S(1)} %all-to-all-done.block_ref), custom_call_target="tpu_custom_call" | custom-call | tf_op jit(solution)/shard_map/merge/pallas_call | solution.py:298
  (5 shorter events, 0.2 us)
Async XLA Ops:
  0.6 0.9 %copy-start = (bf16[4,64,256]{2,1,0:T(8,128)(2,1)S(1)}, bf16[4,64,256]{2,1,0:T(8,128)(2,1)}, u32[]{:S(2)}) copy-start(bf16[4,64,256]{2,1,0:T(8,128)(2,1)} %param.4) | copy-start | bytes 393220
  1.5 1.2 %copy-start.2 = (bf16[4,64,2048]{2,1,0:T(8,128)(2,1)S(1)}, bf16[4,64,2048]{2,1,0:T(8,128)(2,1)}, u32[]{:S(2)}) copy-start(bf16[4,64,2048]{2,1,0:T(8,128)(2,1)} %param.3) | copy-start | bytes 3145732
  3.0 17.5 %collective-permute-start.4 = (bf16[2,256,256]{2,1,0:T(8,128)(2,1)S(1)}, bf16[2,256,256]{2,1,0:T(8,128)(2,1)S(1)}, u32[]{:S(2)}, u32[]{:S(2)}) collective-permute-start(bf16[2,256,256]{2,1,0:T(8,128)(2,1)S(1)} %get-tuple-element.23), channel_id=1, source_target_pairs={{0,4},{4,0},{8,12},{12,8},{16,20},{20,16},{24,28},{28,24},{1,5},{5... | collective-permute-start | bytes 786440 | tf_op jit(solution)/shard_map/ppermute | solution.py:15
  6.1 8.3 %collective-permute-start.3 = (bf16[256,256]{1,0:T(8,128)(2,1)S(1)}, bf16[256,256]{1,0:T(8,128)(2,1)S(1)}, u32[]{:S(2)}, u32[]{:S(2)}) collective-permute-start(bf16[256,256]{1,0:T(8,128)(2,1)S(1)} %bitcast.20), channel_id=1, source_target_pairs={{0,24},{4,28},{8,16},{12,20},{16,8},{20,12},{24,0},{28,4},{1,25},{... | collective-permute-start | bytes 393224 | tf_op jit(solution)/shard_map/ppermute | solution.py:15
  9.7 10.8 %collective-permute-start.2 = (bf16[256,256]{1,0:T(8,128)(2,1)S(1)}, bf16[256,256]{1,0:T(8,128)(2,1)S(1)}, u32[]{:S(2)}, u32[]{:S(2)}) collective-permute-start(bf16[256,256]{1,0:T(8,128)(2,1)S(1)} %bitcast.21), channel_id=1, source_target_pairs={{0,16},{4,20},{8,24},{12,28},{16,0},{20,4},{24,8},{28,12},{1,17},{... | collective-permute-start | bytes 393224 | tf_op jit(solution)/shard_map/ppermute | solution.py:15
  9.7 10.8 %collective-permute-start.1 = (bf16[256,256]{1,0:T(8,128)(2,1)S(1)}, bf16[256,256]{1,0:T(8,128)(2,1)S(1)}, u32[]{:S(2)}, u32[]{:S(2)}) collective-permute-start(bf16[256,256]{1,0:T(8,128)(2,1)S(1)} %bitcast.22), channel_id=1, source_target_pairs={{0,8},{4,12},{8,0},{12,4},{16,24},{20,28},{24,16},{28,20},{1,9},{5... | collective-permute-start | bytes 393224 | tf_op jit(solution)/shard_map/ppermute | solution.py:15
  10.4 15.5 %collective-permute-start = (bf16[3,256,256]{2,1,0:T(8,128)(2,1)S(1)}, bf16[3,256,256]{2,1,0:T(8,128)(2,1)S(1)}, u32[]{:S(2)}, u32[]{:S(2)}) collective-permute-start(bf16[3,256,256]{2,1,0:T(8,128)(2,1)S(1)} %get-tuple-element.20), channel_id=1, source_target_pairs={{0,4},{4,0},{8,12},{12,8},{16,20},{20,16},{24,28},{28,24},{1,5},{5... | collective-permute-start | bytes 1179656 | tf_op jit(solution)/shard_map/ppermute | solution.py:15
  20.6 0.7 copy-start.3
  20.6 1.2 %copy-start.4 = (bf16[2,256,256]{2,1,0:T(8,128)(2,1)}, bf16[2,256,256]{2,1,0:T(8,128)(2,1)S(1)}, u32[]{:S(2)}) copy-start(bf16[2,256,256]{2,1,0:T(8,128)(2,1)S(1)} %get-tuple-element.32) | copy-start | bytes 786436
  21.3 10.1 %collective-permute-start.5 = (bf16[3,256,256]{2,1,0:T(8,128)(2,1)S(1)}, bf16[3,256,256]{2,1,0:T(8,128)(2,1)S(1)}, u32[]{:S(2)}, u32[]{:S(2)}) collective-permute-start(bf16[3,256,256]{2,1,0:T(8,128)(2,1)S(1)} %pad_maximum_fusion.refs_4_), channel_id=1, source_target_pairs={{0,4},{4,0},{8,12},{12,8},{16,20},{20,16},{24,28},{28,24},{1,5},{5... | collective-permute-start | bytes 1179656 | tf_op jit(solution)/shard_map/ppermute | solution.py:15
  23.4 8.1 %copy-start.1 = (bf16[4,64,256]{2,1,0:T(8,128)(2,1)S(1)}, bf16[4,64,256]{2,1,0:T(8,128)(2,1)}, u32[]{:S(2)}) copy-start(bf16[4,64,256]{2,1,0:T(8,128)(2,1)} %param.4) | copy-start | bytes 393220
  23.4 18.7 %collective-permute-start.9 = (bf16[2,256,256]{2,1,0:T(8,128)(2,1)}, bf16[2,256,256]{2,1,0:T(8,128)(2,1)S(1)}, u32[]{:S(2)}, u32[]{:S(2)}) collective-permute-start(bf16[2,256,256]{2,1,0:T(8,128)(2,1)} %copy-done.4), channel_id=1, source_target_pairs={{0,16},{4,20},{8,24},{12,28},{16,0},{20,4},{24,8},{28,12},{1,17},{... | collective-permute-start | bytes 786440 | tf_op jit(solution)/shard_map/ppermute | solution.py:15
  23.6 18.4 %collective-permute-start.10 = (bf16[2,256,256]{2,1,0:T(8,128)(2,1)}, bf16[2,256,256]{2,1,0:T(8,128)(2,1)S(1)}, u32[]{:S(2)}, u32[]{:S(2)}) collective-permute-start(bf16[2,256,256]{2,1,0:T(8,128)(2,1)} %copy-done.3), channel_id=1, source_target_pairs={{0,24},{4,28},{8,16},{12,20},{16,8},{20,12},{24,0},{28,4},{1,25},{... | collective-permute-start | bytes 786440 | tf_op jit(solution)/shard_map/ppermute | solution.py:15
  26.0 17.3 %collective-permute-start.8 = (bf16[2,256,256]{2,1,0:T(8,128)(2,1)S(1)}, bf16[2,256,256]{2,1,0:T(8,128)(2,1)S(1)}, u32[]{:S(2)}, u32[]{:S(2)}) collective-permute-start(bf16[2,256,256]{2,1,0:T(8,128)(2,1)S(1)} %get-tuple-element.31), channel_id=1, source_target_pairs={{0,8},{4,12},{8,0},{12,4},{16,24},{20,28},{24,16},{28,20},{1,9},{5... | collective-permute-start | bytes 786440 | tf_op jit(solution)/shard_map/ppermute | solution.py:15
  31.6 1.6 %collective-permute-start.6 = (bf16[8,4,12,256]{3,2,1,0:T(8,128)(2,1)S(1)}, bf16[8,4,12,256]{3,2,1,0:T(8,128)(2,1)S(1)}, u32[]{:S(2)}, u32[]{:S(2)}) collective-permute-start(bf16[8,4,12,256]{3,2,1,0:T(8,128)(2,1)S(1)} %broadcast_select_fusion.1), channel_id=1, source_target_pairs={{0,1},{1,0},{2,3},{3,2},{4,5},{5,4},{6,7},{7,6},{8,9},{9,8},{10,11... | collective-permute-start | bytes 589832 | tf_op jit(solution)/shard_map/ppermute | solution.py:15
  31.7 1.5 %collective-permute-start.7 = (bf16[8,4,12,256]{3,2,1,0:T(8,128)(2,1)S(1)}, bf16[8,4,12,256]{3,2,1,0:T(8,128)(2,1)S(1)}, u32[]{:S(2)}, u32[]{:S(2)}) collective-permute-start(bf16[8,4,12,256]{3,2,1,0:T(8,128)(2,1)S(1)} %get-tuple-element.38), channel_id=1, source_target_pairs={{1,2},{2,1},{5,6},{6,5},{9,10},{10,9},{13,14},{14,13},{17,18},{18,... | collective-permute-start | bytes 589832 | tf_op jit(solution)/shard_map/ppermute | solution.py:23
  47.3 5.2 %collective-permute-start.11 = (f32[9,128,256]{2,1,0:T(8,128)S(1)}, f32[9,128,256]{2,1,0:T(8,128)S(1)}, u32[]{:S(2)}, u32[]{:S(2)}) collective-permute-start(f32[9,128,256]{2,1,0:T(8,128)S(1)} %get-tuple-element.35), channel_id=1, source_target_pairs={{0,1},{1,0},{2,3},{3,2},{4,5},{5,4},{6,7},{7,6},{8,9},{9,8},{10,11... | collective-permute-start | bytes 3538952 | tf_op jit(solution)/shard_map/ppermute | solution.py:15
  52.6 28.3 %collective-permute-start.12 = (f32[9,128,256]{2,1,0:T(8,128)S(1)}, f32[9,128,256]{2,1,0:T(8,128)S(1)}, u32[]{:S(2)}, u32[]{:S(2)}) collective-permute-start(f32[9,128,256]{2,1,0:T(8,128)S(1)} %add.8.refs_0_), channel_id=1, source_target_pairs={{0,2},{1,3},{2,0},{3,1},{4,6},{5,7},{6,4},{7,5},{8,10},{9,11},{10,... | collective-permute-start | bytes 3538952 | tf_op jit(solution)/shard_map/ppermute | solution.py:15
  53.8 31.9 %all-to-all-start = ((bf16[8,256,256]{2,1,0:T(8,128)(2,1)}), bf16[8,256,256]{2,1,0:T(8,128)(2,1)S(1)}, u32[]{:S(2)}, u32[]{:S(2)}) async-start(bf16[8,256,256]{2,1,0:T(8,128)(2,1)} %back.1), calls=%async_computation | async-start | bytes 2097152 | tf_op jit(solution)/shard_map/all_to_all | solution.py:287
  59.7 21.3 %collective-permute-start.13 = (f32[9,128,256]{2,1,0:T(8,128)S(1)}, f32[9,128,256]{2,1,0:T(8,128)S(1)}, u32[]{:S(2)}, u32[]{:S(2)}) collective-permute-start(f32[9,128,256]{2,1,0:T(8,128)S(1)} %add.8.refs_0_), channel_id=1, source_target_pairs={{0,1},{1,0},{2,3},{3,2},{4,5},{5,4},{6,7},{7,6},{8,9},{9,8},{10,11... | collective-permute-start | bytes 3538952 | tf_op jit(solution)/shard_map/ppermute | solution.py:15
  81.0 2.8 %collective-permute-start.14 = (f32[9,128,256]{2,1,0:T(8,128)S(1)}, f32[9,128,256]{2,1,0:T(8,128)S(1)}, u32[]{:S(2)}, u32[]{:S(2)}) collective-permute-start(f32[9,128,256]{2,1,0:T(8,128)S(1)} %collective-permute-done.12.refs_1_), channel_id=1, source_target_pairs={{0,1},{1,0},{2,3},{3,2},{4,5},{5,4},{6,7},{7,6},{8,9},{9,8},{10,11... | collective-permute-start | bytes 3538952 | tf_op jit(solution)/shard_map/ppermute | solution.py:15

commit v4 on v3

--- a/solution.py
+++ b/solution.py
@@ -108,71 +108,70 @@
             )
 
 
-def back_kernel(shift, me_ref, core_ref, *refs):
-    piece_refs, weight_ref, back_ref = refs[:6], refs[6], refs[7]
-    tile_ref, near_ref, beside_ref, windows_ref, sem = refs[8:]
-    tiles = tile_ref.shape[0]
-    copies = start_all(piece_copies(piece_refs, tile_ref, near_ref, beside_ref, sem))
-    wait_all(copies)
+def windows_kernel(me_ref, core_ref, *refs):
+    piece_refs, windows_ref = refs[:6], refs[6]
+    tile_ref, near_ref, beside_ref, sem = refs[7:]
+    wait_all(start_all(piece_copies(piece_refs, tile_ref, near_ref, beside_ref, sem)))
     windows_of(me_ref[0], core_ref[0], tile_ref, near_ref, beside_ref, windows_ref)
+
+
+def back_kernel(shift, windows_ref, weight_ref, back_ref, flat_ref):
+    tiles, depth = back_ref.shape[0], windows_ref.shape[2]
+    outs = weight_ref.shape[2]
+    for t in range(weight_ref.shape[0]):
+        flat_ref[:, t * outs : (t + 1) * outs] = weight_ref[t]
     for j in range(tiles):
-        lhs = jnp.concatenate([windows_ref[j - shift * (a - 2)] for a in range(3)], axis=1)
-        back_ref[j] = jnp.dot(
-            lhs, weight_ref[...], preferred_element_type=jnp.float32
+        taps = [a for a in range(3) if 0 <= j - shift * (a - 1) < tiles]
+        lhs = jnp.concatenate([windows_ref[j - shift * (a - 2)] for a in taps], axis=1)
+        rhs = flat_ref[:, taps[0] * depth : (taps[-1] + 1) * depth]
+        back_ref[j] = lax.dot_general(
+            lhs, rhs, (((1,), (1,)), ((), ())), preferred_element_type=jnp.float32
         ).astype(back_ref.dtype)
 
 
-def taps_kernel(pad, scale, count, me_ref, core_ref, *refs):
-    piece_refs, strip_from, out_refs = refs[:6], refs[6 : 6 + count], refs[6 + count : -7]
-    tile_ref, near_ref, beside_ref, windows_ref, strip_ref, flipped_ref, sem = refs[-7:]
-    tiles, positions, chans = strip_ref.shape
-    half = chans // len(out_refs)
-    outs = tile_ref.shape[2]
-    core, me = core_ref[0], me_ref[0]
-    copies = start_all(piece_copies(piece_refs, tile_ref, near_ref, beside_ref, sem))
-    strips = start_all(
-        [
-            pltpu.make_async_copy(
-                ref, strip_ref.at[pl.ds(2 * k, 2)], sem.at[tiles + 2 + k]
-            )
-            for k, ref in enumerate(strip_from)
-        ]
-    )
-    wait_all(copies)
-    windows_of(me, core, tile_ref, near_ref, beside_ref, windows_ref)
-    wait_all(strips)
-    for j in range(tiles):
-        x = strip_ref[me ^ j]
-        for c in range(len(out_refs) // 2):
-            first = 2 * half * c
-            low, high = x[:, first : first + half], x[:, first + half : first + 2 * half]
-            mine = jnp.where(core == 0, low, high)
-            other = jnp.where(core == 0, high, low)
-            columns = slice(j * positions, (j + 1) * positions)
-            flipped_ref[first : first + half, columns] = mine.T
-            flipped_ref[first + half : first + 2 * half, columns] = other.T
+def terms_of(pad, scale, flipped, windows_ref, out_ref):
+    positions, outs = windows_ref.shape[1], out_ref.shape[2]
+    tiles = flipped.shape[1] // positions
     for a in range(3):
         move = pad * (a - 1)
         first, last = max(0, move), min(tiles, tiles + move)
-        lhs = flipped_ref[:, first * positions : last * positions]
+        lhs = flipped[:, first * positions : last * positions]
         rhs = windows_ref[pad + first - move : pad + last - move].reshape(
             (last - first) * positions, 3 * outs
         )
         terms = jnp.dot(lhs, rhs, preferred_element_type=jnp.float32) * scale
-        for n, out_ref in enumerate(out_refs):
-            for b in range(3):
-                out_ref[3 * a + b] = terms[n * half : (n + 1) * half, b * outs : (b + 1) * outs]
-
-
-def join_kernel(core_ref, *refs):
-    *parts, out_ref = refs
-    core = core_ref[0]
-    half = parts[0].shape[1]
-    for c in range(len(parts) // 4):
-        mine, mine_x, other, other_x = parts[4 * c : 4 * c + 4]
-        base = 2 * half * c
-        out_ref[:, pl.ds(base + core * half, half), :] = mine[...] + mine_x[...]
-        out_ref[:, pl.ds(base + (1 - core) * half, half), :] = other[...] + other_x[...]
+        for b in range(3):
+            out_ref[3 * a + b] = terms[:, b * outs : (b + 1) * outs]
+
+
+def other_kernel(pad, scale, me_ref, core_ref, *refs):
+    *strip_from, windows_ref, other_ref, mine_ref, strip_ref, flipped_ref, sem = refs
+    tiles, positions, chans = strip_ref.shape
+    half = chans // 2
+    core, me = core_ref[0], me_ref[0]
+    wait_all(
+        start_all(
+            [
+                pltpu.make_async_copy(ref, strip_ref.at[pl.ds(2 * k, 2)], sem.at[k])
+                for k, ref in enumerate(strip_from)
+            ]
+        )
+    )
+    for j in range(tiles):
+        x = strip_ref[me ^ j]
+        low, high = x[:, :half], x[:, half:]
+        columns = slice(j * positions, (j + 1) * positions)
+        mine_ref[:, columns] = jnp.where(core == 0, low, high).T
+        flipped_ref[:, columns] = jnp.where(core == 0, high, low).T
+    terms_of(pad, scale, flipped_ref, windows_ref, other_ref)
+
+
+def mine_kernel(pad, scale, flipped_ref, windows_ref, mine_ref):
+    terms_of(pad, scale, flipped_ref, windows_ref, mine_ref)
+
+
+def join_kernel(half_ref, part_ref, part_x_ref, *refs):
+    refs[-1][...] = part_ref[...] + part_x_ref[...]
 
 
 def vmem(n):
@@ -181,9 +180,6 @@
 
 def whole(*arrays):
     return [pl.BlockSpec(a.shape, lambda i, n=a.ndim: (0,) * n) for a in arrays]
-
-
-CHUNKS = 1
 
 
 def quick(inputs, output_gradient, weight):
@@ -191,7 +187,6 @@
     outs = output_gradient.shape[2]
     tiles = lax.axis_size("row")
     panel = in_chans // tiles
-    chunk = panel // CHUNKS
     positions = rows * width
     shift = DILATION_STEP // rows
     me = lax.axis_index("row").astype(jnp.int32).reshape(1)
@@ -215,12 +210,10 @@
         compiler_params=params,
         name="split",
     )(me, flat, output_gradient.reshape(positions, outs))
-    flat_weight = weight.transpose(0, 1, 3, 2).reshape(9 * outs, panel)
     own = output_gradient.reshape(positions, outs)
     rest = jnp.stack([swap(own, "row", k) for k in (2, 4, 6)])
     got_far = swap(go_far, "row", 1)
     got = swap(go, "row", 1)
-    got, flat_weight = lax.optimization_barrier((got, flat_weight))
 
     def pack(first, arrived):
         count = zs // 2
@@ -245,55 +238,77 @@
 
     pieces = (own, got, rest, rest_y, near, beside)
     hbm = pl.BlockSpec(memory_space=pltpu.HBM)
-    buffers = [
-        pltpu.VMEM((tiles, positions, outs), jnp.bfloat16),
-        pltpu.VMEM(near.shape, jnp.bfloat16),
-        pltpu.VMEM(beside.shape, jnp.bfloat16),
-        pltpu.VMEM((tiles + 2 * shift, positions, 3 * outs), jnp.bfloat16),
-    ]
+    windows = pl.pallas_call(
+        windows_kernel,
+        out_shape=jax.ShapeDtypeStruct((tiles + 2 * shift, positions, 3 * outs), jnp.bfloat16),
+        in_specs=[smem, smem] + [hbm] * 6,
+        out_specs=vmem(1)[0],
+        scratch_shapes=[
+            pltpu.VMEM((tiles, positions, outs), jnp.bfloat16),
+            pltpu.VMEM(near.shape, jnp.bfloat16),
+            pltpu.VMEM(beside.shape, jnp.bfloat16),
+            pltpu.SemaphoreType.DMA((tiles + 2,)),
+        ],
+        compiler_params=params,
+        name="windows",
+    )(me, core, *pieces)
     back = pl.pallas_call(
         lambda *refs: back_kernel(shift, *refs),
         out_shape=jax.ShapeDtypeStruct((tiles, positions, panel), jnp.bfloat16),
-        in_specs=[smem, smem] + [hbm] * 6 + vmem(1),
+        in_specs=vmem(2),
         out_specs=vmem(1)[0],
-        scratch_shapes=buffers + [pltpu.SemaphoreType.DMA((tiles + 2,))],
+        scratch_shapes=[pltpu.VMEM((panel, 9 * outs), jnp.bfloat16)],
         compiler_params=params,
         name="back",
-    )(me, core, *pieces, flat_weight)
-
+    )(windows, weight.reshape(9, panel, outs))
     back, core = lax.optimization_barrier((back, core))
+
     scale = 1.0 / math.sqrt(rows * tiles * width * lax.axis_size("col"))
-    half = jax.ShapeDtypeStruct((9, chunk // 2, outs), jnp.float32)
-    terms = pl.pallas_call(
-        lambda *refs: taps_kernel(shift, scale, zs, *refs),
-        out_shape=(half,) * (2 * CHUNKS),
-        in_specs=[smem, smem] + [hbm] * (6 + zs),
-        out_specs=tuple(vmem(2 * CHUNKS)),
-        scratch_shapes=buffers
-        + [
+    half = jax.ShapeDtypeStruct((9, panel // 2, outs), jnp.float32)
+    theirs, flipped = pl.pallas_call(
+        lambda *refs: other_kernel(shift, scale, *refs),
+        out_shape=(half, jax.ShapeDtypeStruct((panel // 2, tiles * positions), jnp.bfloat16)),
+        in_specs=[smem, smem] + [hbm] * zs + vmem(1),
+        out_specs=tuple(vmem(2)),
+        scratch_shapes=[
             pltpu.VMEM((tiles, positions, panel), jnp.bfloat16),
-            pltpu.VMEM((panel, tiles * positions), jnp.bfloat16),
-            pltpu.SemaphoreType.DMA((tiles + 2 + zs,)),
+            pltpu.VMEM((panel // 2, tiles * positions), jnp.bfloat16),
+            pltpu.SemaphoreType.DMA((zs,)),
         ],
         compiler_params=params,
-        name="taps",
-    )(me, core, *pieces, *strip)
-    parts = []
-    for mine, theirs in zip(terms[::2], terms[1::2]):
-        chip = mine + swap(theirs, "col", 1)
-        across = swap(chip, "col", 2)
-        parts += [chip, across, swap(chip, "col", 1), swap(across, "col", 1)]
+        name="other_terms",
+    )(me, core, *strip, windows)
+    mine = pl.pallas_call(
+        lambda *refs: mine_kernel(shift, scale, *refs),
+        out_shape=half,
+        in_specs=vmem(2),
+        out_specs=vmem(1)[0],
+        compiler_params=params,
+        name="mine_terms",
+    )(flipped, windows)
+    chip = mine + swap(theirs, "col", 1)
+    across = swap(chip, "col", 2)
+    other = (swap(chip, "col", 1), swap(across, "col", 1))
+    grad_weight = None
+    for which, terms in ((core, (chip, across)), (1 - core, other)):
+        before = [] if grad_weight is None else [grad_weight]
+        block = (3, panel // 2, outs)
+        grad_weight = pl.pallas_call(
+            join_kernel,
+            grid_spec=pltpu.PrefetchScalarGridSpec(
+                num_scalar_prefetch=1,
+                grid=(3,),
+                in_specs=[pl.BlockSpec(block, lambda i, h: (i, 0, 0))] * 2
+                + [pl.BlockSpec(memory_space=pl.ANY)] * len(before),
+                out_specs=pl.BlockSpec(block, lambda i, h: (i, h[0], 0)),
+            ),
+            out_shape=jax.ShapeDtypeStruct((9, panel, outs), jnp.float32),
+            input_output_aliases={3: 0} if before else {},
+            compiler_params=params,
+            name="join",
+        )(which, *terms, *before)
 
     grad_back = lax.all_to_all(back, "row", split_axis=0, concat_axis=0, tiled=True)
-    grad_weight = pl.pallas_call(
-        join_kernel,
-        grid=(3,),
-        out_shape=jax.ShapeDtypeStruct((9, panel, outs), jnp.float32),
-        in_specs=[smem] + [pl.BlockSpec((3, chunk // 2, outs), lambda i: (i, 0, 0))] * len(parts),
-        out_specs=pl.BlockSpec((3, panel, outs), lambda i: (i, 0, 0)),
-        compiler_params=params,
-        name="join",
-    )(core, *parts)
     grad_back, grad_weight = lax.optimization_barrier((grad_back, grad_weight))
     grad_in = pl.pallas_call(
         merge_kernel,

time: 87.1 us -> 83 us (0.953)
  local copies, waits for them, and re-layouts: 4.4 us -> 2.15 us
  waiting for transfers between devices: 45.9 us -> 44.9 us
  Pallas kernels: 13 us -> 12.1 us
    pallas_call x1, Pallas kernels: 5.7 us -> 3 us  [quick(): pl.pallas_call(lambda *refs: back_kernel(shift, *refs), out_shape=jax.Sha...]
    pallas_call x2 -> x5, Pallas kernels: 5.92 us -> 7.67 us  [the longest x2 3.15 us: quick(): pl.pallas_call(join_kernel, grid_spec=pltpu.PrefetchScalarGridSpec(num_sc...]
    transpose x1 -> x0, local copies, waits for them, and re-layouts: 1.57 us -> none  [quick(): flat_weight = weight.transpose(0, 1, 3, 2).reshape(9 * outs, panel)]
    all_to_all x1, starting transfers between devices: 5.89 us -> 4.59 us  [quick(): lax.all_to_all(back, 'row', split_axis=0, concat_axis=0, tiled=True)]
    ppermute x14, starting transfers between devices: 15.8 us -> 16.9 us  [swap(): lax.ppermute(x, axis, [(i, i ^ bit) for i in range(lax.axis_size(axis))])]
    ppermute x14, waiting for transfers between devices: 45.9 us -> 44.9 us  [swap(): lax.ppermute(x, axis, [(i, i ^ bit) for i in range(lax.axis_size(axis))])]
    unnamed x10 -> x8, local copies, waits for them, and re-layouts: 2.82 us -> 2.14 us
  transfers between devices with their start and end apart: 16 -> 16, of which waited for: 9 -> 9; matrix products, arithmetic and copies ran while one was open for 2% -> 0% of each run, Pallas kernels for 9% -> 11%
where the time goes in v4:
time: 83 us; the launch traced here: 82.7 us
  waiting for transfers between devices  44.9 us (54%)
  starting transfers between devices  22.3 us (27%)
  Pallas kernels  12.1 us (15%)
  local copies, waits for them, and re-layouts  2.15 us (3%)
    ppermute x14, waiting for transfers between devices, swap(): lax.ppermute(x, axis, [(i, i ^ bit) for i in range(lax.axis_size(axis))])  44.9 us
    ppermute x14, starting transfers between devices, swap(): lax.ppermute(x, axis, [(i, i ^ bit) for i in range(lax.axis_size(axis))])  16.9 us
    all_to_all x1, starting transfers between devices, quick(): lax.all_to_all(back, 'row', split_axis=0, concat_axis=0, tiled=True)  4.59 us
    pallas_call x2, Pallas kernels, quick(): pl.pallas_call(join_kernel, grid_spec=pltpu.PrefetchScalarGridSpec(num_sc...  3.15 us
    pallas_call x1, Pallas kernels, quick(): pl.pallas_call(lambda *refs: back_kernel(shift, *refs), out_shape=jax.Sha...  3 us
    unnamed x8, local copies, waits for them, and re-layouts  2.14 us
    pallas_call x1, Pallas kernels, quick(): pl.pallas_call(windows_kernel, out_shape=jax.ShapeDtypeStruct((tiles + 2...  2.01 us
  transfers between devices with their start and end apart: 16, of which 9 were waited for; matrix products, arithmetic and copies ran while one was open for 0% of the time, Pallas kernels for 11%

profile of v4, /device:TPU:0, one launch (start us, length us, event | category | flops | bytes accessed | tf_op | source)
XLA Modules:
  0.0 82.7 jit_solution(1892977624385355938)
XLA Ops:
  0.6 0.0 copy-start
  0.6 0.9 %copy-done = bf16[4,64,256]{2,1,0:T(8,128)(2,1)S(1)} copy-done((bf16[4,64,256]{2,1,0:T(8,128)(2,1)S(1)}, bf16[4,64,256]{2,1,0:T(8,128)(2,1)}, u32[]{:S(2)}) %copy-start) | copy-done | bytes 131096
  1.5 0.0 copy-start.3
  1.5 1.2 %copy-done.3 = bf16[4,64,2048]{2,1,0:T(8,128)(2,1)S(1)} copy-done((bf16[4,64,2048]{2,1,0:T(8,128)(2,1)S(1)}, bf16[4,64,2048]{2,1,0:T(8,128)(2,1)}, u32[]{:S(2)}) %copy-start.3) | copy-done | bytes 1048600
  2.8 0.2 split.1
  3.0 3.0 %collective-permute-start.4 = (bf16[2,256,256]{2,1,0:T(8,128)(2,1)S(1)}, bf16[2,256,256]{2,1,0:T(8,128)(2,1)S(1)}, u32[]{:S(2)}, u32[]{:S(2)}) collective-permute-start(bf16[2,256,256]{2,1,0:T(8,128)(2,1)S(1)} %get-tuple-element.20), channel_id=1, source_target_pairs={{0,4},{4,0},{8,12},{12,8},{16,20},{20,16},{24,28},{28,24},{1,5},{5... | collective-permute-start | bytes 786440 | tf_op jit(solution)/shard_map/ppermute | solution.py:15
  6.1 3.6 %collective-permute-start.3 = (bf16[256,256]{1,0:T(8,128)(2,1)S(1)}, bf16[256,256]{1,0:T(8,128)(2,1)S(1)}, u32[]{:S(2)}, u32[]{:S(2)}) collective-permute-start(bf16[256,256]{1,0:T(8,128)(2,1)S(1)} %bitcast.18), channel_id=1, source_target_pairs={{0,24},{4,28},{8,16},{12,20},{16,8},{20,12},{24,0},{28,4},{1,25},{... | collective-permute-start | bytes 393224 | tf_op jit(solution)/shard_map/ppermute | solution.py:15
  9.7 0.0 collective-permute-start.2
  9.7 0.8 collective-permute-start.1
  10.4 0.3 collective-permute-start
  10.7 3.6 %collective-permute-done.3 = bf16[256,256]{1,0:T(8,128)(2,1)S(1)} collective-permute-done((bf16[256,256]{1,0:T(8,128)(2,1)S(1)}, bf16[256,256]{1,0:T(8,128)(2,1)S(1)}, u32[]{:S(2)}, u32[]{:S(2)}) %collective-permute-start.3) | collective-permute-done | bytes 131104 | tf_op jit(solution)/shard_map/ppermute | solution.py:15
  14.3 6.1 %collective-permute-done.2 = bf16[256,256]{1,0:T(8,128)(2,1)S(1)} collective-permute-done((bf16[256,256]{1,0:T(8,128)(2,1)S(1)}, bf16[256,256]{1,0:T(8,128)(2,1)S(1)}, u32[]{:S(2)}, u32[]{:S(2)}) %collective-permute-start.2) | collective-permute-done | bytes 131104 | tf_op jit(solution)/shard_map/ppermute | solution.py:15
  20.5 0.0 collective-permute-done.1
  20.5 0.0 copy-start.1
  20.5 0.0 collective-permute-done.4.refs_1_
  20.6 0.6 collective-permute-start.5
  21.1 0.2 collective-permute-start.9
  21.3 2.3 %collective-permute-start.10 = (bf16[2,256,256]{2,1,0:T(8,128)(2,1)S(1)}, bf16[2,256,256]{2,1,0:T(8,128)(2,1)S(1)}, u32[]{:S(2)}, u32[]{:S(2)}) collective-permute-start(bf16[2,256,256]{2,1,0:T(8,128)(2,1)S(1)} %get-tuple-element.29), channel_id=1, source_target_pairs={{0,24},{4,28},{8,16},{12,20},{16,8},{20,12},{24,0},{28,4},{1,25},{... | collective-permute-start | bytes 786440 | tf_op jit(solution)/shard_map/ppermute | solution.py:15
  23.6 0.0 collective-permute-done.refs_1_
  23.7 1.1 %collective-permute-start.8 = (bf16[2,256,256]{2,1,0:T(8,128)(2,1)S(1)}, bf16[2,256,256]{2,1,0:T(8,128)(2,1)S(1)}, u32[]{:S(2)}, u32[]{:S(2)}) collective-permute-start(bf16[2,256,256]{2,1,0:T(8,128)(2,1)S(1)} %get-tuple-element.27), channel_id=1, source_target_pairs={{0,8},{4,12},{8,0},{12,4},{16,24},{20,28},{24,16},{28,20},{1,9},{5... | collective-permute-start | bytes 786440 | tf_op jit(solution)/shard_map/ppermute | solution.py:15
  24.8 6.0 %collective-permute-done.5.refs_3_ = bf16[3,256,256]{2,1,0:T(8,128)(2,1)S(1)} collective-permute-done((bf16[3,256,256]{2,1,0:T(8,128)(2,1)S(1)}, bf16[3,256,256]{2,1,0:T(8,128)(2,1)S(1)}, u32[]{:S(2)}, u32[]{:S(2)}) %collective-permute-start.5) | collective-permute-done | bytes 393248 | tf_op jit(solution)/shard_map/ppermute | solution.py:15
  30.8 0.0 copy-done.1
  30.8 0.2 broadcast_select_fusion
  31.0 0.1 collective-permute-start.6
  31.1 0.0 copy-start.2
  31.1 0.8 collective-permute-start.7
  31.9 0.7 collective-permute-done.6.refs_4_
  32.6 0.0 collective-permute-done.7.refs_5_
  32.6 2.0 %windows.1.refs_0_.refs_6_.refs_1_ = bf16[14,256,768]{2,1,0:T(8,128)(2,1)S(1)} custom-call(s32[1]{0:T(128)} %bitcast.me_ref.refs_0_, s32[1]{0:T(128)} %bitcast.1.core_ref.refs_1_.half_ref, bf16[256,256]{1,0:T(8,128)(2,1)S(1)} %bitcast.22, bf16[3,256,256]{2,1,0:T(8,128)(2,1)S(1)} %collective-permute-done.refs_1_, ...), custom_call_target="tpu_custom_call" | custom-call | tf_op jit(solution)/shard_map/windows/pallas_call | solution.py:241
  34.6 0.0 copy-done.2
  34.6 3.0 %back.1 = bf16[8,256,256]{2,1,0:T(8,128)(2,1)} custom-call(bf16[14,256,768]{2,1,0:T(8,128)(2,1)S(1)} %windows.1.refs_0_.refs_6_.refs_1_, bf16[9,256,256]{2,1,0:T(8,128)(2,1)S(1)} %bitcast.23), custom_call_target="tpu_custom_call" | custom-call | tf_op jit(solution)/shard_map/back/pallas_call | solution.py:255
  37.6 1.9 %collective-permute-done.9.refs_4_ = bf16[2,256,256]{2,1,0:T(8,128)(2,1)S(1)} collective-permute-done((bf16[2,256,256]{2,1,0:T(8,128)(2,1)S(1)}, bf16[2,256,256]{2,1,0:T(8,128)(2,1)S(1)}, u32[]{:S(2)}, u32[]{:S(2)}) %collective-permute-start.9) | collective-permute-done | bytes 262176 | tf_op jit(solution)/shard_map/ppermute | solution.py:15
  39.5 0.0 collective-permute-done.10.refs_5_
  39.5 1.4 %collective-permute-done.8.refs_3_ = bf16[2,256,256]{2,1,0:T(8,128)(2,1)S(1)} collective-permute-done((bf16[2,256,256]{2,1,0:T(8,128)(2,1)S(1)}, bf16[2,256,256]{2,1,0:T(8,128)(2,1)S(1)}, u32[]{:S(2)}, u32[]{:S(2)}) %collective-permute-start.8) | collective-permute-done | bytes 262176 | tf_op jit(solution)/shard_map/ppermute | solution.py:15
  40.9 1.4 %other_terms.1 = (f32[9,128,256]{2,1,0:T(8,128)S(1)}, bf16[128,2048]{1,0:T(8,128)(2,1)S(1)}) custom-call(s32[1]{0:T(128)} %bitcast.me_ref.refs_0_, s32[1]{0:T(128)} %bitcast.1.core_ref.refs_1_.half_ref, bf16[2,256,256]{2,1,0:T(8,128)(2,1)S(1)} %get-tuple-element.26.refs_2_, bf16[2,256,256]{2,1,0:T(8,128)(2,1)S(1)} %collective-permute-done.8.refs_3_, ...), custom_call_target="tpu_custom_call" | custom-call | tf_op jit(solution)/shard_map/other_terms/pallas_call | solution.py:268
  42.3 3.8 %collective-permute-start.11 = (f32[9,128,256]{2,1,0:T(8,128)S(1)}, f32[9,128,256]{2,1,0:T(8,128)S(1)}, u32[]{:S(2)}, u32[]{:S(2)}) collective-permute-start(f32[9,128,256]{2,1,0:T(8,128)S(1)} %get-tuple-element.31), channel_id=1, source_target_pairs={{0,1},{1,0},{2,3},{3,2},{4,5},{5,4},{6,7},{7,6},{8,9},{9,8},{10,11... | collective-permute-start | bytes 3538952 | tf_op jit(solution)/shard_map/ppermute | solution.py:15
  46.2 1.1 %mine_terms.1 = f32[9,128,256]{2,1,0:T(8,128)S(1)} custom-call(bf16[128,2048]{1,0:T(8,128)(2,1)S(1)} %get-tuple-element.30.refs_0_, bf16[14,256,768]{2,1,0:T(8,128)(2,1)S(1)} %windows.1.refs_0_.refs_6_.refs_1_), custom_call_target="tpu_custom_call" | custom-call | tf_op jit(solution)/shard_map/mine_terms/pallas_call | solution.py:281
  47.3 1.4 %collective-permute-done.11 = f32[9,128,256]{2,1,0:T(8,128)S(1)} collective-permute-done((f32[9,128,256]{2,1,0:T(8,128)S(1)}, f32[9,128,256]{2,1,0:T(8,128)S(1)}, u32[]{:S(2)}, u32[]{:S(2)}) %collective-permute-start.11) | collective-permute-done | bytes 1179680 | tf_op jit(solution)/shard_map/ppermute | solution.py:15
  48.6 0.2 add.8.part_ref
  48.9 1.2 %collective-permute-start.13 = (f32[9,128,256]{2,1,0:T(8,128)S(1)}, f32[9,128,256]{2,1,0:T(8,128)S(1)}, u32[]{:S(2)}, u32[]{:S(2)}) collective-permute-start(f32[9,128,256]{2,1,0:T(8,128)S(1)} %add.8.part_ref), channel_id=1, source_target_pairs={{0,2},{1,3},{2,0},{3,1},{4,6},{5,7},{6,4},{7,5},{8,10},{9,11},{10,... | collective-permute-start | bytes 3538952 | tf_op jit(solution)/shard_map/ppermute | solution.py:15
  50.0 4.6 %all-to-all-start = ((bf16[8,256,256]{2,1,0:T(8,128)(2,1)}), bf16[8,256,256]{2,1,0:T(8,128)(2,1)S(1)}, u32[]{:S(2)}, u32[]{:S(2)}) async-start(bf16[8,256,256]{2,1,0:T(8,128)(2,1)} %back.1), calls=%async_computation | async-start | bytes 2097152 | tf_op jit(solution)/shard_map/all_to_all | solution.py:311
  54.6 0.0 collective-permute-start.12
  54.6 22.6 %collective-permute-done.13.part_x_ref = f32[9,128,256]{2,1,0:T(8,128)S(1)} collective-permute-done((f32[9,128,256]{2,1,0:T(8,128)S(1)}, f32[9,128,256]{2,1,0:T(8,128)S(1)}, u32[]{:S(2)}, u32[]{:S(2)}) %collective-permute-start.13) | collective-permute-done | bytes 1179680 | tf_op jit(solution)/shard_map/ppermute | solution.py:15
  77.2 0.0 collective-permute-start.14
  77.2 1.6 %join.2.refs_0_ = f32[9,256,256]{2,1,0:T(8,128)} custom-call(s32[1]{0:T(128)} %bitcast.1.core_ref.refs_1_.half_ref, f32[9,128,256]{2,1,0:T(8,128)S(1)} %add.8.part_ref, f32[9,128,256]{2,1,0:T(8,128)S(1)} %collective-permute-done.13.part_x_ref), custom_call_target="tpu_custom_call" | custom-call | tf_op jit(solution)/shard_map/join/pallas_call | solution.py:296
  78.8 0.0 collective-permute-done.12.part_ref
  78.8 1.3 %collective-permute-done.14.part_x_ref = f32[9,128,256]{2,1,0:T(8,128)S(1)} collective-permute-done((f32[9,128,256]{2,1,0:T(8,128)S(1)}, f32[9,128,256]{2,1,0:T(8,128)S(1)}, u32[]{:S(2)}, u32[]{:S(2)}) %collective-permute-start.14) | collective-permute-done | bytes 1179680 | tf_op jit(solution)/shard_map/ppermute | solution.py:15
  80.0 1.6 %join.3 = f32[9,256,256]{2,1,0:T(8,128)} custom-call(s32[1]{0:T(128)S(6)} %sub.3.half_ref, f32[9,128,256]{2,1,0:T(8,128)S(1)} %collective-permute-done.12.part_ref, f32[9,128,256]{2,1,0:T(8,128)S(1)} %collective-permute-done.14.part_x_ref, f32[9,256,256]{2,1,0:T(8,128)} %join.2.refs_0_), custom_call_target="tpu_custom_call", output_to_operand_aliasing={{}: (3, {})} | custom-call | tf_op jit(solution)/shard_map/join/pallas_call | solution.py:296
  81.6 0.0 all-to-all-done.block_ref
  81.6 1.1 %merge.1 = bf16[256,2048]{1,0:T(8,128)(2,1)} custom-call(bf16[8,256,256]{2,1,0:T(8,128)(2,1)S(1)} %all-to-all-done.block_ref), custom_call_target="tpu_custom_call" | custom-call | tf_op jit(solution)/shard_map/merge/pallas_call | solution.py:313
  (5 shorter events, 0.2 us)
Async XLA Ops:
  0.6 0.9 %copy-start = (bf16[4,64,256]{2,1,0:T(8,128)(2,1)S(1)}, bf16[4,64,256]{2,1,0:T(8,128)(2,1)}, u32[]{:S(2)}) copy-start(bf16[4,64,256]{2,1,0:T(8,128)(2,1)} %param.4) | copy-start | bytes 393220
  1.5 1.2 %copy-start.3 = (bf16[4,64,2048]{2,1,0:T(8,128)(2,1)S(1)}, bf16[4,64,2048]{2,1,0:T(8,128)(2,1)}, u32[]{:S(2)}) copy-start(bf16[4,64,2048]{2,1,0:T(8,128)(2,1)} %param.3) | copy-start | bytes 3145732
  3.0 17.5 %collective-permute-start.4 = (bf16[2,256,256]{2,1,0:T(8,128)(2,1)S(1)}, bf16[2,256,256]{2,1,0:T(8,128)(2,1)S(1)}, u32[]{:S(2)}, u32[]{:S(2)}) collective-permute-start(bf16[2,256,256]{2,1,0:T(8,128)(2,1)S(1)} %get-tuple-element.20), channel_id=1, source_target_pairs={{0,4},{4,0},{8,12},{12,8},{16,20},{20,16},{24,28},{28,24},{1,5},{5... | collective-permute-start | bytes 786440 | tf_op jit(solution)/shard_map/ppermute | solution.py:15
  6.1 8.3 %collective-permute-start.3 = (bf16[256,256]{1,0:T(8,128)(2,1)S(1)}, bf16[256,256]{1,0:T(8,128)(2,1)S(1)}, u32[]{:S(2)}, u32[]{:S(2)}) collective-permute-start(bf16[256,256]{1,0:T(8,128)(2,1)S(1)} %bitcast.18), channel_id=1, source_target_pairs={{0,24},{4,28},{8,16},{12,20},{16,8},{20,12},{24,0},{28,4},{1,25},{... | collective-permute-start | bytes 393224 | tf_op jit(solution)/shard_map/ppermute | solution.py:15
  9.7 10.8 %collective-permute-start.2 = (bf16[256,256]{1,0:T(8,128)(2,1)S(1)}, bf16[256,256]{1,0:T(8,128)(2,1)S(1)}, u32[]{:S(2)}, u32[]{:S(2)}) collective-permute-start(bf16[256,256]{1,0:T(8,128)(2,1)S(1)} %bitcast.19), channel_id=1, source_target_pairs={{0,16},{4,20},{8,24},{12,28},{16,0},{20,4},{24,8},{28,12},{1,17},{... | collective-permute-start | bytes 393224 | tf_op jit(solution)/shard_map/ppermute | solution.py:15
  9.7 10.8 %collective-permute-start.1 = (bf16[256,256]{1,0:T(8,128)(2,1)S(1)}, bf16[256,256]{1,0:T(8,128)(2,1)S(1)}, u32[]{:S(2)}, u32[]{:S(2)}) collective-permute-start(bf16[256,256]{1,0:T(8,128)(2,1)S(1)} %bitcast.20), channel_id=1, source_target_pairs={{0,8},{4,12},{8,0},{12,4},{16,24},{20,28},{24,16},{28,20},{1,9},{5... | collective-permute-start | bytes 393224 | tf_op jit(solution)/shard_map/ppermute | solution.py:15
  10.4 13.2 %collective-permute-start = (bf16[3,256,256]{2,1,0:T(8,128)(2,1)S(1)}, bf16[3,256,256]{2,1,0:T(8,128)(2,1)S(1)}, u32[]{:S(2)}, u32[]{:S(2)}) collective-permute-start(bf16[3,256,256]{2,1,0:T(8,128)(2,1)S(1)} %get-tuple-element.18), channel_id=1, source_target_pairs={{0,4},{4,0},{8,12},{12,8},{16,20},{20,16},{24,28},{28,24},{1,5},{5... | collective-permute-start | bytes 1179656 | tf_op jit(solution)/shard_map/ppermute | solution.py:15
  20.5 10.3 %copy-start.1 = (bf16[4,64,256]{2,1,0:T(8,128)(2,1)S(1)}, bf16[4,64,256]{2,1,0:T(8,128)(2,1)}, u32[]{:S(2)}) copy-start(bf16[4,64,256]{2,1,0:T(8,128)(2,1)} %param.4) | copy-start | bytes 393220
  20.6 10.2 %collective-permute-start.5 = (bf16[3,256,256]{2,1,0:T(8,128)(2,1)S(1)}, bf16[3,256,256]{2,1,0:T(8,128)(2,1)S(1)}, u32[]{:S(2)}, u32[]{:S(2)}) collective-permute-start(bf16[3,256,256]{2,1,0:T(8,128)(2,1)S(1)} %pad_maximum_fusion.refs_2_), channel_id=1, source_target_pairs={{0,4},{4,0},{8,12},{12,8},{16,20},{20,16},{24,28},{28,24},{1,5},{5... | collective-permute-start | bytes 1179656 | tf_op jit(solution)/shard_map/ppermute | solution.py:15
  21.1 18.4 %collective-permute-start.9 = (bf16[2,256,256]{2,1,0:T(8,128)(2,1)S(1)}, bf16[2,256,256]{2,1,0:T(8,128)(2,1)S(1)}, u32[]{:S(2)}, u32[]{:S(2)}) collective-permute-start(bf16[2,256,256]{2,1,0:T(8,128)(2,1)S(1)} %get-tuple-element.28), channel_id=1, source_target_pairs={{0,16},{4,20},{8,24},{12,28},{16,0},{20,4},{24,8},{28,12},{1,17},{... | collective-permute-start | bytes 786440 | tf_op jit(solution)/shard_map/ppermute | solution.py:15
  21.3 18.2 %collective-permute-start.10 = (bf16[2,256,256]{2,1,0:T(8,128)(2,1)S(1)}, bf16[2,256,256]{2,1,0:T(8,128)(2,1)S(1)}, u32[]{:S(2)}, u32[]{:S(2)}) collective-permute-start(bf16[2,256,256]{2,1,0:T(8,128)(2,1)S(1)} %get-tuple-element.29), channel_id=1, source_target_pairs={{0,24},{4,28},{8,16},{12,20},{16,8},{20,12},{24,0},{28,4},{1,25},{... | collective-permute-start | bytes 786440 | tf_op jit(solution)/shard_map/ppermute | solution.py:15
  23.7 17.2 %collective-permute-start.8 = (bf16[2,256,256]{2,1,0:T(8,128)(2,1)S(1)}, bf16[2,256,256]{2,1,0:T(8,128)(2,1)S(1)}, u32[]{:S(2)}, u32[]{:S(2)}) collective-permute-start(bf16[2,256,256]{2,1,0:T(8,128)(2,1)S(1)} %get-tuple-element.27), channel_id=1, source_target_pairs={{0,8},{4,12},{8,0},{12,4},{16,24},{20,28},{24,16},{28,20},{1,9},{5... | collective-permute-start | bytes 786440 | tf_op jit(solution)/shard_map/ppermute | solution.py:15
  31.0 1.6 %collective-permute-start.6 = (bf16[8,4,12,256]{3,2,1,0:T(8,128)(2,1)S(1)}, bf16[8,4,12,256]{3,2,1,0:T(8,128)(2,1)S(1)}, u32[]{:S(2)}, u32[]{:S(2)}) collective-permute-start(bf16[8,4,12,256]{3,2,1,0:T(8,128)(2,1)S(1)} %broadcast_select_fusion.1), channel_id=1, source_target_pairs={{0,1},{1,0},{2,3},{3,2},{4,5},{5,4},{6,7},{7,6},{8,9},{9,8},{10,11... | collective-permute-start | bytes 589832 | tf_op jit(solution)/shard_map/ppermute | solution.py:15
  31.1 3.5 %copy-start.2 = (bf16[3,3,256,256]{3,2,1,0:T(8,128)(2,1)S(1)}, bf16[3,3,256,256]{3,2,1,0:T(8,128)(2,1)}, u32[]{:S(2)}) copy-start(bf16[3,3,256,256]{3,2,1,0:T(8,128)(2,1)} %param.5) | copy-start | bytes 3538948
  31.1 1.5 %collective-permute-start.7 = (bf16[8,4,12,256]{3,2,1,0:T(8,128)(2,1)S(1)}, bf16[8,4,12,256]{3,2,1,0:T(8,128)(2,1)S(1)}, u32[]{:S(2)}, u32[]{:S(2)}) collective-permute-start(bf16[8,4,12,256]{3,2,1,0:T(8,128)(2,1)S(1)} %get-tuple-element.34), channel_id=1, source_target_pairs={{1,2},{2,1},{5,6},{6,5},{9,10},{10,9},{13,14},{14,13},{17,18},{18,... | collective-permute-start | bytes 589832 | tf_op jit(solution)/shard_map/ppermute | solution.py:23
  42.3 6.3 %collective-permute-start.11 = (f32[9,128,256]{2,1,0:T(8,128)S(1)}, f32[9,128,256]{2,1,0:T(8,128)S(1)}, u32[]{:S(2)}, u32[]{:S(2)}) collective-permute-start(f32[9,128,256]{2,1,0:T(8,128)S(1)} %get-tuple-element.31), channel_id=1, source_target_pairs={{0,1},{1,0},{2,3},{3,2},{4,5},{5,4},{6,7},{7,6},{8,9},{9,8},{10,11... | collective-permute-start | bytes 3538952 | tf_op jit(solution)/shard_map/ppermute | solution.py:15
  48.9 28.3 %collective-permute-start.13 = (f32[9,128,256]{2,1,0:T(8,128)S(1)}, f32[9,128,256]{2,1,0:T(8,128)S(1)}, u32[]{:S(2)}, u32[]{:S(2)}) collective-permute-start(f32[9,128,256]{2,1,0:T(8,128)S(1)} %add.8.part_ref), channel_id=1, source_target_pairs={{0,2},{1,3},{2,0},{3,1},{4,6},{5,7},{6,4},{7,5},{8,10},{9,11},{10,... | collective-permute-start | bytes 3538952 | tf_op jit(solution)/shard_map/ppermute | solution.py:15
  50.0 31.6 %all-to-all-start = ((bf16[8,256,256]{2,1,0:T(8,128)(2,1)}), bf16[8,256,256]{2,1,0:T(8,128)(2,1)S(1)}, u32[]{:S(2)}, u32[]{:S(2)}) async-start(bf16[8,256,256]{2,1,0:T(8,128)(2,1)} %back.1), calls=%async_computation | async-start | bytes 2097152 | tf_op jit(solution)/shard_map/all_to_all | solution.py:311
  54.6 24.1 %collective-permute-start.12 = (f32[9,128,256]{2,1,0:T(8,128)S(1)}, f32[9,128,256]{2,1,0:T(8,128)S(1)}, u32[]{:S(2)}, u32[]{:S(2)}) collective-permute-start(f32[9,128,256]{2,1,0:T(8,128)S(1)} %add.8.part_ref), channel_id=1, source_target_pairs={{0,1},{1,0},{2,3},{3,2},{4,5},{5,4},{6,7},{7,6},{8,9},{9,8},{10,11... | collective-permute-start | bytes 3538952 | tf_op jit(solution)/shard_map/ppermute | solution.py:15
  77.2 2.8 %collective-permute-start.14 = (f32[9,128,256]{2,1,0:T(8,128)S(1)}, f32[9,128,256]{2,1,0:T(8,128)S(1)}, u32[]{:S(2)}, u32[]{:S(2)}) collective-permute-start(f32[9,128,256]{2,1,0:T(8,128)S(1)} %collective-permute-done.13.part_x_ref), channel_id=1, source_target_pairs={{0,1},{1,0},{2,3},{3,2},{4,5},{5,4},{6,7},{7,6},{8,9},{9,8},{10,11... | collective-permute-start | bytes 3538952 | tf_op jit(solution)/shard_map/ppermute | solution.py:15

commit v5 on v4

--- a/solution.py
+++ b/solution.py
@@ -211,7 +211,6 @@
         name="split",
     )(me, flat, output_gradient.reshape(positions, outs))
     own = output_gradient.reshape(positions, outs)
-    rest = jnp.stack([swap(own, "row", k) for k in (2, 4, 6)])
     got_far = swap(go_far, "row", 1)
     got = swap(go, "row", 1)
 
@@ -228,7 +227,9 @@
         )(stay, arrived)
 
     far_pairs = pack(zs // 2, got_far)
-    rest, *far_pairs = lax.optimization_barrier((rest, *far_pairs))
+    far = swap(own, "row", 4)
+    far, *far_pairs = lax.optimization_barrier((far, *far_pairs))
+    rest = jnp.stack([swap(own, "row", 2), far, swap(far, "row", 2)])
     pairs = [*pack(0, got), *far_pairs]
     strip = [p if k == 0 else swap(p, "row", 2 * k) for k, p in enumerate(pairs)]
 
@@ -252,17 +253,6 @@
         compiler_params=params,
         name="windows",
     )(me, core, *pieces)
-    back = pl.pallas_call(
-        lambda *refs: back_kernel(shift, *refs),
-        out_shape=jax.ShapeDtypeStruct((tiles, positions, panel), jnp.bfloat16),
-        in_specs=vmem(2),
-        out_specs=vmem(1)[0],
-        scratch_shapes=[pltpu.VMEM((panel, 9 * outs), jnp.bfloat16)],
-        compiler_params=params,
-        name="back",
-    )(windows, weight.reshape(9, panel, outs))
-    back, core = lax.optimization_barrier((back, core))
-
     scale = 1.0 / math.sqrt(rows * tiles * width * lax.axis_size("col"))
     half = jax.ShapeDtypeStruct((9, panel // 2, outs), jnp.float32)
     theirs, flipped = pl.pallas_call(
@@ -278,6 +268,16 @@
         compiler_params=params,
         name="other_terms",
     )(me, core, *strip, windows)
+    weight, theirs = lax.optimization_barrier((weight, theirs))
+    back = pl.pallas_call(
+        lambda *refs: back_kernel(shift, *refs),
+        out_shape=jax.ShapeDtypeStruct((tiles, positions, panel), jnp.bfloat16),
+        in_specs=vmem(2),
+        out_specs=vmem(1)[0],
+        scratch_shapes=[pltpu.VMEM((panel, 9 * outs), jnp.bfloat16)],
+        compiler_params=params,
+        name="back",
+    )(windows, weight.reshape(9, panel, outs))
     mine = pl.pallas_call(
         lambda *refs: mine_kernel(shift, scale, *refs),
         out_shape=half,
@@ -287,6 +287,7 @@
         name="mine_terms",
     )(flipped, windows)
     chip = mine + swap(theirs, "col", 1)
+    chip, back = lax.optimization_barrier((chip, back))
     across = swap(chip, "col", 2)
     other = (swap(chip, "col", 1), swap(across, "col", 1))
     grad_weight = None

time: 83 us -> 81.1 us (0.977)
  waiting for transfers between devices: 44.9 us -> 37.3 us
  starting transfers between devices: 22.3 us -> 27 us
    ppermute x14, waiting for transfers between devices: 44.9 us -> 36.6 us  [swap(): lax.ppermute(x, axis, [(i, i ^ bit) for i in range(lax.axis_size(axis))])]
    ppermute x14, starting transfers between devices: 16.9 us -> 20.8 us  [swap(): lax.ppermute(x, axis, [(i, i ^ bit) for i in range(lax.axis_size(axis))])]
    all_to_all x1, starting transfers between devices: 4.59 us -> 5.59 us  [quick(): lax.all_to_all(back, 'row', split_axis=0, concat_axis=0, tiled=True)]
    pallas_call x1, Pallas kernels: 0.24 us -> 1.1 us  [quick(): pl.pallas_call(split_kernel, grid=(2,), out_shape=[jax.ShapeDtypeStruct((...]
    unnamed x8 -> x9, local copies, waits for them, and re-layouts: 2.14 us -> 2.33 us
  transfers between devices with their start and end apart: 16 -> 16, of which waited for: 9 -> 8; matrix products, arithmetic and copies ran while one was open for 0% -> 1% of each run, Pallas kernels for 11% -> 11%
where the time goes in v5:
time: 81.1 us; the launch traced here: 80.6 us
  waiting for transfers between devices  37.3 us (46%)
  starting transfers between devices  27 us (33%)
  Pallas kernels  12.8 us (16%)
  local copies, waits for them, and re-layouts  2.36 us (3%)
    ppermute x14, waiting for transfers between devices, swap(): lax.ppermute(x, axis, [(i, i ^ bit) for i in range(lax.axis_size(axis))])  36.6 us
    ppermute x14, starting transfers between devices, swap(): lax.ppermute(x, axis, [(i, i ^ bit) for i in range(lax.axis_size(axis))])  20.8 us
    all_to_all x1, starting transfers between devices, quick(): lax.all_to_all(back, 'row', split_axis=0, concat_axis=0, tiled=True)  5.59 us
    pallas_call x2, Pallas kernels, quick(): pl.pallas_call(join_kernel, grid_spec=pltpu.PrefetchScalarGridSpec(num_sc...  3.15 us
    pallas_call x1, Pallas kernels, quick(): pl.pallas_call(lambda *refs: back_kernel(shift, *refs), out_shape=jax.Sha...  3 us
    unnamed x9, local copies, waits for them, and re-layouts  2.33 us
    pallas_call x1, Pallas kernels, quick(): pl.pallas_call(windows_kernel, out_shape=jax.ShapeDtypeStruct((tiles + 2...  1.82 us
  transfers between devices with their start and end apart: 16, of which 8 were waited for; matrix products, arithmetic and copies ran while one was open for 1% of the time, Pallas kernels for 11%

profile of v5, /device:TPU:0, one launch (start us, length us, event | category | flops | bytes accessed | tf_op | source)
XLA Modules:
  0.0 80.6 jit_solution(10314625156626140415)
XLA Ops:
  0.6 0.0 copy-start.1
  0.6 1.2 %copy-done.1 = bf16[4,64,2048]{2,1,0:T(8,128)(2,1)S(1)} copy-done((bf16[4,64,2048]{2,1,0:T(8,128)(2,1)S(1)}, bf16[4,64,2048]{2,1,0:T(8,128)(2,1)}, u32[]{:S(2)}) %copy-start.1) | copy-done | bytes 1048600
  1.9 1.1 %split.1 = (bf16[4,256,256]{2,1,0:T(8,128)(2,1)S(1)}, bf16[3,256,256]{2,1,0:T(8,128)(2,1)S(1)}, bf16[2,256,256]{2,1,0:T(8,128)(2,1)S(1)}) custom-call(s32[1]{0:T(128)} %bitcast.me_ref.refs_0_, bf16[256,2048]{1,0:T(8,128)(2,1)S(1)} %bitcast.20, bf16[256,256]{1,0:T(8,128)(2,1)} %bitcast.3.own_ref.refs_0_), custom_call_target="tpu_custom_call" | custom-call | tf_op jit(solution)/shard_map/split/pallas_call | solution.py:200
  3.0 3.0 %collective-permute-start.3 = (bf16[2,256,256]{2,1,0:T(8,128)(2,1)S(1)}, bf16[2,256,256]{2,1,0:T(8,128)(2,1)S(1)}, u32[]{:S(2)}, u32[]{:S(2)}) collective-permute-start(bf16[2,256,256]{2,1,0:T(8,128)(2,1)S(1)} %get-tuple-element.24), channel_id=1, source_target_pairs={{0,4},{4,0},{8,12},{12,8},{16,20},{20,16},{24,28},{28,24},{1,5},{5... | collective-permute-start | bytes 786440 | tf_op jit(solution)/shard_map/ppermute | solution.py:15
  6.0 2.6 %collective-permute-start.2 = (bf16[256,256]{1,0:T(8,128)(2,1)}, bf16[256,256]{1,0:T(8,128)(2,1)S(1)}, u32[]{:S(2)}, u32[]{:S(2)}) collective-permute-start(bf16[256,256]{1,0:T(8,128)(2,1)} %bitcast.3.own_ref.refs_0_), channel_id=1, source_target_pairs={{0,16},{4,20},{8,24},{12,28},{16,0},{20,4},{24,8},{28,12},{1,17},{... | collective-permute-start | bytes 393224 | tf_op jit(solution)/shard_map/ppermute | solution.py:15
  8.6 0.5 collective-permute-start
  9.1 1.6 %collective-permute-start.6 = (bf16[256,256]{1,0:T(8,128)(2,1)}, bf16[256,256]{1,0:T(8,128)(2,1)S(1)}, u32[]{:S(2)}, u32[]{:S(2)}) collective-permute-start(bf16[256,256]{1,0:T(8,128)(2,1)} %bitcast.3.own_ref.refs_0_), channel_id=1, source_target_pairs={{0,8},{4,12},{8,0},{12,4},{16,24},{20,28},{24,16},{28,20},{1,9},{5... | collective-permute-start | bytes 393224 | tf_op jit(solution)/shard_map/ppermute | solution.py:15
  10.7 2.5 %collective-permute-done.3.refs_1_ = bf16[2,256,256]{2,1,0:T(8,128)(2,1)S(1)} collective-permute-done((bf16[2,256,256]{2,1,0:T(8,128)(2,1)S(1)}, bf16[2,256,256]{2,1,0:T(8,128)(2,1)S(1)}, u32[]{:S(2)}, u32[]{:S(2)}) %collective-permute-start.3) | collective-permute-done | bytes 262176 | tf_op jit(solution)/shard_map/ppermute | solution.py:15
  13.2 1.8 %collective-permute-done.2 = bf16[256,256]{1,0:T(8,128)(2,1)S(1)} collective-permute-done((bf16[256,256]{1,0:T(8,128)(2,1)}, bf16[256,256]{1,0:T(8,128)(2,1)S(1)}, u32[]{:S(2)}, u32[]{:S(2)}) %collective-permute-start.2) | collective-permute-done | bytes 131104 | tf_op jit(solution)/shard_map/ppermute | solution.py:15
  15.0 0.7 collective-permute-start.7
  15.7 0.9 %bitcast_dynamic-update-slice_fusion = bf16[8,4,64,256]{3,2,1,0:T(8,128)(2,1)S(1)} fusion(bf16[4,64,256]{2,1,0:T(8,128)(2,1)} %param.4), kind=kLoop, calls=%fused_computation.3 | loop fusion | bytes 262144
  16.6 3.3 %collective-permute-start.4 = (bf16[2,256,256]{2,1,0:T(8,128)(2,1)S(1)}, bf16[2,256,256]{2,1,0:T(8,128)(2,1)S(1)}, u32[]{:S(2)}, u32[]{:S(2)}) collective-permute-start(bf16[2,256,256]{2,1,0:T(8,128)(2,1)S(1)} %get-tuple-element.27), channel_id=1, source_target_pairs={{0,16},{4,20},{8,24},{12,28},{16,0},{20,4},{24,8},{28,12},{1,17},{... | collective-permute-start | bytes 786440 | tf_op jit(solution)/shard_map/ppermute | solution.py:15
  19.9 0.4 collective-permute-start.5
  20.3 0.0 collective-permute-done.6
  20.3 0.0 collective-permute-done.7
  20.4 0.5 collective-permute-start.8
  20.9 0.0 collective-permute-done.refs_1_
  21.0 1.7 %collective-permute-start.1 = (bf16[2,256,256]{2,1,0:T(8,128)(2,1)S(1)}, bf16[2,256,256]{2,1,0:T(8,128)(2,1)S(1)}, u32[]{:S(2)}, u32[]{:S(2)}) collective-permute-start(bf16[2,256,256]{2,1,0:T(8,128)(2,1)S(1)} %get-tuple-element.23), channel_id=1, source_target_pairs={{0,8},{4,12},{8,0},{12,4},{16,24},{20,28},{24,16},{28,20},{1,9},{5... | collective-permute-start | bytes 786440 | tf_op jit(solution)/shard_map/ppermute | solution.py:15
  22.7 7.8 %collective-permute-done.8.refs_3_ = bf16[3,256,256]{2,1,0:T(8,128)(2,1)S(1)} collective-permute-done((bf16[3,256,256]{2,1,0:T(8,128)(2,1)S(1)}, bf16[3,256,256]{2,1,0:T(8,128)(2,1)S(1)}, u32[]{:S(2)}, u32[]{:S(2)}) %collective-permute-start.8) | collective-permute-done | bytes 393248 | tf_op jit(solution)/shard_map/ppermute | solution.py:15
  30.5 0.1 broadcast_select_fusion
  30.6 0.7 collective-permute-start.10
  31.3 2.9 %collective-permute-start.9 = (bf16[8,4,12,256]{3,2,1,0:T(8,128)(2,1)S(1)}, bf16[8,4,12,256]{3,2,1,0:T(8,128)(2,1)S(1)}, u32[]{:S(2)}, u32[]{:S(2)}) collective-permute-start(bf16[8,4,12,256]{3,2,1,0:T(8,128)(2,1)S(1)} %get-tuple-element.39), channel_id=1, source_target_pairs={{0,1},{1,0},{2,3},{3,2},{4,5},{5,4},{6,7},{7,6},{8,9},{9,8},{10,11... | collective-permute-start | bytes 589832 | tf_op jit(solution)/shard_map/ppermute | solution.py:15
  34.2 0.0 collective-permute-done.10.refs_5_
  34.2 1.2 %collective-permute-done.9.refs_4_ = bf16[8,4,12,256]{3,2,1,0:T(8,128)(2,1)S(1)} collective-permute-done((bf16[8,4,12,256]{3,2,1,0:T(8,128)(2,1)S(1)}, bf16[8,4,12,256]{3,2,1,0:T(8,128)(2,1)S(1)}, u32[]{:S(2)}, u32[]{:S(2)}) %collective-permute-start.9) | collective-permute-done | bytes 196640 | tf_op jit(solution)/shard_map/ppermute | solution.py:15
  35.4 1.8 %windows.1.refs_6_.refs_1_.refs_0_ = bf16[14,256,768]{2,1,0:T(8,128)(2,1)S(1)} custom-call(s32[1]{0:T(128)} %bitcast.me_ref.refs_0_, s32[1]{0:T(128)} %bitcast.1.core_ref.refs_1_.half_ref, bf16[256,256]{1,0:T(8,128)(2,1)} %bitcast.3.own_ref.refs_0_, bf16[3,256,256]{2,1,0:T(8,128)(2,1)S(1)} %collective-permute-done.refs_1_, ...), custom_call_target="tpu_custom_call" | custom-call | tf_op jit(solution)/shard_map/windows/pallas_call | solution.py:242
  37.2 1.1 %collective-permute-done.4.refs_4_ = bf16[2,256,256]{2,1,0:T(8,128)(2,1)S(1)} collective-permute-done((bf16[2,256,256]{2,1,0:T(8,128)(2,1)S(1)}, bf16[2,256,256]{2,1,0:T(8,128)(2,1)S(1)}, u32[]{:S(2)}, u32[]{:S(2)}) %collective-permute-start.4) | collective-permute-done | bytes 262176 | tf_op jit(solution)/shard_map/ppermute | solution.py:15
  38.3 0.0 collective-permute-done.5.refs_5_
  38.3 0.0 collective-permute-done.1.refs_3_
  38.3 1.4 %other_terms.1 = (f32[9,128,256]{2,1,0:T(8,128)S(1)}, bf16[128,2048]{1,0:T(8,128)(2,1)S(1)}) custom-call(s32[1]{0:T(128)} %bitcast.me_ref.refs_0_, s32[1]{0:T(128)} %bitcast.1.core_ref.refs_1_.half_ref, bf16[2,256,256]{2,1,0:T(8,128)(2,1)S(1)} %get-tuple-element.22.refs_2_, bf16[2,256,256]{2,1,0:T(8,128)(2,1)S(1)} %collective-permute-done.1.refs_3_, ...), custom_call_target="tpu_custom_call" | custom-call | tf_op jit(solution)/shard_map/other_terms/pallas_call | solution.py:258
  39.7 2.1 %collective-permute-start.11 = (f32[9,128,256]{2,1,0:T(8,128)S(1)}, f32[9,128,256]{2,1,0:T(8,128)S(1)}, u32[]{:S(2)}, u32[]{:S(2)}) collective-permute-start(f32[9,128,256]{2,1,0:T(8,128)S(1)} %get-tuple-element.32), channel_id=1, source_target_pairs={{0,1},{1,0},{2,3},{3,2},{4,5},{5,4},{6,7},{7,6},{8,9},{9,8},{10,11... | collective-permute-start | bytes 3538952 | tf_op jit(solution)/shard_map/ppermute | solution.py:15
  41.8 0.0 copy-start
  41.8 1.1 %mine_terms.1 = f32[9,128,256]{2,1,0:T(8,128)S(1)} custom-call(bf16[128,2048]{1,0:T(8,128)(2,1)S(1)} %get-tuple-element.30.refs_0_, bf16[14,256,768]{2,1,0:T(8,128)(2,1)S(1)} %windows.1.refs_6_.refs_1_.refs_0_), custom_call_target="tpu_custom_call" | custom-call | tf_op jit(solution)/shard_map/mine_terms/pallas_call | solution.py:281
  42.9 0.1 copy-done
  43.1 3.0 %back.1 = bf16[8,256,256]{2,1,0:T(8,128)(2,1)} custom-call(bf16[14,256,768]{2,1,0:T(8,128)(2,1)S(1)} %windows.1.refs_6_.refs_1_.refs_0_, bf16[9,256,256]{2,1,0:T(8,128)(2,1)S(1)} %bitcast.19), custom_call_target="tpu_custom_call" | custom-call | tf_op jit(solution)/shard_map/back/pallas_call | solution.py:272
  46.1 0.0 collective-permute-done.11
  46.1 0.2 add.8.part_ref
  46.3 1.5 %collective-permute-start.13 = (f32[9,128,256]{2,1,0:T(8,128)S(1)}, f32[9,128,256]{2,1,0:T(8,128)S(1)}, u32[]{:S(2)}, u32[]{:S(2)}) collective-permute-start(f32[9,128,256]{2,1,0:T(8,128)S(1)} %add.8.part_ref), channel_id=1, source_target_pairs={{0,2},{1,3},{2,0},{3,1},{4,6},{5,7},{6,4},{7,5},{8,10},{9,11},{10,... | collective-permute-start | bytes 3538952 | tf_op jit(solution)/shard_map/ppermute | solution.py:15
  47.7 5.6 %all-to-all-start = ((bf16[8,256,256]{2,1,0:T(8,128)(2,1)}), bf16[8,256,256]{2,1,0:T(8,128)(2,1)S(1)}, u32[]{:S(2)}, u32[]{:S(2)}) async-start(bf16[8,256,256]{2,1,0:T(8,128)(2,1)} %back.1), calls=%async_computation | async-start | bytes 2097152 | tf_op jit(solution)/shard_map/all_to_all | solution.py:312
  53.3 0.0 collective-permute-start.12
  53.3 21.0 %collective-permute-done.13.part_x_ref = f32[9,128,256]{2,1,0:T(8,128)S(1)} collective-permute-done((f32[9,128,256]{2,1,0:T(8,128)S(1)}, f32[9,128,256]{2,1,0:T(8,128)S(1)}, u32[]{:S(2)}, u32[]{:S(2)}) %collective-permute-start.13) | collective-permute-done | bytes 1179680 | tf_op jit(solution)/shard_map/ppermute | solution.py:15
  74.4 0.0 collective-permute-start.14
  74.4 1.6 %join.2.refs_0_ = f32[9,256,256]{2,1,0:T(8,128)} custom-call(s32[1]{0:T(128)} %bitcast.1.core_ref.refs_1_.half_ref, f32[9,128,256]{2,1,0:T(8,128)S(1)} %add.8.part_ref, f32[9,128,256]{2,1,0:T(8,128)S(1)} %collective-permute-done.13.part_x_ref), custom_call_target="tpu_custom_call" | custom-call | tf_op jit(solution)/shard_map/join/pallas_call | solution.py:297
  75.9 0.0 collective-permute-done.12.part_ref
  75.9 1.3 %collective-permute-done.14.part_x_ref = f32[9,128,256]{2,1,0:T(8,128)S(1)} collective-permute-done((f32[9,128,256]{2,1,0:T(8,128)S(1)}, f32[9,128,256]{2,1,0:T(8,128)S(1)}, u32[]{:S(2)}, u32[]{:S(2)}) %collective-permute-start.14) | collective-permute-done | bytes 1179680 | tf_op jit(solution)/shard_map/ppermute | solution.py:15
  77.2 1.6 %join.3 = f32[9,256,256]{2,1,0:T(8,128)} custom-call(s32[1]{0:T(128)S(6)} %sub.3.half_ref, f32[9,128,256]{2,1,0:T(8,128)S(1)} %collective-permute-done.12.part_ref, f32[9,128,256]{2,1,0:T(8,128)S(1)} %collective-permute-done.14.part_x_ref, f32[9,256,256]{2,1,0:T(8,128)} %join.2.refs_0_), custom_call_target="tpu_custom_call", output_to_operand_aliasing={{}: (3, {})} | custom-call | tf_op jit(solution)/shard_map/join/pallas_call | solution.py:297
  78.8 0.7 all-to-all-done.block_ref
  79.5 1.1 %merge.1 = bf16[256,2048]{1,0:T(8,128)(2,1)} custom-call(bf16[8,256,256]{2,1,0:T(8,128)(2,1)S(1)} %all-to-all-done.block_ref), custom_call_target="tpu_custom_call" | custom-call | tf_op jit(solution)/shard_map/merge/pallas_call | solution.py:314
  (9 shorter events, 0.2 us)
Async XLA Ops:
  0.6 1.2 %copy-start.1 = (bf16[4,64,2048]{2,1,0:T(8,128)(2,1)S(1)}, bf16[4,64,2048]{2,1,0:T(8,128)(2,1)}, u32[]{:S(2)}) copy-start(bf16[4,64,2048]{2,1,0:T(8,128)(2,1)} %param.3) | copy-start | bytes 3145732
  3.0 10.2 %collective-permute-start.3 = (bf16[2,256,256]{2,1,0:T(8,128)(2,1)S(1)}, bf16[2,256,256]{2,1,0:T(8,128)(2,1)S(1)}, u32[]{:S(2)}, u32[]{:S(2)}) collective-permute-start(bf16[2,256,256]{2,1,0:T(8,128)(2,1)S(1)} %get-tuple-element.24), channel_id=1, source_target_pairs={{0,4},{4,0},{8,12},{12,8},{16,20},{20,16},{24,28},{28,24},{1,5},{5... | collective-permute-start | bytes 786440 | tf_op jit(solution)/shard_map/ppermute | solution.py:15
  6.0 9.0 %collective-permute-start.2 = (bf16[256,256]{1,0:T(8,128)(2,1)}, bf16[256,256]{1,0:T(8,128)(2,1)S(1)}, u32[]{:S(2)}, u32[]{:S(2)}) collective-permute-start(bf16[256,256]{1,0:T(8,128)(2,1)} %bitcast.3.own_ref.refs_0_), channel_id=1, source_target_pairs={{0,16},{4,20},{8,24},{12,28},{16,0},{20,4},{24,8},{28,12},{1,17},{... | collective-permute-start | bytes 393224 | tf_op jit(solution)/shard_map/ppermute | solution.py:15
  8.6 12.3 %collective-permute-start = (bf16[3,256,256]{2,1,0:T(8,128)(2,1)S(1)}, bf16[3,256,256]{2,1,0:T(8,128)(2,1)S(1)}, u32[]{:S(2)}, u32[]{:S(2)}) collective-permute-start(bf16[3,256,256]{2,1,0:T(8,128)(2,1)S(1)} %get-tuple-element.21), channel_id=1, source_target_pairs={{0,4},{4,0},{8,12},{12,8},{16,20},{20,16},{24,28},{28,24},{1,5},{5... | collective-permute-start | bytes 1179656 | tf_op jit(solution)/shard_map/ppermute | solution.py:15
  9.1 11.3 %collective-permute-start.6 = (bf16[256,256]{1,0:T(8,128)(2,1)}, bf16[256,256]{1,0:T(8,128)(2,1)S(1)}, u32[]{:S(2)}, u32[]{:S(2)}) collective-permute-start(bf16[256,256]{1,0:T(8,128)(2,1)} %bitcast.3.own_ref.refs_0_), channel_id=1, source_target_pairs={{0,8},{4,12},{8,0},{12,4},{16,24},{20,28},{24,16},{28,20},{1,9},{5... | collective-permute-start | bytes 393224 | tf_op jit(solution)/shard_map/ppermute | solution.py:15
  15.0 5.4 %collective-permute-start.7 = (bf16[256,256]{1,0:T(8,128)(2,1)S(1)}, bf16[256,256]{1,0:T(8,128)(2,1)S(1)}, u32[]{:S(2)}, u32[]{:S(2)}) collective-permute-start(bf16[256,256]{1,0:T(8,128)(2,1)S(1)} %collective-permute-done.2), channel_id=1, source_target_pairs={{0,8},{4,12},{8,0},{12,4},{16,24},{20,28},{24,16},{28,20},{1,9},{5... | collective-permute-start | bytes 393224 | tf_op jit(solution)/shard_map/ppermute | solution.py:15
  16.6 21.7 %collective-permute-start.4 = (bf16[2,256,256]{2,1,0:T(8,128)(2,1)S(1)}, bf16[2,256,256]{2,1,0:T(8,128)(2,1)S(1)}, u32[]{:S(2)}, u32[]{:S(2)}) collective-permute-start(bf16[2,256,256]{2,1,0:T(8,128)(2,1)S(1)} %get-tuple-element.27), channel_id=1, source_target_pairs={{0,16},{4,20},{8,24},{12,28},{16,0},{20,4},{24,8},{28,12},{1,17},{... | collective-permute-start | bytes 786440 | tf_op jit(solution)/shard_map/ppermute | solution.py:15
  19.9 18.4 %collective-permute-start.5 = (bf16[2,256,256]{2,1,0:T(8,128)(2,1)S(1)}, bf16[2,256,256]{2,1,0:T(8,128)(2,1)S(1)}, u32[]{:S(2)}, u32[]{:S(2)}) collective-permute-start(bf16[2,256,256]{2,1,0:T(8,128)(2,1)S(1)} %get-tuple-element.28), channel_id=1, source_target_pairs={{0,24},{4,28},{8,16},{12,20},{16,8},{20,12},{24,0},{28,4},{1,25},{... | collective-permute-start | bytes 786440 | tf_op jit(solution)/shard_map/ppermute | solution.py:15
  20.4 10.1 %collective-permute-start.8 = (bf16[3,256,256]{2,1,0:T(8,128)(2,1)S(1)}, bf16[3,256,256]{2,1,0:T(8,128)(2,1)S(1)}, u32[]{:S(2)}, u32[]{:S(2)}) collective-permute-start(bf16[3,256,256]{2,1,0:T(8,128)(2,1)S(1)} %pad_maximum_fusion.refs_2_), channel_id=1, source_target_pairs={{0,4},{4,0},{8,12},{12,8},{16,20},{20,16},{24,28},{28,24},{1,5},{5... | collective-permute-start | bytes 1179656 | tf_op jit(solution)/shard_map/ppermute | solution.py:15
  21.0 17.4 %collective-permute-start.1 = (bf16[2,256,256]{2,1,0:T(8,128)(2,1)S(1)}, bf16[2,256,256]{2,1,0:T(8,128)(2,1)S(1)}, u32[]{:S(2)}, u32[]{:S(2)}) collective-permute-start(bf16[2,256,256]{2,1,0:T(8,128)(2,1)S(1)} %get-tuple-element.23), channel_id=1, source_target_pairs={{0,8},{4,12},{8,0},{12,4},{16,24},{20,28},{24,16},{28,20},{1,9},{5... | collective-permute-start | bytes 786440 | tf_op jit(solution)/shard_map/ppermute | solution.py:15
  30.6 3.6 %collective-permute-start.10 = (bf16[8,4,12,256]{3,2,1,0:T(8,128)(2,1)S(1)}, bf16[8,4,12,256]{3,2,1,0:T(8,128)(2,1)S(1)}, u32[]{:S(2)}, u32[]{:S(2)}) collective-permute-start(bf16[8,4,12,256]{3,2,1,0:T(8,128)(2,1)S(1)} %get-tuple-element.38), channel_id=1, source_target_pairs={{1,2},{2,1},{5,6},{6,5},{9,10},{10,9},{13,14},{14,13},{17,18},{18,... | collective-permute-start | bytes 589832 | tf_op jit(solution)/shard_map/ppermute | solution.py:23
  31.3 4.1 %collective-permute-start.9 = (bf16[8,4,12,256]{3,2,1,0:T(8,128)(2,1)S(1)}, bf16[8,4,12,256]{3,2,1,0:T(8,128)(2,1)S(1)}, u32[]{:S(2)}, u32[]{:S(2)}) collective-permute-start(bf16[8,4,12,256]{3,2,1,0:T(8,128)(2,1)S(1)} %get-tuple-element.39), channel_id=1, source_target_pairs={{0,1},{1,0},{2,3},{3,2},{4,5},{5,4},{6,7},{7,6},{8,9},{9,8},{10,11... | collective-permute-start | bytes 589832 | tf_op jit(solution)/shard_map/ppermute | solution.py:15
  39.7 6.3 %collective-permute-start.11 = (f32[9,128,256]{2,1,0:T(8,128)S(1)}, f32[9,128,256]{2,1,0:T(8,128)S(1)}, u32[]{:S(2)}, u32[]{:S(2)}) collective-permute-start(f32[9,128,256]{2,1,0:T(8,128)S(1)} %get-tuple-element.32), channel_id=1, source_target_pairs={{0,1},{1,0},{2,3},{3,2},{4,5},{5,4},{6,7},{7,6},{8,9},{9,8},{10,11... | collective-permute-start | bytes 3538952 | tf_op jit(solution)/shard_map/ppermute | solution.py:15
  41.8 1.3 %copy-start = (bf16[3,3,256,256]{3,2,1,0:T(8,128)(2,1)S(1)}, bf16[3,3,256,256]{3,2,1,0:T(8,128)(2,1)}, u32[]{:S(2)}) copy-start(bf16[3,3,256,256]{3,2,1,0:T(8,128)(2,1)} %param.5) | copy-start | bytes 3538948
  46.3 28.1 %collective-permute-start.13 = (f32[9,128,256]{2,1,0:T(8,128)S(1)}, f32[9,128,256]{2,1,0:T(8,128)S(1)}, u32[]{:S(2)}, u32[]{:S(2)}) collective-permute-start(f32[9,128,256]{2,1,0:T(8,128)S(1)} %add.8.part_ref), channel_id=1, source_target_pairs={{0,2},{1,3},{2,0},{3,1},{4,6},{5,7},{6,4},{7,5},{8,10},{9,11},{10,... | collective-permute-start | bytes 3538952 | tf_op jit(solution)/shard_map/ppermute | solution.py:15
  47.7 31.7 %all-to-all-start = ((bf16[8,256,256]{2,1,0:T(8,128)(2,1)}), bf16[8,256,256]{2,1,0:T(8,128)(2,1)S(1)}, u32[]{:S(2)}, u32[]{:S(2)}) async-start(bf16[8,256,256]{2,1,0:T(8,128)(2,1)} %back.1), calls=%async_computation | async-start | bytes 2097152 | tf_op jit(solution)/shard_map/all_to_all | solution.py:312
  53.3 22.6 %collective-permute-start.12 = (f32[9,128,256]{2,1,0:T(8,128)S(1)}, f32[9,128,256]{2,1,0:T(8,128)S(1)}, u32[]{:S(2)}, u32[]{:S(2)}) collective-permute-start(f32[9,128,256]{2,1,0:T(8,128)S(1)} %add.8.part_ref), channel_id=1, source_target_pairs={{0,1},{1,0},{2,3},{3,2},{4,5},{5,4},{6,7},{7,6},{8,9},{9,8},{10,11... | collective-permute-start | bytes 3538952 | tf_op jit(solution)/shard_map/ppermute | solution.py:15
  74.4 2.8 %collective-permute-start.14 = (f32[9,128,256]{2,1,0:T(8,128)S(1)}, f32[9,128,256]{2,1,0:T(8,128)S(1)}, u32[]{:S(2)}, u32[]{:S(2)}) collective-permute-start(f32[9,128,256]{2,1,0:T(8,128)S(1)} %collective-permute-done.13.part_x_ref), channel_id=1, source_target_pairs={{0,1},{1,0},{2,3},{3,2},{4,5},{5,4},{6,7},{7,6},{8,9},{9,8},{10,11... | collective-permute-start | bytes 3538952 | tf_op jit(solution)/shard_map/ppermute | solution.py:15

commit v6 on v5

--- a/solution.py
+++ b/solution.py
@@ -26,20 +26,18 @@
     return near, beside
 
 
-def split_kernel(me_ref, in_ref, own_ref, stay_ref, go_ref, go_far_ref):
+def split_kernel(me_ref, in_ref, own_ref, stay_ref, go_own_ref, go_near_ref, go_far_ref):
     zs, _, panel = stay_ref.shape
 
     def channels(owner):
         return in_ref[:, pl.ds(pl.multiple_of(owner * panel, 128), panel)]
 
+    targets = [go_own_ref.at[0], go_near_ref.at[0], go_far_ref.at[0], go_far_ref.at[1]]
     for k in range(zs):
         owner = me_ref[0] ^ (2 * k)
         stay_ref[k] = channels(owner)
-        if k < zs // 2:
-            go_ref[k] = channels(owner ^ 1)
-        else:
-            go_far_ref[k - zs // 2] = channels(owner ^ 1)
-    go_ref[zs // 2] = own_ref[...]
+        targets[k][...] = channels(owner ^ 1)
+    go_near_ref[1] = own_ref[...]
 
 
 def pack_kernel(first, stay_ref, got_ref, *out_refs):
@@ -66,14 +64,16 @@
 
 
 def piece_copies(piece_refs, tile_ref, near_ref, beside_ref, sem):
-    own_ref, got_ref, rest_ref, rest_y_ref, near_from, beside_from = piece_refs
+    own_ref, got_ref, rest_ref, rest_y_ref, *relayed_refs, near_from, beside_from = piece_refs
     tiles = tile_ref.shape[0]
     copies = []
     for k in range(tiles):
         if k < 2:
             source = got_ref.at[got_ref.shape[0] - 1] if k else own_ref
+        elif k < tiles - 2:
+            source = (rest_y_ref if k % 2 else rest_ref).at[k // 2 - 1]
         else:
-            source = (rest_y_ref if k % 2 else rest_ref).at[k // 2 - 1]
+            source = relayed_refs[k % 2]
         copies.append(pltpu.make_async_copy(source, tile_ref.at[k], sem.at[k]))
     copies.append(pltpu.make_async_copy(near_from, near_ref, sem.at[tiles]))
     copies.append(pltpu.make_async_copy(beside_from, beside_ref, sem.at[tiles + 1]))
@@ -85,10 +85,6 @@
     rows, step = near_ref.shape[1:3]
     width = positions // rows
     pad = (windows_ref.shape[0] - tiles) // 2
-    zeros = jnp.zeros(windows_ref.shape[1:], windows_ref.dtype)
-    for k in range(pad):
-        windows_ref[k] = zeros
-        windows_ref[pad + tiles + k] = zeros
     for k in range(tiles):
         tile = tile_ref[k].reshape(rows, width, outs)
         at = k if k < 2 else k // 2 + 1 + k % 2 * (tiles // 2 - 1)
@@ -109,24 +105,40 @@
 
 
 def windows_kernel(me_ref, core_ref, *refs):
-    piece_refs, windows_ref = refs[:6], refs[6]
-    tile_ref, near_ref, beside_ref, sem = refs[7:]
+    piece_refs, windows_ref = refs[:8], refs[8]
+    tile_ref, near_ref, beside_ref, sem = refs[9:]
     wait_all(start_all(piece_copies(piece_refs, tile_ref, near_ref, beside_ref, sem)))
     windows_of(me_ref[0], core_ref[0], tile_ref, near_ref, beside_ref, windows_ref)
 
 
 def back_kernel(shift, windows_ref, weight_ref, back_ref, flat_ref):
-    tiles, depth = back_ref.shape[0], windows_ref.shape[2]
-    outs = weight_ref.shape[2]
+    tiles, positions, chans = back_ref.shape
+    depth, outs = windows_ref.shape[2], weight_ref.shape[2]
     for t in range(weight_ref.shape[0]):
         flat_ref[:, t * outs : (t + 1) * outs] = weight_ref[t]
-    for j in range(tiles):
-        taps = [a for a in range(3) if 0 <= j - shift * (a - 1) < tiles]
-        lhs = jnp.concatenate([windows_ref[j - shift * (a - 2)] for a in taps], axis=1)
+    reach = [[a for a in range(3) if 0 <= j - shift * (a - 1) < tiles] for j in range(tiles)]
+    first = 0
+    while first < tiles:
+        taps, last = reach[first], first + 1
+        while last < tiles and reach[last] == taps:
+            last += 1
+        lhs = jnp.concatenate(
+            [
+                windows_ref[pl.ds(shift + first - shift * (a - 1), last - first)].reshape(
+                    (last - first) * positions, depth
+                )
+                for a in taps
+            ],
+            axis=1,
+        )
         rhs = flat_ref[:, taps[0] * depth : (taps[-1] + 1) * depth]
-        back_ref[j] = lax.dot_general(
+        product = lax.dot_general(
             lhs, rhs, (((1,), (1,)), ((), ())), preferred_element_type=jnp.float32
-        ).astype(back_ref.dtype)
+        )
+        back_ref[pl.ds(first, last - first)] = product.astype(back_ref.dtype).reshape(
+            last - first, positions, chans
+        )
+        first = last
 
 
 def terms_of(pad, scale, flipped, windows_ref, out_ref):
@@ -149,11 +161,14 @@
     tiles, positions, chans = strip_ref.shape
     half = chans // 2
     core, me = core_ref[0], me_ref[0]
+    stay_ref, got_ref, *pair_refs = strip_from
+    places = [(stay_ref.at[pl.ds(0, 1)], 0, 1), (got_ref, 1, 1)]
+    places += [(ref, 2 * k, 2) for k, ref in enumerate(pair_refs, 1)]
     wait_all(
         start_all(
             [
-                pltpu.make_async_copy(ref, strip_ref.at[pl.ds(2 * k, 2)], sem.at[k])
-                for k, ref in enumerate(strip_from)
+                pltpu.make_async_copy(ref, strip_ref.at[pl.ds(first, count)], sem.at[n])
+                for n, (ref, first, count) in enumerate(places)
             ]
         )
     )
@@ -196,8 +211,8 @@
 
     zs = tiles // 2
     flat = inputs.reshape(positions, in_chans)
-    sizes = (zs, zs // 2 + 1, zs // 2)
-    stay, go, go_far = pl.pallas_call(
+    sizes = (zs, 1, 2, 2)
+    stay, go_own, go_near, go_far = pl.pallas_call(
         split_kernel,
         grid=(2,),
         out_shape=[jax.ShapeDtypeStruct((n, positions, panel), jnp.bfloat16) for n in sizes],
@@ -212,10 +227,9 @@
     )(me, flat, output_gradient.reshape(positions, outs))
     own = output_gradient.reshape(positions, outs)
     got_far = swap(go_far, "row", 1)
-    got = swap(go, "row", 1)
-
-    def pack(first, arrived):
-        count = zs // 2
+    got = swap(go_near, "row", 1)
+
+    def pack(first, count, arrived):
         return pl.pallas_call(
             lambda *refs: pack_kernel(first, *refs),
             grid=(1,),
@@ -226,23 +240,27 @@
             name="pack",
         )(stay, arrived)
 
-    far_pairs = pack(zs // 2, got_far)
+    far_pairs = pack(2, 2, got_far)
     far = swap(own, "row", 4)
     far, *far_pairs = lax.optimization_barrier((far, *far_pairs))
-    rest = jnp.stack([swap(own, "row", 2), far, swap(far, "row", 2)])
-    pairs = [*pack(0, got), *far_pairs]
-    strip = [p if k == 0 else swap(p, "row", 2 * k) for k, p in enumerate(pairs)]
-
+    rest = jnp.stack([swap(own, "row", 2), far])
+    relayed = swap(far, "row", 2)
+    pairs = [*pack(1, 1, got), *far_pairs]
+    got_own = swap(go_own, "row", 1)
+    strip = [stay, got_own] + [swap(p, "row", 2 * k) for k, p in enumerate(pairs, 1)]
+
+    relayed, strip[1] = lax.optimization_barrier((relayed, strip[1]))
     rest_y = swap(rest, "row", 1)
-    stacked = jnp.concatenate([own[None], got[zs // 2 :], rest, rest_y])
+    relayed_y = swap(relayed, "row", 1)
+    stacked = jnp.concatenate([own[None], got[1:], rest, relayed[None], rest_y, relayed_y[None]])
     near, beside = rims(stacked.reshape(tiles, rows, width, outs), DILATION_STEP, core)
 
-    pieces = (own, got, rest, rest_y, near, beside)
+    pieces = (own, got, rest, rest_y, relayed, relayed_y, near, beside)
     hbm = pl.BlockSpec(memory_space=pltpu.HBM)
     windows = pl.pallas_call(
         windows_kernel,
         out_shape=jax.ShapeDtypeStruct((tiles + 2 * shift, positions, 3 * outs), jnp.bfloat16),
-        in_specs=[smem, smem] + [hbm] * 6,
+        in_specs=[smem, smem] + [hbm] * 8,
         out_specs=vmem(1)[0],
         scratch_shapes=[
             pltpu.VMEM((tiles, positions, outs), jnp.bfloat16),
@@ -258,12 +276,12 @@
     theirs, flipped = pl.pallas_call(
         lambda *refs: other_kernel(shift, scale, *refs),
         out_shape=(half, jax.ShapeDtypeStruct((panel // 2, tiles * positions), jnp.bfloat16)),
-        in_specs=[smem, smem] + [hbm] * zs + vmem(1),
+        in_specs=[smem, smem] + [hbm] * (zs + 1) + vmem(1),
         out_specs=tuple(vmem(2)),
         scratch_shapes=[
             pltpu.VMEM((tiles, positions, panel), jnp.bfloat16),
             pltpu.VMEM((panel // 2, tiles * positions), jnp.bfloat16),
-            pltpu.SemaphoreType.DMA((zs,)),
+            pltpu.SemaphoreType.DMA((zs + 1,)),
         ],
         compiler_params=params,
         name="other_terms",

time: 81.1 us -> 80.9 us (level)
    ppermute x14 -> x16, starting transfers between devices: 20.8 us -> 22.6 us  [swap(): lax.ppermute(x, axis, [(i, i ^ bit) for i in range(lax.axis_size(axis))])]
    all_to_all x1, starting transfers between devices: 5.59 us -> 4.28 us  [quick(): lax.all_to_all(back, 'row', split_axis=0, concat_axis=0, tiled=True)]
    unnamed x9 -> x10, local copies, waits for them, and re-layouts: 2.33 us -> 2.34 us
    ppermute x14 -> x16, waiting for transfers between devices: 36.6 us -> 36.6 us  [swap(): lax.ppermute(x, axis, [(i, i ^ bit) for i in range(lax.axis_size(axis))])]
  transfers between devices with their start and end apart: 16 -> 18, of which waited for: 8 -> 7; matrix products, arithmetic and copies ran while one was open for 1% -> 1% of each run, Pallas kernels for 11% -> 11%
where the time goes in v6:
time: 80.9 us; the launch traced here: 80.5 us
  waiting for transfers between devices  36.6 us (45%)
  starting transfers between devices  27.5 us (34%)
  Pallas kernels  12.9 us (16%)
  local copies, waits for them, and re-layouts  2.36 us (3%)
  between operations  0.84 us (1%)
    ppermute x16, waiting for transfers between devices, swap(): lax.ppermute(x, axis, [(i, i ^ bit) for i in range(lax.axis_size(axis))])  36.6 us
    ppermute x16, starting transfers between devices, swap(): lax.ppermute(x, axis, [(i, i ^ bit) for i in range(lax.axis_size(axis))])  22.6 us
    all_to_all x1, starting transfers between devices, quick(): lax.all_to_all(back, 'row', split_axis=0, concat_axis=0, tiled=True)  4.28 us
    pallas_call x2, Pallas kernels, quick(): pl.pallas_call(join_kernel, grid_spec=pltpu.PrefetchScalarGridSpec(num_sc...  3.15 us
    pallas_call x1, Pallas kernels, quick(): pl.pallas_call(lambda *refs: back_kernel(shift, *refs), out_shape=jax.Sha...  2.99 us
    unnamed x10, local copies, waits for them, and re-layouts  2.34 us
    pallas_call x1, Pallas kernels, quick(): pl.pallas_call(lambda *refs: other_kernel(shift, scale, *refs), out_shape...  1.7 us
    pallas_call x1, Pallas kernels, quick(): pl.pallas_call(windows_kernel, out_shape=jax.ShapeDtypeStruct((tiles + 2...  1.67 us
  transfers between devices with their start and end apart: 18, of which 7 were waited for; matrix products, arithmetic and copies ran while one was open for 1% of the time, Pallas kernels for 11%

profile of v6, /device:TPU:0, one launch (start us, length us, event | category | flops | bytes accessed | tf_op | source)
XLA Modules:
  0.0 80.5 jit_solution(14957019752876952038)
XLA Ops:
  0.6 0.0 copy-start.1
  0.6 1.2 %copy-done.1 = bf16[4,64,2048]{2,1,0:T(8,128)(2,1)S(1)} copy-done((bf16[4,64,2048]{2,1,0:T(8,128)(2,1)S(1)}, bf16[4,64,2048]{2,1,0:T(8,128)(2,1)}, u32[]{:S(2)}) %copy-start.1) | copy-done | bytes 1048600
  1.9 1.1 %split.1 = (bf16[4,256,256]{2,1,0:T(8,128)(2,1)S(1)}, bf16[1,256,256]{2,1,0:T(8,128)(2,1)S(1)}, bf16[2,256,256]{2,1,0:T(8,128)(2,1)S(1)}, bf16[2,256,256]{2,1,0:T(8,128)(2,1)S(1)}) custom-call(s32[1]{0:T(128)} %bitcast.me_ref.refs_0_, bf16[256,2048]{1,0:T(8,128)(2,1)S(1)} %bitcast.19, bf16[256,256]{1,0:T(8,128)(2,1)} %bitcast.3.own_ref.refs_0_), custom_call_target="tpu_custom_call" | custom-call | tf_op jit(solution)/shard_map/split/pallas_call | solution.py:215
  3.0 3.0 %collective-permute-start.1 = (bf16[2,256,256]{2,1,0:T(8,128)(2,1)S(1)}, bf16[2,256,256]{2,1,0:T(8,128)(2,1)S(1)}, u32[]{:S(2)}, u32[]{:S(2)}) collective-permute-start(bf16[2,256,256]{2,1,0:T(8,128)(2,1)S(1)} %get-tuple-element.22), channel_id=1, source_target_pairs={{0,4},{4,0},{8,12},{12,8},{16,20},{20,16},{24,28},{28,24},{1,5},{5... | collective-permute-start | bytes 786440 | tf_op jit(solution)/shard_map/ppermute | solution.py:15
  6.0 1.6 %collective-permute-start.8 = (bf16[256,256]{1,0:T(8,128)(2,1)}, bf16[256,256]{1,0:T(8,128)(2,1)S(1)}, u32[]{:S(2)}, u32[]{:S(2)}) collective-permute-start(bf16[256,256]{1,0:T(8,128)(2,1)} %bitcast.3.own_ref.refs_0_), channel_id=1, source_target_pairs={{0,8},{4,12},{8,0},{12,4},{16,24},{20,28},{24,16},{28,20},{1,9},{5... | collective-permute-start | bytes 393224 | tf_op jit(solution)/shard_map/ppermute | solution.py:15
  7.6 2.6 %collective-permute-start = (bf16[256,256]{1,0:T(8,128)(2,1)}, bf16[256,256]{1,0:T(8,128)(2,1)S(1)}, u32[]{:S(2)}, u32[]{:S(2)}) collective-permute-start(bf16[256,256]{1,0:T(8,128)(2,1)} %bitcast.3.own_ref.refs_0_), channel_id=1, source_target_pairs={{0,16},{4,20},{8,24},{12,28},{16,0},{20,4},{24,8},{28,12},{1,17},{... | collective-permute-start | bytes 393224 | tf_op jit(solution)/shard_map/ppermute | solution.py:15
  10.2 0.5 collective-permute-start.3
  10.7 1.5 %collective-permute-start.4 = (bf16[2,256,256]{2,1,0:T(8,128)(2,1)S(1)}, bf16[2,256,256]{2,1,0:T(8,128)(2,1)S(1)}, u32[]{:S(2)}, u32[]{:S(2)}) collective-permute-start(bf16[2,256,256]{2,1,0:T(8,128)(2,1)S(1)} %get-tuple-element.28), channel_id=1, source_target_pairs={{0,4},{4,0},{8,12},{12,8},{16,20},{20,16},{24,28},{28,24},{1,5},{5... | collective-permute-start | bytes 786440 | tf_op jit(solution)/shard_map/ppermute | solution.py:15
  12.2 0.9 %bitcast_dynamic-update-slice_fusion = bf16[8,4,64,256]{3,2,1,0:T(8,128)(2,1)S(1)} fusion(bf16[4,64,256]{2,1,0:T(8,128)(2,1)} %param.4), kind=kLoop, calls=%fused_computation.3 | loop fusion | bytes 262144
  13.1 0.0 collective-permute-done.1.refs_1_
  13.2 3.2 %collective-permute-done = bf16[256,256]{1,0:T(8,128)(2,1)S(1)} collective-permute-done((bf16[256,256]{1,0:T(8,128)(2,1)}, bf16[256,256]{1,0:T(8,128)(2,1)S(1)}, u32[]{:S(2)}, u32[]{:S(2)}) %collective-permute-start) | collective-permute-done | bytes 131104 | tf_op jit(solution)/shard_map/ppermute | solution.py:15
  16.3 0.2 collective-permute-start.2
  16.6 0.0 collective-permute-done.8
  16.6 0.6 collective-permute-start.9
  17.2 2.7 %collective-permute-start.6 = (bf16[2,256,256]{2,1,0:T(8,128)(2,1)S(1)}, bf16[2,256,256]{2,1,0:T(8,128)(2,1)S(1)}, u32[]{:S(2)}, u32[]{:S(2)}) collective-permute-start(bf16[2,256,256]{2,1,0:T(8,128)(2,1)S(1)} %get-tuple-element.29), channel_id=1, source_target_pairs={{0,16},{4,20},{8,24},{12,28},{16,0},{20,4},{24,8},{28,12},{1,17},{... | collective-permute-start | bytes 786440 | tf_op jit(solution)/shard_map/ppermute | solution.py:15
  19.9 2.4 %collective-permute-done.4.refs_1_ = bf16[2,256,256]{2,1,0:T(8,128)(2,1)S(1)} collective-permute-done((bf16[2,256,256]{2,1,0:T(8,128)(2,1)S(1)}, bf16[2,256,256]{2,1,0:T(8,128)(2,1)S(1)}, u32[]{:S(2)}, u32[]{:S(2)}) %collective-permute-start.4) | collective-permute-done | bytes 262176 | tf_op jit(solution)/shard_map/ppermute | solution.py:15
  22.2 3.5 %collective-permute-start.7 = (bf16[2,256,256]{2,1,0:T(8,128)(2,1)S(1)}, bf16[2,256,256]{2,1,0:T(8,128)(2,1)S(1)}, u32[]{:S(2)}, u32[]{:S(2)}) collective-permute-start(bf16[2,256,256]{2,1,0:T(8,128)(2,1)S(1)} %get-tuple-element.30), channel_id=1, source_target_pairs={{0,24},{4,28},{8,16},{12,20},{16,8},{20,12},{24,0},{28,4},{1,25},{... | collective-permute-start | bytes 786440 | tf_op jit(solution)/shard_map/ppermute | solution.py:15
  25.8 0.0 collective-permute-done.3.refs_3_
  25.8 0.1 collective-permute-start.5
  25.9 0.0 collective-permute-done.2.refs_4_
  25.9 1.6 %collective-permute-start.10 = (bf16[256,256]{1,0:T(8,128)(2,1)S(1)}, bf16[256,256]{1,0:T(8,128)(2,1)S(1)}, u32[]{:S(2)}, u32[]{:S(2)}) collective-permute-start(bf16[256,256]{1,0:T(8,128)(2,1)S(1)} %collective-permute-done.2.refs_4_), channel_id=1, source_target_pairs={{0,4},{4,0},{8,12},{12,8},{16,20},{20,16},{24,28},{28,24},{1,5},{5... | collective-permute-start | bytes 393224 | tf_op jit(solution)/shard_map/ppermute | solution.py:15
  27.5 0.0 collective-permute-done.9.refs_3_
  27.5 3.4 %collective-permute-done.10.refs_5_ = bf16[256,256]{1,0:T(8,128)(2,1)S(1)} collective-permute-done((bf16[256,256]{1,0:T(8,128)(2,1)S(1)}, bf16[256,256]{1,0:T(8,128)(2,1)S(1)}, u32[]{:S(2)}, u32[]{:S(2)}) %collective-permute-start.10) | collective-permute-done | bytes 131104 | tf_op jit(solution)/shard_map/ppermute | solution.py:15
  30.9 0.1 broadcast_select_fusion
  31.0 0.7 collective-permute-start.12
  31.7 2.9 %collective-permute-start.11 = (bf16[8,4,12,256]{3,2,1,0:T(8,128)(2,1)S(1)}, bf16[8,4,12,256]{3,2,1,0:T(8,128)(2,1)S(1)}, u32[]{:S(2)}, u32[]{:S(2)}) collective-permute-start(bf16[8,4,12,256]{3,2,1,0:T(8,128)(2,1)S(1)} %get-tuple-element.41), channel_id=1, source_target_pairs={{0,1},{1,0},{2,3},{3,2},{4,5},{5,4},{6,7},{7,6},{8,9},{9,8},{10,11... | collective-permute-start | bytes 589832 | tf_op jit(solution)/shard_map/ppermute | solution.py:15
  34.6 0.0 collective-permute-done.12.refs_7_
  34.6 1.2 %collective-permute-done.11.refs_6_ = bf16[8,4,12,256]{3,2,1,0:T(8,128)(2,1)S(1)} collective-permute-done((bf16[8,4,12,256]{3,2,1,0:T(8,128)(2,1)S(1)}, bf16[8,4,12,256]{3,2,1,0:T(8,128)(2,1)S(1)}, u32[]{:S(2)}, u32[]{:S(2)}) %collective-permute-start.11) | collective-permute-done | bytes 196640 | tf_op jit(solution)/shard_map/ppermute | solution.py:15
  35.8 1.7 %windows.1.refs_7_.refs_1_.refs_0_ = bf16[14,256,768]{2,1,0:T(8,128)(2,1)S(1)} custom-call(s32[1]{0:T(128)} %bitcast.me_ref.refs_0_, s32[1]{0:T(128)} %bitcast.1.core_ref.refs_1_.half_ref, bf16[256,256]{1,0:T(8,128)(2,1)} %bitcast.3.own_ref.refs_0_, bf16[2,256,256]{2,1,0:T(8,128)(2,1)S(1)} %collective-permute-done.4.refs_1_, ...), custom_call_target="tpu_custom_call" | custom-call | tf_op jit(solution)/shard_map/windows/pallas_call | solution.py:260
  37.5 0.0 collective-permute-done.6.refs_5_
  37.5 0.0 collective-permute-done.7.refs_6_
  37.5 2.8 %collective-permute-done.5.refs_4_ = bf16[2,256,256]{2,1,0:T(8,128)(2,1)S(1)} collective-permute-done((bf16[2,256,256]{2,1,0:T(8,128)(2,1)S(1)}, bf16[2,256,256]{2,1,0:T(8,128)(2,1)S(1)}, u32[]{:S(2)}, u32[]{:S(2)}) %collective-permute-start.5) | collective-permute-done | bytes 262176 | tf_op jit(solution)/shard_map/ppermute | solution.py:15
  40.3 1.7 %other_terms.1 = (f32[9,128,256]{2,1,0:T(8,128)S(1)}, bf16[128,2048]{1,0:T(8,128)(2,1)S(1)}) custom-call(s32[1]{0:T(128)} %bitcast.me_ref.refs_0_, s32[1]{0:T(128)} %bitcast.1.core_ref.refs_1_.half_ref, bf16[4,256,256]{2,1,0:T(8,128)(2,1)S(1)} %get-tuple-element.21.refs_0_.refs_2_, bf16[1,256,256]{2,1,0:T(8,128)(2,1)S(1)} %collective-permute-done.3.refs_3_, ...), custom_call_target="tpu_custom_call" | custom-call | tf_op jit(solution)/shard_map/other_terms/pallas_call | solution.py:276
  42.0 0.4 collective-permute-start.13
  42.4 0.0 copy-start
  42.4 1.1 %mine_terms.1 = f32[9,128,256]{2,1,0:T(8,128)S(1)} custom-call(bf16[128,2048]{1,0:T(8,128)(2,1)S(1)} %get-tuple-element.32.refs_0_, bf16[14,256,768]{2,1,0:T(8,128)(2,1)S(1)} %windows.1.refs_7_.refs_1_.refs_0_), custom_call_target="tpu_custom_call" | custom-call | tf_op jit(solution)/shard_map/mine_terms/pallas_call | solution.py:299
  43.5 0.1 copy-done
  43.7 3.0 %back.1 = bf16[8,256,256]{2,1,0:T(8,128)(2,1)} custom-call(bf16[14,256,768]{2,1,0:T(8,128)(2,1)S(1)} %windows.1.refs_7_.refs_1_.refs_0_, bf16[9,256,256]{2,1,0:T(8,128)(2,1)S(1)} %bitcast.18), custom_call_target="tpu_custom_call" | custom-call | tf_op jit(solution)/shard_map/back/pallas_call | solution.py:290
  46.7 0.0 collective-permute-done.13
  46.7 0.2 add.8.part_ref
  46.9 1.4 %collective-permute-start.15 = (f32[9,128,256]{2,1,0:T(8,128)S(1)}, f32[9,128,256]{2,1,0:T(8,128)S(1)}, u32[]{:S(2)}, u32[]{:S(2)}) collective-permute-start(f32[9,128,256]{2,1,0:T(8,128)S(1)} %add.8.part_ref), channel_id=1, source_target_pairs={{0,2},{1,3},{2,0},{3,1},{4,6},{5,7},{6,4},{7,5},{8,10},{9,11},{10,... | collective-permute-start | bytes 3538952 | tf_op jit(solution)/shard_map/ppermute | solution.py:15
  48.3 4.3 %all-to-all-start = ((bf16[8,256,256]{2,1,0:T(8,128)(2,1)}), bf16[8,256,256]{2,1,0:T(8,128)(2,1)S(1)}, u32[]{:S(2)}, u32[]{:S(2)}) async-start(bf16[8,256,256]{2,1,0:T(8,128)(2,1)} %back.1), calls=%async_computation | async-start | bytes 2097152 | tf_op jit(solution)/shard_map/all_to_all | solution.py:330
  52.6 0.0 collective-permute-start.14
  52.6 22.4 %collective-permute-done.15.part_x_ref = f32[9,128,256]{2,1,0:T(8,128)S(1)} collective-permute-done((f32[9,128,256]{2,1,0:T(8,128)S(1)}, f32[9,128,256]{2,1,0:T(8,128)S(1)}, u32[]{:S(2)}, u32[]{:S(2)}) %collective-permute-start.15) | collective-permute-done | bytes 1179680 | tf_op jit(solution)/shard_map/ppermute | solution.py:15
  75.0 0.0 collective-permute-start.16
  75.0 1.6 %join.2.refs_0_ = f32[9,256,256]{2,1,0:T(8,128)} custom-call(s32[1]{0:T(128)} %bitcast.1.core_ref.refs_1_.half_ref, f32[9,128,256]{2,1,0:T(8,128)S(1)} %add.8.part_ref, f32[9,128,256]{2,1,0:T(8,128)S(1)} %collective-permute-done.15.part_x_ref), custom_call_target="tpu_custom_call" | custom-call | tf_op jit(solution)/shard_map/join/pallas_call | solution.py:315
  76.6 0.0 collective-permute-done.14.part_ref
  76.6 1.3 %collective-permute-done.16.part_x_ref = f32[9,128,256]{2,1,0:T(8,128)S(1)} collective-permute-done((f32[9,128,256]{2,1,0:T(8,128)S(1)}, f32[9,128,256]{2,1,0:T(8,128)S(1)}, u32[]{:S(2)}, u32[]{:S(2)}) %collective-permute-start.16) | collective-permute-done | bytes 1179680 | tf_op jit(solution)/shard_map/ppermute | solution.py:15
  77.9 1.6 %join.3 = f32[9,256,256]{2,1,0:T(8,128)} custom-call(s32[1]{0:T(128)S(6)} %sub.3.half_ref, f32[9,128,256]{2,1,0:T(8,128)S(1)} %collective-permute-done.14.part_ref, f32[9,128,256]{2,1,0:T(8,128)S(1)} %collective-permute-done.16.part_x_ref, f32[9,256,256]{2,1,0:T(8,128)} %join.2.refs_0_), custom_call_target="tpu_custom_call", output_to_operand_aliasing={{}: (3, {})} | custom-call | tf_op jit(solution)/shard_map/join/pallas_call | solution.py:315
  79.4 0.0 all-to-all-done.block_ref
  79.4 1.1 %merge.1 = bf16[256,2048]{1,0:T(8,128)(2,1)} custom-call(bf16[8,256,256]{2,1,0:T(8,128)(2,1)S(1)} %all-to-all-done.block_ref), custom_call_target="tpu_custom_call" | custom-call | tf_op jit(solution)/shard_map/merge/pallas_call | solution.py:332
  (10 shorter events, 0.2 us)
Async XLA Ops:
  0.6 1.2 %copy-start.1 = (bf16[4,64,2048]{2,1,0:T(8,128)(2,1)S(1)}, bf16[4,64,2048]{2,1,0:T(8,128)(2,1)}, u32[]{:S(2)}) copy-start(bf16[4,64,2048]{2,1,0:T(8,128)(2,1)} %param.3) | copy-start | bytes 3145732
  3.0 10.1 %collective-permute-start.1 = (bf16[2,256,256]{2,1,0:T(8,128)(2,1)S(1)}, bf16[2,256,256]{2,1,0:T(8,128)(2,1)S(1)}, u32[]{:S(2)}, u32[]{:S(2)}) collective-permute-start(bf16[2,256,256]{2,1,0:T(8,128)(2,1)S(1)} %get-tuple-element.22), channel_id=1, source_target_pairs={{0,4},{4,0},{8,12},{12,8},{16,20},{20,16},{24,28},{28,24},{1,5},{5... | collective-permute-start | bytes 786440 | tf_op jit(solution)/shard_map/ppermute | solution.py:15
  6.0 10.6 %collective-permute-start.8 = (bf16[256,256]{1,0:T(8,128)(2,1)}, bf16[256,256]{1,0:T(8,128)(2,1)S(1)}, u32[]{:S(2)}, u32[]{:S(2)}) collective-permute-start(bf16[256,256]{1,0:T(8,128)(2,1)} %bitcast.3.own_ref.refs_0_), channel_id=1, source_target_pairs={{0,8},{4,12},{8,0},{12,4},{16,24},{20,28},{24,16},{28,20},{1,9},{5... | collective-permute-start | bytes 393224 | tf_op jit(solution)/shard_map/ppermute | solution.py:15
  7.6 8.8 %collective-permute-start = (bf16[256,256]{1,0:T(8,128)(2,1)}, bf16[256,256]{1,0:T(8,128)(2,1)S(1)}, u32[]{:S(2)}, u32[]{:S(2)}) collective-permute-start(bf16[256,256]{1,0:T(8,128)(2,1)} %bitcast.3.own_ref.refs_0_), channel_id=1, source_target_pairs={{0,16},{4,20},{8,24},{12,28},{16,0},{20,4},{24,8},{28,12},{1,17},{... | collective-permute-start | bytes 393224 | tf_op jit(solution)/shard_map/ppermute | solution.py:15
  10.2 15.6 %collective-permute-start.3 = (bf16[1,256,256]{2,1,0:T(8,128)(2,1)S(1)}, bf16[1,256,256]{2,1,0:T(8,128)(2,1)S(1)}, u32[]{:S(2)}, u32[]{:S(2)}) collective-permute-start(bf16[1,256,256]{2,1,0:T(8,128)(2,1)S(1)} %get-tuple-element.26), channel_id=1, source_target_pairs={{0,4},{4,0},{8,12},{12,8},{16,20},{20,16},{24,28},{28,24},{1,5},{5... | collective-permute-start | bytes 393224 | tf_op jit(solution)/shard_map/ppermute | solution.py:15
  10.7 11.5 %collective-permute-start.4 = (bf16[2,256,256]{2,1,0:T(8,128)(2,1)S(1)}, bf16[2,256,256]{2,1,0:T(8,128)(2,1)S(1)}, u32[]{:S(2)}, u32[]{:S(2)}) collective-permute-start(bf16[2,256,256]{2,1,0:T(8,128)(2,1)S(1)} %get-tuple-element.28), channel_id=1, source_target_pairs={{0,4},{4,0},{8,12},{12,8},{16,20},{20,16},{24,28},{28,24},{1,5},{5... | collective-permute-start | bytes 786440 | tf_op jit(solution)/shard_map/ppermute | solution.py:15
  16.3 9.5 %collective-permute-start.2 = (bf16[256,256]{1,0:T(8,128)(2,1)S(1)}, bf16[256,256]{1,0:T(8,128)(2,1)S(1)}, u32[]{:S(2)}, u32[]{:S(2)}) collective-permute-start(bf16[256,256]{1,0:T(8,128)(2,1)S(1)} %collective-permute-done), channel_id=1, source_target_pairs={{0,8},{4,12},{8,0},{12,4},{16,24},{20,28},{24,16},{28,20},{1,9},{5... | collective-permute-start | bytes 393224 | tf_op jit(solution)/shard_map/ppermute | solution.py:15
  16.6 10.9 %collective-permute-start.9 = (bf16[2,256,256]{2,1,0:T(8,128)(2,1)S(1)}, bf16[2,256,256]{2,1,0:T(8,128)(2,1)S(1)}, u32[]{:S(2)}, u32[]{:S(2)}) collective-permute-start(bf16[2,256,256]{2,1,0:T(8,128)(2,1)S(1)} %pad_maximum_fusion.refs_2_), channel_id=1, source_target_pairs={{0,4},{4,0},{8,12},{12,8},{16,20},{20,16},{24,28},{28,24},{1,5},{5... | collective-permute-start | bytes 786440 | tf_op jit(solution)/shard_map/ppermute | solution.py:15
  17.2 20.3 %collective-permute-start.6 = (bf16[2,256,256]{2,1,0:T(8,128)(2,1)S(1)}, bf16[2,256,256]{2,1,0:T(8,128)(2,1)S(1)}, u32[]{:S(2)}, u32[]{:S(2)}) collective-permute-start(bf16[2,256,256]{2,1,0:T(8,128)(2,1)S(1)} %get-tuple-element.29), channel_id=1, source_target_pairs={{0,16},{4,20},{8,24},{12,28},{16,0},{20,4},{24,8},{28,12},{1,17},{... | collective-permute-start | bytes 786440 | tf_op jit(solution)/shard_map/ppermute | solution.py:15
  22.2 15.3 %collective-permute-start.7 = (bf16[2,256,256]{2,1,0:T(8,128)(2,1)S(1)}, bf16[2,256,256]{2,1,0:T(8,128)(2,1)S(1)}, u32[]{:S(2)}, u32[]{:S(2)}) collective-permute-start(bf16[2,256,256]{2,1,0:T(8,128)(2,1)S(1)} %get-tuple-element.30), channel_id=1, source_target_pairs={{0,24},{4,28},{8,16},{12,20},{16,8},{20,12},{24,0},{28,4},{1,25},{... | collective-permute-start | bytes 786440 | tf_op jit(solution)/shard_map/ppermute | solution.py:15
  25.8 14.5 %collective-permute-start.5 = (bf16[2,256,256]{2,1,0:T(8,128)(2,1)S(1)}, bf16[2,256,256]{2,1,0:T(8,128)(2,1)S(1)}, u32[]{:S(2)}, u32[]{:S(2)}) collective-permute-start(bf16[2,256,256]{2,1,0:T(8,128)(2,1)S(1)} %pack.3), channel_id=1, source_target_pairs={{0,8},{4,12},{8,0},{12,4},{16,24},{20,28},{24,16},{28,20},{1,9},{5... | collective-permute-start | bytes 786440 | tf_op jit(solution)/shard_map/ppermute | solution.py:15
  25.9 5.0 %collective-permute-start.10 = (bf16[256,256]{1,0:T(8,128)(2,1)S(1)}, bf16[256,256]{1,0:T(8,128)(2,1)S(1)}, u32[]{:S(2)}, u32[]{:S(2)}) collective-permute-start(bf16[256,256]{1,0:T(8,128)(2,1)S(1)} %collective-permute-done.2.refs_4_), channel_id=1, source_target_pairs={{0,4},{4,0},{8,12},{12,8},{16,20},{20,16},{24,28},{28,24},{1,5},{5... | collective-permute-start | bytes 393224 | tf_op jit(solution)/shard_map/ppermute | solution.py:15
  31.0 3.6 %collective-permute-start.12 = (bf16[8,4,12,256]{3,2,1,0:T(8,128)(2,1)S(1)}, bf16[8,4,12,256]{3,2,1,0:T(8,128)(2,1)S(1)}, u32[]{:S(2)}, u32[]{:S(2)}) collective-permute-start(bf16[8,4,12,256]{3,2,1,0:T(8,128)(2,1)S(1)} %get-tuple-element.40), channel_id=1, source_target_pairs={{1,2},{2,1},{5,6},{6,5},{9,10},{10,9},{13,14},{14,13},{17,18},{18,... | collective-permute-start | bytes 589832 | tf_op jit(solution)/shard_map/ppermute | solution.py:23
  31.7 4.1 %collective-permute-start.11 = (bf16[8,4,12,256]{3,2,1,0:T(8,128)(2,1)S(1)}, bf16[8,4,12,256]{3,2,1,0:T(8,128)(2,1)S(1)}, u32[]{:S(2)}, u32[]{:S(2)}) collective-permute-start(bf16[8,4,12,256]{3,2,1,0:T(8,128)(2,1)S(1)} %get-tuple-element.41), channel_id=1, source_target_pairs={{0,1},{1,0},{2,3},{3,2},{4,5},{5,4},{6,7},{7,6},{8,9},{9,8},{10,11... | collective-permute-start | bytes 589832 | tf_op jit(solution)/shard_map/ppermute | solution.py:15
  42.0 4.7 %collective-permute-start.13 = (f32[9,128,256]{2,1,0:T(8,128)S(1)}, f32[9,128,256]{2,1,0:T(8,128)S(1)}, u32[]{:S(2)}, u32[]{:S(2)}) collective-permute-start(f32[9,128,256]{2,1,0:T(8,128)S(1)} %get-tuple-element.34), channel_id=1, source_target_pairs={{0,1},{1,0},{2,3},{3,2},{4,5},{5,4},{6,7},{7,6},{8,9},{9,8},{10,11... | collective-permute-start | bytes 3538952 | tf_op jit(solution)/shard_map/ppermute | solution.py:15
  42.4 1.3 %copy-start = (bf16[3,3,256,256]{3,2,1,0:T(8,128)(2,1)S(1)}, bf16[3,3,256,256]{3,2,1,0:T(8,128)(2,1)}, u32[]{:S(2)}) copy-start(bf16[3,3,256,256]{3,2,1,0:T(8,128)(2,1)} %param.5) | copy-start | bytes 3538948
  46.9 28.1 %collective-permute-start.15 = (f32[9,128,256]{2,1,0:T(8,128)S(1)}, f32[9,128,256]{2,1,0:T(8,128)S(1)}, u32[]{:S(2)}, u32[]{:S(2)}) collective-permute-start(f32[9,128,256]{2,1,0:T(8,128)S(1)} %add.8.part_ref), channel_id=1, source_target_pairs={{0,2},{1,3},{2,0},{3,1},{4,6},{5,7},{6,4},{7,5},{8,10},{9,11},{10,... | collective-permute-start | bytes 3538952 | tf_op jit(solution)/shard_map/ppermute | solution.py:15
  48.3 31.1 %all-to-all-start = ((bf16[8,256,256]{2,1,0:T(8,128)(2,1)}), bf16[8,256,256]{2,1,0:T(8,128)(2,1)S(1)}, u32[]{:S(2)}, u32[]{:S(2)}) async-start(bf16[8,256,256]{2,1,0:T(8,128)(2,1)} %back.1), calls=%async_computation | async-start | bytes 2097152 | tf_op jit(solution)/shard_map/all_to_all | solution.py:330
  52.6 24.0 %collective-permute-start.14 = (f32[9,128,256]{2,1,0:T(8,128)S(1)}, f32[9,128,256]{2,1,0:T(8,128)S(1)}, u32[]{:S(2)}, u32[]{:S(2)}) collective-permute-start(f32[9,128,256]{2,1,0:T(8,128)S(1)} %add.8.part_ref), channel_id=1, source_target_pairs={{0,1},{1,0},{2,3},{3,2},{4,5},{5,4},{6,7},{7,6},{8,9},{9,8},{10,11... | collective-permute-start | bytes 3538952 | tf_op jit(solution)/shard_map/ppermute | solution.py:15
  75.0 2.8 %collective-permute-start.16 = (f32[9,128,256]{2,1,0:T(8,128)S(1)}, f32[9,128,256]{2,1,0:T(8,128)S(1)}, u32[]{:S(2)}, u32[]{:S(2)}) collective-permute-start(f32[9,128,256]{2,1,0:T(8,128)S(1)} %collective-permute-done.15.part_x_ref), channel_id=1, source_target_pairs={{0,1},{1,0},{2,3},{3,2},{4,5},{5,4},{6,7},{7,6},{8,9},{9,8},{10,11... | collective-permute-start | bytes 3538952 | tf_op jit(solution)/shard_map/ppermute | solution.py:15

commit v7 on v6

--- a/solution.py
+++ b/solution.py
@@ -311,12 +311,12 @@
     grad_weight = None
     for which, terms in ((core, (chip, across)), (1 - core, other)):
         before = [] if grad_weight is None else [grad_weight]
-        block = (3, panel // 2, outs)
+        block = (9, panel // 2, outs)
         grad_weight = pl.pallas_call(
             join_kernel,
             grid_spec=pltpu.PrefetchScalarGridSpec(
                 num_scalar_prefetch=1,
-                grid=(3,),
+                grid=(1,),
                 in_specs=[pl.BlockSpec(block, lambda i, h: (i, 0, 0))] * 2
                 + [pl.BlockSpec(memory_space=pl.ANY)] * len(before),
                 out_specs=pl.BlockSpec(block, lambda i, h: (i, h[0], 0)),

time: 80.9 us -> 80.4 us (level)
  Pallas kernels: 12.9 us -> 12 us
    pallas_call x2, Pallas kernels: 3.15 us -> 2.27 us  [quick(): pl.pallas_call(join_kernel, grid_spec=pltpu.PrefetchScalarGridSpec(num_sc...]
  transfers between devices with their start and end apart: 18 -> 18, of which waited for: 7 -> 7; matrix products, arithmetic and copies ran while one was open for 1% -> 1% of each run, Pallas kernels for 11% -> 10%
where the time goes in v7:
time: 80.4 us; the launch traced here: 80.1 us
  waiting for transfers between devices  37.1 us (46%)
  starting transfers between devices  27.5 us (34%)
  Pallas kernels  12 us (15%)
  local copies, waits for them, and re-layouts  2.36 us (3%)
  between operations  0.84 us (1%)
    ppermute x16, waiting for transfers between devices, swap(): lax.ppermute(x, axis, [(i, i ^ bit) for i in range(lax.axis_size(axis))])  37.1 us
    ppermute x16, starting transfers between devices, swap(): lax.ppermute(x, axis, [(i, i ^ bit) for i in range(lax.axis_size(axis))])  22.6 us
    all_to_all x1, starting transfers between devices, quick(): lax.all_to_all(back, 'row', split_axis=0, concat_axis=0, tiled=True)  4.28 us
    pallas_call x1, Pallas kernels, quick(): pl.pallas_call(lambda *refs: back_kernel(shift, *refs), out_shape=jax.Sha...  2.99 us
    unnamed x10, local copies, waits for them, and re-layouts  2.34 us
    pallas_call x2, Pallas kernels, quick(): pl.pallas_call(join_kernel, grid_spec=pltpu.PrefetchScalarGridSpec(num_sc...  2.27 us
    pallas_call x1, Pallas kernels, quick(): pl.pallas_call(lambda *refs: other_kernel(shift, scale, *refs), out_shape...  1.7 us
    pallas_call x1, Pallas kernels, quick(): pl.pallas_call(windows_kernel, out_shape=jax.ShapeDtypeStruct((tiles + 2...  1.67 us
  transfers between devices with their start and end apart: 18, of which 7 were waited for; matrix products, arithmetic and copies ran while one was open for 1% of the time, Pallas kernels for 10%

profile of v7, /device:TPU:0, one launch (start us, length us, event | category | flops | bytes accessed | tf_op | source)
XLA Modules:
  0.0 80.1 jit_solution(14849511137853139171)
XLA Ops:
  0.6 0.0 copy-start.1
  0.6 1.2 %copy-done.1 = bf16[4,64,2048]{2,1,0:T(8,128)(2,1)S(1)} copy-done((bf16[4,64,2048]{2,1,0:T(8,128)(2,1)S(1)}, bf16[4,64,2048]{2,1,0:T(8,128)(2,1)}, u32[]{:S(2)}) %copy-start.1) | copy-done | bytes 1048600
  1.9 1.1 %split.1 = (bf16[4,256,256]{2,1,0:T(8,128)(2,1)S(1)}, bf16[1,256,256]{2,1,0:T(8,128)(2,1)S(1)}, bf16[2,256,256]{2,1,0:T(8,128)(2,1)S(1)}, bf16[2,256,256]{2,1,0:T(8,128)(2,1)S(1)}) custom-call(s32[1]{0:T(128)} %bitcast.me_ref.refs_0_, bf16[256,2048]{1,0:T(8,128)(2,1)S(1)} %bitcast.19, bf16[256,256]{1,0:T(8,128)(2,1)} %bitcast.3.own_ref.refs_0_), custom_call_target="tpu_custom_call" | custom-call | tf_op jit(solution)/shard_map/split/pallas_call | solution.py:215
  3.0 3.0 %collective-permute-start.1 = (bf16[2,256,256]{2,1,0:T(8,128)(2,1)S(1)}, bf16[2,256,256]{2,1,0:T(8,128)(2,1)S(1)}, u32[]{:S(2)}, u32[]{:S(2)}) collective-permute-start(bf16[2,256,256]{2,1,0:T(8,128)(2,1)S(1)} %get-tuple-element.22), channel_id=1, source_target_pairs={{0,4},{4,0},{8,12},{12,8},{16,20},{20,16},{24,28},{28,24},{1,5},{5... | collective-permute-start | bytes 786440 | tf_op jit(solution)/shard_map/ppermute | solution.py:15
  6.0 1.6 %collective-permute-start.8 = (bf16[256,256]{1,0:T(8,128)(2,1)}, bf16[256,256]{1,0:T(8,128)(2,1)S(1)}, u32[]{:S(2)}, u32[]{:S(2)}) collective-permute-start(bf16[256,256]{1,0:T(8,128)(2,1)} %bitcast.3.own_ref.refs_0_), channel_id=1, source_target_pairs={{0,8},{4,12},{8,0},{12,4},{16,24},{20,28},{24,16},{28,20},{1,9},{5... | collective-permute-start | bytes 393224 | tf_op jit(solution)/shard_map/ppermute | solution.py:15
  7.6 2.6 %collective-permute-start = (bf16[256,256]{1,0:T(8,128)(2,1)}, bf16[256,256]{1,0:T(8,128)(2,1)S(1)}, u32[]{:S(2)}, u32[]{:S(2)}) collective-permute-start(bf16[256,256]{1,0:T(8,128)(2,1)} %bitcast.3.own_ref.refs_0_), channel_id=1, source_target_pairs={{0,16},{4,20},{8,24},{12,28},{16,0},{20,4},{24,8},{28,12},{1,17},{... | collective-permute-start | bytes 393224 | tf_op jit(solution)/shard_map/ppermute | solution.py:15
  10.2 0.5 collective-permute-start.3
  10.7 1.5 %collective-permute-start.4 = (bf16[2,256,256]{2,1,0:T(8,128)(2,1)S(1)}, bf16[2,256,256]{2,1,0:T(8,128)(2,1)S(1)}, u32[]{:S(2)}, u32[]{:S(2)}) collective-permute-start(bf16[2,256,256]{2,1,0:T(8,128)(2,1)S(1)} %get-tuple-element.28), channel_id=1, source_target_pairs={{0,4},{4,0},{8,12},{12,8},{16,20},{20,16},{24,28},{28,24},{1,5},{5... | collective-permute-start | bytes 786440 | tf_op jit(solution)/shard_map/ppermute | solution.py:15
  12.2 0.9 %bitcast_dynamic-update-slice_fusion = bf16[8,4,64,256]{3,2,1,0:T(8,128)(2,1)S(1)} fusion(bf16[4,64,256]{2,1,0:T(8,128)(2,1)} %param.4), kind=kLoop, calls=%fused_computation.3 | loop fusion | bytes 262144
  13.1 0.0 collective-permute-done.1.refs_1_
  13.2 3.2 %collective-permute-done = bf16[256,256]{1,0:T(8,128)(2,1)S(1)} collective-permute-done((bf16[256,256]{1,0:T(8,128)(2,1)}, bf16[256,256]{1,0:T(8,128)(2,1)S(1)}, u32[]{:S(2)}, u32[]{:S(2)}) %collective-permute-start) | collective-permute-done | bytes 131104 | tf_op jit(solution)/shard_map/ppermute | solution.py:15
  16.3 0.2 collective-permute-start.2
  16.6 0.0 collective-permute-done.8
  16.6 0.6 collective-permute-start.9
  17.2 2.7 %collective-permute-start.6 = (bf16[2,256,256]{2,1,0:T(8,128)(2,1)S(1)}, bf16[2,256,256]{2,1,0:T(8,128)(2,1)S(1)}, u32[]{:S(2)}, u32[]{:S(2)}) collective-permute-start(bf16[2,256,256]{2,1,0:T(8,128)(2,1)S(1)} %get-tuple-element.29), channel_id=1, source_target_pairs={{0,16},{4,20},{8,24},{12,28},{16,0},{20,4},{24,8},{28,12},{1,17},{... | collective-permute-start | bytes 786440 | tf_op jit(solution)/shard_map/ppermute | solution.py:15
  19.9 2.4 %collective-permute-done.4.refs_1_ = bf16[2,256,256]{2,1,0:T(8,128)(2,1)S(1)} collective-permute-done((bf16[2,256,256]{2,1,0:T(8,128)(2,1)S(1)}, bf16[2,256,256]{2,1,0:T(8,128)(2,1)S(1)}, u32[]{:S(2)}, u32[]{:S(2)}) %collective-permute-start.4) | collective-permute-done | bytes 262176 | tf_op jit(solution)/shard_map/ppermute | solution.py:15
  22.2 3.5 %collective-permute-start.7 = (bf16[2,256,256]{2,1,0:T(8,128)(2,1)S(1)}, bf16[2,256,256]{2,1,0:T(8,128)(2,1)S(1)}, u32[]{:S(2)}, u32[]{:S(2)}) collective-permute-start(bf16[2,256,256]{2,1,0:T(8,128)(2,1)S(1)} %get-tuple-element.30), channel_id=1, source_target_pairs={{0,24},{4,28},{8,16},{12,20},{16,8},{20,12},{24,0},{28,4},{1,25},{... | collective-permute-start | bytes 786440 | tf_op jit(solution)/shard_map/ppermute | solution.py:15
  25.8 0.0 collective-permute-done.3.refs_3_
  25.8 0.1 collective-permute-start.5
  25.9 0.0 collective-permute-done.2.refs_4_
  25.9 1.6 %collective-permute-start.10 = (bf16[256,256]{1,0:T(8,128)(2,1)S(1)}, bf16[256,256]{1,0:T(8,128)(2,1)S(1)}, u32[]{:S(2)}, u32[]{:S(2)}) collective-permute-start(bf16[256,256]{1,0:T(8,128)(2,1)S(1)} %collective-permute-done.2.refs_4_), channel_id=1, source_target_pairs={{0,4},{4,0},{8,12},{12,8},{16,20},{20,16},{24,28},{28,24},{1,5},{5... | collective-permute-start | bytes 393224 | tf_op jit(solution)/shard_map/ppermute | solution.py:15
  27.5 0.0 collective-permute-done.9.refs_3_
  27.5 3.4 %collective-permute-done.10.refs_5_ = bf16[256,256]{1,0:T(8,128)(2,1)S(1)} collective-permute-done((bf16[256,256]{1,0:T(8,128)(2,1)S(1)}, bf16[256,256]{1,0:T(8,128)(2,1)S(1)}, u32[]{:S(2)}, u32[]{:S(2)}) %collective-permute-start.10) | collective-permute-done | bytes 131104 | tf_op jit(solution)/shard_map/ppermute | solution.py:15
  30.9 0.1 broadcast_select_fusion
  31.0 0.7 collective-permute-start.12
  31.7 2.9 %collective-permute-start.11 = (bf16[8,4,12,256]{3,2,1,0:T(8,128)(2,1)S(1)}, bf16[8,4,12,256]{3,2,1,0:T(8,128)(2,1)S(1)}, u32[]{:S(2)}, u32[]{:S(2)}) collective-permute-start(bf16[8,4,12,256]{3,2,1,0:T(8,128)(2,1)S(1)} %get-tuple-element.41), channel_id=1, source_target_pairs={{0,1},{1,0},{2,3},{3,2},{4,5},{5,4},{6,7},{7,6},{8,9},{9,8},{10,11... | collective-permute-start | bytes 589832 | tf_op jit(solution)/shard_map/ppermute | solution.py:15
  34.6 0.0 collective-permute-done.12.refs_7_
  34.6 1.2 %collective-permute-done.11.refs_6_ = bf16[8,4,12,256]{3,2,1,0:T(8,128)(2,1)S(1)} collective-permute-done((bf16[8,4,12,256]{3,2,1,0:T(8,128)(2,1)S(1)}, bf16[8,4,12,256]{3,2,1,0:T(8,128)(2,1)S(1)}, u32[]{:S(2)}, u32[]{:S(2)}) %collective-permute-start.11) | collective-permute-done | bytes 196640 | tf_op jit(solution)/shard_map/ppermute | solution.py:15
  35.8 1.7 %windows.1.refs_7_.refs_1_.refs_0_ = bf16[14,256,768]{2,1,0:T(8,128)(2,1)S(1)} custom-call(s32[1]{0:T(128)} %bitcast.me_ref.refs_0_, s32[1]{0:T(128)} %bitcast.1.core_ref.refs_1_.half_ref, bf16[256,256]{1,0:T(8,128)(2,1)} %bitcast.3.own_ref.refs_0_, bf16[2,256,256]{2,1,0:T(8,128)(2,1)S(1)} %collective-permute-done.4.refs_1_, ...), custom_call_target="tpu_custom_call" | custom-call | tf_op jit(solution)/shard_map/windows/pallas_call | solution.py:260
  37.5 0.0 collective-permute-done.6.refs_5_
  37.5 0.0 collective-permute-done.7.refs_6_
  37.5 2.8 %collective-permute-done.5.refs_4_ = bf16[2,256,256]{2,1,0:T(8,128)(2,1)S(1)} collective-permute-done((bf16[2,256,256]{2,1,0:T(8,128)(2,1)S(1)}, bf16[2,256,256]{2,1,0:T(8,128)(2,1)S(1)}, u32[]{:S(2)}, u32[]{:S(2)}) %collective-permute-start.5) | collective-permute-done | bytes 262176 | tf_op jit(solution)/shard_map/ppermute | solution.py:15
  40.3 1.7 %other_terms.1 = (f32[9,128,256]{2,1,0:T(8,128)S(1)}, bf16[128,2048]{1,0:T(8,128)(2,1)S(1)}) custom-call(s32[1]{0:T(128)} %bitcast.me_ref.refs_0_, s32[1]{0:T(128)} %bitcast.1.core_ref.refs_1_.half_ref, bf16[4,256,256]{2,1,0:T(8,128)(2,1)S(1)} %get-tuple-element.21.refs_0_.refs_2_, bf16[1,256,256]{2,1,0:T(8,128)(2,1)S(1)} %collective-permute-done.3.refs_3_, ...), custom_call_target="tpu_custom_call" | custom-call | tf_op jit(solution)/shard_map/other_terms/pallas_call | solution.py:276
  42.0 0.4 collective-permute-start.13
  42.4 0.0 copy-start
  42.4 1.1 %mine_terms.1 = f32[9,128,256]{2,1,0:T(8,128)S(1)} custom-call(bf16[128,2048]{1,0:T(8,128)(2,1)S(1)} %get-tuple-element.32.refs_0_, bf16[14,256,768]{2,1,0:T(8,128)(2,1)S(1)} %windows.1.refs_7_.refs_1_.refs_0_), custom_call_target="tpu_custom_call" | custom-call | tf_op jit(solution)/shard_map/mine_terms/pallas_call | solution.py:299
  43.5 0.1 copy-done
  43.7 3.0 %back.1 = bf16[8,256,256]{2,1,0:T(8,128)(2,1)} custom-call(bf16[14,256,768]{2,1,0:T(8,128)(2,1)S(1)} %windows.1.refs_7_.refs_1_.refs_0_, bf16[9,256,256]{2,1,0:T(8,128)(2,1)S(1)} %bitcast.18), custom_call_target="tpu_custom_call" | custom-call | tf_op jit(solution)/shard_map/back/pallas_call | solution.py:290
  46.7 0.0 collective-permute-done.13
  46.7 0.2 add.8.part_ref
  46.9 1.4 %collective-permute-start.15 = (f32[9,128,256]{2,1,0:T(8,128)S(1)}, f32[9,128,256]{2,1,0:T(8,128)S(1)}, u32[]{:S(2)}, u32[]{:S(2)}) collective-permute-start(f32[9,128,256]{2,1,0:T(8,128)S(1)} %add.8.part_ref), channel_id=1, source_target_pairs={{0,2},{1,3},{2,0},{3,1},{4,6},{5,7},{6,4},{7,5},{8,10},{9,11},{10,... | collective-permute-start | bytes 3538952 | tf_op jit(solution)/shard_map/ppermute | solution.py:15
  48.3 4.3 %all-to-all-start = ((bf16[8,256,256]{2,1,0:T(8,128)(2,1)}), bf16[8,256,256]{2,1,0:T(8,128)(2,1)S(1)}, u32[]{:S(2)}, u32[]{:S(2)}) async-start(bf16[8,256,256]{2,1,0:T(8,128)(2,1)} %back.1), calls=%async_computation | async-start | bytes 2097152 | tf_op jit(solution)/shard_map/all_to_all | solution.py:330
  52.6 0.0 collective-permute-start.14
  52.6 22.4 %collective-permute-done.15.part_x_ref = f32[9,128,256]{2,1,0:T(8,128)S(1)} collective-permute-done((f32[9,128,256]{2,1,0:T(8,128)S(1)}, f32[9,128,256]{2,1,0:T(8,128)S(1)}, u32[]{:S(2)}, u32[]{:S(2)}) %collective-permute-start.15) | collective-permute-done | bytes 1179680 | tf_op jit(solution)/shard_map/ppermute | solution.py:15
  75.0 0.0 collective-permute-start.16
  75.0 1.1 %join.2.refs_0_ = f32[9,256,256]{2,1,0:T(8,128)} custom-call(s32[1]{0:T(128)} %bitcast.1.core_ref.refs_1_.half_ref, f32[9,128,256]{2,1,0:T(8,128)S(1)} %add.8.part_ref, f32[9,128,256]{2,1,0:T(8,128)S(1)} %collective-permute-done.15.part_x_ref), custom_call_target="tpu_custom_call" | custom-call | tf_op jit(solution)/shard_map/join/pallas_call | solution.py:315
  76.1 0.0 collective-permute-done.14.part_ref
  76.1 1.7 %collective-permute-done.16.part_x_ref = f32[9,128,256]{2,1,0:T(8,128)S(1)} collective-permute-done((f32[9,128,256]{2,1,0:T(8,128)S(1)}, f32[9,128,256]{2,1,0:T(8,128)S(1)}, u32[]{:S(2)}, u32[]{:S(2)}) %collective-permute-start.16) | collective-permute-done | bytes 1179680 | tf_op jit(solution)/shard_map/ppermute | solution.py:15
  77.9 1.1 %join.3 = f32[9,256,256]{2,1,0:T(8,128)} custom-call(s32[1]{0:T(128)S(6)} %sub.3.half_ref, f32[9,128,256]{2,1,0:T(8,128)S(1)} %collective-permute-done.14.part_ref, f32[9,128,256]{2,1,0:T(8,128)S(1)} %collective-permute-done.16.part_x_ref, f32[9,256,256]{2,1,0:T(8,128)} %join.2.refs_0_), custom_call_target="tpu_custom_call", output_to_operand_aliasing={{}: (3, {})} | custom-call | tf_op jit(solution)/shard_map/join/pallas_call | solution.py:315
  79.0 0.0 all-to-all-done.block_ref
  79.0 1.1 %merge.1 = bf16[256,2048]{1,0:T(8,128)(2,1)} custom-call(bf16[8,256,256]{2,1,0:T(8,128)(2,1)S(1)} %all-to-all-done.block_ref), custom_call_target="tpu_custom_call" | custom-call | tf_op jit(solution)/shard_map/merge/pallas_call | solution.py:332
  (10 shorter events, 0.2 us)
Async XLA Ops:
  0.6 1.2 %copy-start.1 = (bf16[4,64,2048]{2,1,0:T(8,128)(2,1)S(1)}, bf16[4,64,2048]{2,1,0:T(8,128)(2,1)}, u32[]{:S(2)}) copy-start(bf16[4,64,2048]{2,1,0:T(8,128)(2,1)} %param.3) | copy-start | bytes 3145732
  3.0 10.1 %collective-permute-start.1 = (bf16[2,256,256]{2,1,0:T(8,128)(2,1)S(1)}, bf16[2,256,256]{2,1,0:T(8,128)(2,1)S(1)}, u32[]{:S(2)}, u32[]{:S(2)}) collective-permute-start(bf16[2,256,256]{2,1,0:T(8,128)(2,1)S(1)} %get-tuple-element.22), channel_id=1, source_target_pairs={{0,4},{4,0},{8,12},{12,8},{16,20},{20,16},{24,28},{28,24},{1,5},{5... | collective-permute-start | bytes 786440 | tf_op jit(solution)/shard_map/ppermute | solution.py:15
  6.0 10.6 %collective-permute-start.8 = (bf16[256,256]{1,0:T(8,128)(2,1)}, bf16[256,256]{1,0:T(8,128)(2,1)S(1)}, u32[]{:S(2)}, u32[]{:S(2)}) collective-permute-start(bf16[256,256]{1,0:T(8,128)(2,1)} %bitcast.3.own_ref.refs_0_), channel_id=1, source_target_pairs={{0,8},{4,12},{8,0},{12,4},{16,24},{20,28},{24,16},{28,20},{1,9},{5... | collective-permute-start | bytes 393224 | tf_op jit(solution)/shard_map/ppermute | solution.py:15
  7.6 8.8 %collective-permute-start = (bf16[256,256]{1,0:T(8,128)(2,1)}, bf16[256,256]{1,0:T(8,128)(2,1)S(1)}, u32[]{:S(2)}, u32[]{:S(2)}) collective-permute-start(bf16[256,256]{1,0:T(8,128)(2,1)} %bitcast.3.own_ref.refs_0_), channel_id=1, source_target_pairs={{0,16},{4,20},{8,24},{12,28},{16,0},{20,4},{24,8},{28,12},{1,17},{... | collective-permute-start | bytes 393224 | tf_op jit(solution)/shard_map/ppermute | solution.py:15
  10.2 15.6 %collective-permute-start.3 = (bf16[1,256,256]{2,1,0:T(8,128)(2,1)S(1)}, bf16[1,256,256]{2,1,0:T(8,128)(2,1)S(1)}, u32[]{:S(2)}, u32[]{:S(2)}) collective-permute-start(bf16[1,256,256]{2,1,0:T(8,128)(2,1)S(1)} %get-tuple-element.26), channel_id=1, source_target_pairs={{0,4},{4,0},{8,12},{12,8},{16,20},{20,16},{24,28},{28,24},{1,5},{5... | collective-permute-start | bytes 393224 | tf_op jit(solution)/shard_map/ppermute | solution.py:15
  10.7 11.5 %collective-permute-start.4 = (bf16[2,256,256]{2,1,0:T(8,128)(2,1)S(1)}, bf16[2,256,256]{2,1,0:T(8,128)(2,1)S(1)}, u32[]{:S(2)}, u32[]{:S(2)}) collective-permute-start(bf16[2,256,256]{2,1,0:T(8,128)(2,1)S(1)} %get-tuple-element.28), channel_id=1, source_target_pairs={{0,4},{4,0},{8,12},{12,8},{16,20},{20,16},{24,28},{28,24},{1,5},{5... | collective-permute-start | bytes 786440 | tf_op jit(solution)/shard_map/ppermute | solution.py:15
  16.3 9.5 %collective-permute-start.2 = (bf16[256,256]{1,0:T(8,128)(2,1)S(1)}, bf16[256,256]{1,0:T(8,128)(2,1)S(1)}, u32[]{:S(2)}, u32[]{:S(2)}) collective-permute-start(bf16[256,256]{1,0:T(8,128)(2,1)S(1)} %collective-permute-done), channel_id=1, source_target_pairs={{0,8},{4,12},{8,0},{12,4},{16,24},{20,28},{24,16},{28,20},{1,9},{5... | collective-permute-start | bytes 393224 | tf_op jit(solution)/shard_map/ppermute | solution.py:15
  16.6 10.9 %collective-permute-start.9 = (bf16[2,256,256]{2,1,0:T(8,128)(2,1)S(1)}, bf16[2,256,256]{2,1,0:T(8,128)(2,1)S(1)}, u32[]{:S(2)}, u32[]{:S(2)}) collective-permute-start(bf16[2,256,256]{2,1,0:T(8,128)(2,1)S(1)} %pad_maximum_fusion.refs_2_), channel_id=1, source_target_pairs={{0,4},{4,0},{8,12},{12,8},{16,20},{20,16},{24,28},{28,24},{1,5},{5... | collective-permute-start | bytes 786440 | tf_op jit(solution)/shard_map/ppermute | solution.py:15
  17.2 20.3 %collective-permute-start.6 = (bf16[2,256,256]{2,1,0:T(8,128)(2,1)S(1)}, bf16[2,256,256]{2,1,0:T(8,128)(2,1)S(1)}, u32[]{:S(2)}, u32[]{:S(2)}) collective-permute-start(bf16[2,256,256]{2,1,0:T(8,128)(2,1)S(1)} %get-tuple-element.29), channel_id=1, source_target_pairs={{0,16},{4,20},{8,24},{12,28},{16,0},{20,4},{24,8},{28,12},{1,17},{... | collective-permute-start | bytes 786440 | tf_op jit(solution)/shard_map/ppermute | solution.py:15
  22.2 15.3 %collective-permute-start.7 = (bf16[2,256,256]{2,1,0:T(8,128)(2,1)S(1)}, bf16[2,256,256]{2,1,0:T(8,128)(2,1)S(1)}, u32[]{:S(2)}, u32[]{:S(2)}) collective-permute-start(bf16[2,256,256]{2,1,0:T(8,128)(2,1)S(1)} %get-tuple-element.30), channel_id=1, source_target_pairs={{0,24},{4,28},{8,16},{12,20},{16,8},{20,12},{24,0},{28,4},{1,25},{... | collective-permute-start | bytes 786440 | tf_op jit(solution)/shard_map/ppermute | solution.py:15
  25.8 14.5 %collective-permute-start.5 = (bf16[2,256,256]{2,1,0:T(8,128)(2,1)S(1)}, bf16[2,256,256]{2,1,0:T(8,128)(2,1)S(1)}, u32[]{:S(2)}, u32[]{:S(2)}) collective-permute-start(bf16[2,256,256]{2,1,0:T(8,128)(2,1)S(1)} %pack.3), channel_id=1, source_target_pairs={{0,8},{4,12},{8,0},{12,4},{16,24},{20,28},{24,16},{28,20},{1,9},{5... | collective-permute-start | bytes 786440 | tf_op jit(solution)/shard_map/ppermute | solution.py:15
  25.9 5.0 %collective-permute-start.10 = (bf16[256,256]{1,0:T(8,128)(2,1)S(1)}, bf16[256,256]{1,0:T(8,128)(2,1)S(1)}, u32[]{:S(2)}, u32[]{:S(2)}) collective-permute-start(bf16[256,256]{1,0:T(8,128)(2,1)S(1)} %collective-permute-done.2.refs_4_), channel_id=1, source_target_pairs={{0,4},{4,0},{8,12},{12,8},{16,20},{20,16},{24,28},{28,24},{1,5},{5... | collective-permute-start | bytes 393224 | tf_op jit(solution)/shard_map/ppermute | solution.py:15
  31.0 3.6 %collective-permute-start.12 = (bf16[8,4,12,256]{3,2,1,0:T(8,128)(2,1)S(1)}, bf16[8,4,12,256]{3,2,1,0:T(8,128)(2,1)S(1)}, u32[]{:S(2)}, u32[]{:S(2)}) collective-permute-start(bf16[8,4,12,256]{3,2,1,0:T(8,128)(2,1)S(1)} %get-tuple-element.40), channel_id=1, source_target_pairs={{1,2},{2,1},{5,6},{6,5},{9,10},{10,9},{13,14},{14,13},{17,18},{18,... | collective-permute-start | bytes 589832 | tf_op jit(solution)/shard_map/ppermute | solution.py:23
  31.7 4.1 %collective-permute-start.11 = (bf16[8,4,12,256]{3,2,1,0:T(8,128)(2,1)S(1)}, bf16[8,4,12,256]{3,2,1,0:T(8,128)(2,1)S(1)}, u32[]{:S(2)}, u32[]{:S(2)}) collective-permute-start(bf16[8,4,12,256]{3,2,1,0:T(8,128)(2,1)S(1)} %get-tuple-element.41), channel_id=1, source_target_pairs={{0,1},{1,0},{2,3},{3,2},{4,5},{5,4},{6,7},{7,6},{8,9},{9,8},{10,11... | collective-permute-start | bytes 589832 | tf_op jit(solution)/shard_map/ppermute | solution.py:15
  42.0 4.7 %collective-permute-start.13 = (f32[9,128,256]{2,1,0:T(8,128)S(1)}, f32[9,128,256]{2,1,0:T(8,128)S(1)}, u32[]{:S(2)}, u32[]{:S(2)}) collective-permute-start(f32[9,128,256]{2,1,0:T(8,128)S(1)} %get-tuple-element.34), channel_id=1, source_target_pairs={{0,1},{1,0},{2,3},{3,2},{4,5},{5,4},{6,7},{7,6},{8,9},{9,8},{10,11... | collective-permute-start | bytes 3538952 | tf_op jit(solution)/shard_map/ppermute | solution.py:15
  42.4 1.3 %copy-start = (bf16[3,3,256,256]{3,2,1,0:T(8,128)(2,1)S(1)}, bf16[3,3,256,256]{3,2,1,0:T(8,128)(2,1)}, u32[]{:S(2)}) copy-start(bf16[3,3,256,256]{3,2,1,0:T(8,128)(2,1)} %param.5) | copy-start | bytes 3538948
  46.9 28.1 %collective-permute-start.15 = (f32[9,128,256]{2,1,0:T(8,128)S(1)}, f32[9,128,256]{2,1,0:T(8,128)S(1)}, u32[]{:S(2)}, u32[]{:S(2)}) collective-permute-start(f32[9,128,256]{2,1,0:T(8,128)S(1)} %add.8.part_ref), channel_id=1, source_target_pairs={{0,2},{1,3},{2,0},{3,1},{4,6},{5,7},{6,4},{7,5},{8,10},{9,11},{10,... | collective-permute-start | bytes 3538952 | tf_op jit(solution)/shard_map/ppermute | solution.py:15
  48.3 30.7 %all-to-all-start = ((bf16[8,256,256]{2,1,0:T(8,128)(2,1)}), bf16[8,256,256]{2,1,0:T(8,128)(2,1)S(1)}, u32[]{:S(2)}, u32[]{:S(2)}) async-start(bf16[8,256,256]{2,1,0:T(8,128)(2,1)} %back.1), calls=%async_computation | async-start | bytes 2097152 | tf_op jit(solution)/shard_map/all_to_all | solution.py:330
  52.6 23.6 %collective-permute-start.14 = (f32[9,128,256]{2,1,0:T(8,128)S(1)}, f32[9,128,256]{2,1,0:T(8,128)S(1)}, u32[]{:S(2)}, u32[]{:S(2)}) collective-permute-start(f32[9,128,256]{2,1,0:T(8,128)S(1)} %add.8.part_ref), channel_id=1, source_target_pairs={{0,1},{1,0},{2,3},{3,2},{4,5},{5,4},{6,7},{7,6},{8,9},{9,8},{10,11... | collective-permute-start | bytes 3538952 | tf_op jit(solution)/shard_map/ppermute | solution.py:15
  75.0 2.8 %collective-permute-start.16 = (f32[9,128,256]{2,1,0:T(8,128)S(1)}, f32[9,128,256]{2,1,0:T(8,128)S(1)}, u32[]{:S(2)}, u32[]{:S(2)}) collective-permute-start(f32[9,128,256]{2,1,0:T(8,128)S(1)} %collective-permute-done.15.part_x_ref), channel_id=1, source_target_pairs={{0,1},{1,0},{2,3},{3,2},{4,5},{5,4},{6,7},{7,6},{8,9},{9,8},{10,11... | collective-permute-start | bytes 3538952 | tf_op jit(solution)/shard_map/ppermute | solution.py:15
